TPU v7x, 32 devices: a whole 2x2x4 slice. The times are simulated.
32 devices in a mesh: dp: 4 (over y, x), expert: 8 (over z, core).
Axes of the slice: x: 2, y: 2, z: 4, core: 2. Of those that a mesh axis runs over, the one named last changes fastest.
Arguments:
- routing: int32 [4096, 2], P(('dp', 'expert')), may hold values from 0 to 7, all different within a row; in each aligned block of 128 rows (0 to 127, 128 to 255, ...) at most 48 rows name the same one
- gates: float32 [4096, 2], P(('dp', 'expert')), may hold values from 0.1 to 1
- hidden: bfloat16 [4, 8, 8, 48, 768], P('dp', 'expert'), may hold values from -6 to 6
- w_down: bfloat16 [8, 768, 2048], P('expert'), may hold values from -0.21875 to 0.21875
- dout: bfloat16 [4096, 2048], P(('dp', 'expert')), may hold values from -6 to 6
Outputs:
- combined: bfloat16 [4096, 2048], P(('dp', 'expert'))
- grad_gates: float32 [4096, 2], P(('dp', 'expert'))
- grad_hidden: bfloat16 [4, 8, 8, 48, 768], P('dp', 'expert')
- grad_down: float32 [8, 768, 2048], P('expert', None, 'dp')
Inputs may be any that keep to these rules, and one draw needn't show every extreme that they name: `routing`: in each aligned block of 128 rows (the rows of one device) no expert is named by more than 48 picks, and in some block an expert is named by exactly 48.
All inputs are finite; a program needn't handle non-finite values.
Results may differ from a plain program's by a relative error of at most 0.013.
Values may be sent and summed in bfloat16 or wider, within the bound.
No kernel may reach another device: no remote copies, remote signals or barrier semaphores. Data moves between devices by JAX's collectives and lax.ppermute only.
A program may use at most 64 MiB of HBM per device.

v0:
```python
import jax
import jax.numpy as jnp
from jax import lax
from jax.sharding import PartitionSpec as P


def slot_index(routing, experts, capacity):
    flattened = routing.reshape(-1)
    onehot = (flattened[:, None] == jnp.arange(experts, dtype=jnp.int32)[None, :]).astype(jnp.int32)
    before = jnp.cumsum(onehot, axis=0) - onehot
    ranking = jnp.sum(before * onehot, axis=1)
    return flattened * capacity + ranking


def on_device(routing, gates, hidden, w_down, dout):
    experts = lax.axis_size("expert")
    capacity = hidden.shape[3]
    hidden_units = w_down.shape[1]
    model_width = w_down.shape[2]
    tok_rows = routing.shape[0]
    picks_per = routing.shape[1]
    weight = w_down[0]
    input_rows = hidden[0, 0].reshape(-1, hidden_units)
    outputs = jnp.dot(input_rows, weight, preferred_element_type=jnp.float32).astype(jnp.bfloat16)
    outputs = outputs.reshape(experts, capacity, model_width)
    returned = lax.all_to_all(outputs, "expert", split_axis=0, concat_axis=0, tiled=True)
    location = slot_index(routing, experts, capacity)
    picked = jnp.take(returned.reshape(experts * capacity, model_width), location, axis=0)
    picked = picked.reshape(tok_rows, picks_per, model_width).astype(jnp.float32)
    combined = jnp.sum(gates[..., None] * picked, axis=1).astype(jnp.bfloat16)
    grad_float = dout.astype(jnp.float32)
    grad_gates = jnp.sum(picked * grad_float[:, None, :], axis=2)
    scaled = (
        (gates[..., None] * grad_float[:, None, :]).astype(jnp.bfloat16).reshape(-1, model_width)
    )
    slot_grads = jnp.zeros((experts * capacity, model_width), jnp.bfloat16).at[location].set(scaled)
    slot_grads = slot_grads.reshape(experts, capacity, model_width)
    received = lax.all_to_all(slot_grads, "expert", split_axis=0, concat_axis=0, tiled=True)
    count_items = received.shape[1]
    flattened = received.reshape(-1, model_width)
    grad_rows = lax.dot_general(
        flattened, weight, (((1,), (1,)), ((), ())), preferred_element_type=jnp.float32
    )
    grad_hidden = grad_rows.astype(jnp.bfloat16).reshape(experts, count_items, hidden_units)
    arrived_rows = received.reshape(-1, model_width)
    partial_grad = lax.dot_general(
        input_rows, arrived_rows, (((0,), (0,)), ((), ())), preferred_element_type=jnp.float32
    )
    grad_down = lax.psum_scatter(
        partial_grad.astype(jnp.bfloat16), "dp", scatter_dimension=1, tiled=True
    ).astype(jnp.float32)
    return (combined, grad_gates, grad_hidden[None, None], grad_down[None])


def solution(mesh):
    placed = (
        P(("dp", "expert"), None),
        P(("dp", "expert"), None),
        P("dp", "expert", None, None, None),
        P("expert", None, None),
        P(("dp", "expert"), None),
    )
    return jax.shard_map(
        on_device,
        mesh=mesh,
        in_specs=placed,
        out_specs=(
            P(("dp", "expert"), None),
            P(("dp", "expert"), None),
            P("dp", "expert", None, None, None),
            P("expert", None, "dp"),
        ),
        check_vma=False,
    )
```

profile of v0, /device:TPU:0, one launch (start us, length us, event | category | flops | bytes accessed | tf_op | source)
XLA Modules:
  0.0 149.6 jit_solution(16430531975301789222)
XLA Ops:
  7.2 0.0 copy-start
  7.2 0.0 reduce-scatter.2.cloned.1.call-start
  7.2 0.9 copy.13
  8.2 0.1 eq.26
  8.3 0.1 reshape.102
  8.5 0.6 reduce-window.6
  9.1 0.2 slice_reduce_fusion
  9.3 0.8 copy.12
  10.1 0.1 mul.66
  10.2 0.1 mul.61
  10.4 3.5 %mul.63 = f32[128,2,2048]{2,1,0:T(2,128)} broadcast(bf16[128,2048]{1,0:T(8,128)(2,1)} %param.9), dimensions={0,2} | broadcast | bytes 2621440 | tf_op jit(solution)/shard_map/mul | solution.py:32
  13.8 3.7 %mul.64 = f32[256,2048]{1,0:T(8,128)} reshape(f32[128,2,2048]{2,1,0:T(2,128)} %mul.63) | data formatting | bytes 4194304 | tf_op jit(solution)/shard_map/mul | solution.py:32
  17.5 0.1 fusion.15
  17.6 4.5 %scatter_custom_fusion = bf16[384,2048]{1,0:T(8,128)(2,1)} fusion(s32[256]{0:T(256)S(1)} %bitcast.40, f32[256,2048]{1,0:T(8,128)} %mul.64, f32[256]{0:T(256)S(1)} %mul.66, bf16[]{:T(256)} %constant.28.clone.1), kind=kCustom, calls=%fused_computation.14 | custom fusion | flops 1048576 | bytes 3671042 | tf_op jit(solution)/shard_map/scatter | solution.py:36
  22.1 44.3 %all_to_all.10 = bf16[8,48,2048]{2,1,0:T(8,128)(2,1)S(1)} all-to-all(bf16[8,48,2048]{2,1,0:T(8,128)(2,1)} %bitcast.35), channel_id=1, replica_groups=mesh['dp'=4,'expert'=8] {'expert'}, dimensions={0} | all-to-all | bytes 3145728 | tf_op jit(solution)/shard_map/all_to_all | solution.py:38
  66.4 1.2 copy-done.1
  67.6 3.5 %fusion.4 = bf16[768,2048]{0,1:T(8,128)(2,1)} fusion(bf16[384,2048]{1,0:T(8,128)(2,1)S(1)} %bitcast.36, bf16[384,768]{1,0:T(8,128)(2,1)S(1)} %bitcast.43), kind=kOutput, calls=%fused_computation.7 | convolution fusion | flops 1209532416 | bytes 5308416 | tf_op jit(solution)/shard_map/dot_general | solution.py:46
  71.1 0.0 reduce-scatter.2.cloned.1.call-update
  71.2 3.6 %fusion.5 = bf16[384,2048]{1,0:T(8,128)(2,1)} fusion(bf16[384,768]{1,0:T(8,128)(2,1)} %bitcast.42, bf16[1,768,2048]{2,1,0:T(8,128)(2,1)S(1)} %copy-done), kind=kOutput, calls=%fused_computation.8 | convolution fusion | flops 1208745984 | bytes 5308416 | tf_op jit(solution)/shard_map/dot_general | solution.py:24
  74.8 4.5 %all-to-all-start = ((bf16[8,48,2048]{2,1,0:T(8,128)(2,1)}), bf16[8,48,2048]{2,1,0:T(8,128)(2,1)}, u32[]{:S(2)}, u32[]{:S(2)}) async-start(bf16[8,48,2048]{2,1,0:T(8,128)(2,1)} %bitcast.38), calls=%async_computation | async-start | bytes 3145728 | tf_op jit(solution)/shard_map/all_to_all | solution.py:26
  79.3 0.1 reduce_sum.34
  79.4 0.1 broadcast_in_dim.33
  79.6 37.3 %all-to-all-done = bf16[8,48,2048]{2,1,0:T(8,128)(2,1)} async-done(((bf16[8,48,2048]{2,1,0:T(8,128)(2,1)}), bf16[8,48,2048]{2,1,0:T(8,128)(2,1)}, u32[]{:S(2)}, u32[]{:S(2)}) %all-to-all-start) | async-done | bytes 1572896 | tf_op jit(solution)/shard_map/all_to_all | solution.py:26
  116.9 4.9 %gather_fusion = bf16[256,2048]{1,0:T(8,128)(2,1)} fusion(bf16[384,2048]{1,0:T(8,128)(2,1)} %bitcast.5, s32[1024]{0:T(1024)S(1)} %pad_clamp_fusion), kind=kCustom, calls=%fused_computation | custom fusion | bytes 2098176 | tf_op jit(solution)/shard_map/jit(_take)/gather | solution.py:28
  121.9 2.5 %gather.7 = bf16[128,2,2048]{2,1,0:T(2,128)(2,1)} reshape(bf16[256,2048]{1,0:T(8,128)(2,1)} %gather_fusion) | data formatting | bytes 2097152 | tf_op jit(solution)/shard_map/jit(_take)/gather | solution.py:28
  124.4 2.3 %multiply_reduce_fusion = f32[256]{0:T(256)S(1)} fusion(f32[256,2048]{1,0:T(8,128)} %mul.64, bf16[256,2048]{1,0:T(8,128)(2,1)} %gather_fusion, pred[256]{0:T(512)(128)(4,1)S(1)} %broadcast_in_dim.33), kind=kLoop, calls=%fused_computation.10 | loop fusion | flops 2096896 | bytes 3147008 | tf_op jit(solution)/shard_map/reduce_sum | solution.py:32
  126.7 0.1 reduce_sum.38
  126.8 0.6 copy.17
  127.4 6.2 %multiply_reduce_fusion.1 = bf16[128,2048]{1,0:T(8,128)(2,1)} fusion(bf16[128,2,2048]{2,1,0:T(2,128)(2,1)} %gather.7, pred[128,2]{1,0:T(8,128)(4,1)S(1)} %compare_and_fusion, f32[128,2]{1,0:T(8,128)S(1)} %copy.12), kind=kLoop, calls=%fused_computation.11 | loop fusion | flops 1835008 | bytes 1574144 | tf_op jit(solution)/shard_map/reduce_sum | solution.py:30
  133.7 3.6 %fusion.8 = bf16[384,768]{1,0:T(8,128)(2,1)} fusion(bf16[384,2048]{1,0:T(8,128)(2,1)} %bitcast.37, bf16[1,768,2048]{2,1,0:T(8,128)(2,1)S(1)} %copy-done), kind=kOutput, calls=%fused_computation.13 | convolution fusion | flops 1208254464 | bytes 5308416 | tf_op jit(solution)/shard_map/dot_general | solution.py:41
  137.3 2.4 %bitcast_convert_fusion = f32[1,768,512]{1,2,0:T(8,128)} fusion(bf16[768,512]{0,1:T(8,128)(2,1)} %reduce-scatter.2.cloned.1.call-done), kind=kLoop, calls=%fused_computation.16 | loop fusion | flops 393216 | bytes 2359296 | tf_op jit(solution)/shard_map/broadcast_in_dim | solution.py:52
  139.7 3.0 %copy.18 = f32[1,768,512]{2,1,0:T(8,128)} copy(f32[1,768,512]{1,2,0:T(8,128)} %bitcast_convert_fusion) | data formatting | bytes 3145728
  (12 shorter events, 0.1 us)
Async XLA Ops:
  7.2 64.0 %copy-start = (bf16[1,768,2048]{2,1,0:T(8,128)(2,1)S(1)}, bf16[1,768,2048]{2,1,0:T(8,128)(2,1)}, u32[]{:S(2)}) copy-start(bf16[1,768,2048]{2,1,0:T(8,128)(2,1)} %param.8) | copy-start | bytes 9437188
  7.2 130.2 %reduce-scatter.2.cloned.1.call-start = ((), (), s32[]{:S(2)}) async-start(), calls=%async_computation.3 | async-start | bytes 3932160 | tf_op jit(solution)/shard_map/reduce_scatter | solution.py:49
  22.1 45.5 %copy-start.2 = (bf16[1,1,8,48,768]{4,3,2,1,0:T(8,128)(2,1)S(1)}, bf16[1,1,8,48,768]{4,3,2,1,0:T(8,128)(2,1)}, u32[]{:S(2)}) copy-start(bf16[1,1,8,48,768]{4,3,2,1,0:T(8,128)(2,1)} %param.7) | copy-start | bytes 1769476
  66.4 1.2 copy-start.1
  74.8 42.1 %all-to-all-start = ((bf16[8,48,2048]{2,1,0:T(8,128)(2,1)}), bf16[8,48,2048]{2,1,0:T(8,128)(2,1)}, u32[]{:S(2)}, u32[]{:S(2)}) async-start(bf16[8,48,2048]{2,1,0:T(8,128)(2,1)} %bitcast.38), calls=%async_computation | async-start | bytes 3145728 | tf_op jit(solution)/shard_map/all_to_all | solution.py:26
Sparse Core Ops, SparseCore 0:
  71.3 42.8 reduce-scatter.1
where the time goes:
time: 150 us
  blocking collectives  44.3 us (30%)
  waiting for transfers between devices  37.3 us (25%)
  local copies, waits for them, and re-layouts  22.4 us (15%)
  other arithmetic  16.2 us (11%)
  between operations  14.1 us (9%)
  matrix products  10.8 us (7%)
  starting transfers between devices  4.53 us (3%)
    all_to_all x1, blocking collectives, on_device(): lax.all_to_all(slot_grads, 'expert', split_axis=0, concat_axis=0, tiled=T...  44.3 us
    all_to_all x1, waiting for transfers between devices, on_device(): lax.all_to_all(outputs, 'expert', split_axis=0, concat_axis=0, tiled=True)  37.3 us
    gather x2, local copies, waits for them, and re-layouts, on_device(): jnp.take(returned.reshape(experts * capacity, model_width), location, axi...  7.46 us
    mul x2, local copies, waits for them, and re-layouts, on_device(): grad_gates = jnp.sum(picked * grad_float[:, None, :], axis=2)  7.1 us
    unnamed x10, local copies, waits for them, and re-layouts  6.61 us
    reduce_sum x1, other arithmetic, on_device(): combined = jnp.sum(gates[..., None] * picked, axis=1).astype(jnp.bfloat16)  6.24 us
    scatter x1, other arithmetic, on_device(): jnp.zeros((experts * capacity, model_width), jnp.bfloat16).at[location]  4.54 us
    all_to_all x1, starting transfers between devices, on_device(): lax.all_to_all(outputs, 'expert', split_axis=0, concat_axis=0, tiled=True)  4.49 us
  transfers between devices with their start and end apart: 2, of which 1 were waited for; matrix products, arithmetic and copies ran while one was open for 16% of the time, Pallas kernels for 0%

commit v1 on v0

--- a/solution.py
+++ b/solution.py
@@ -1,7 +1,188 @@
+import functools
+
 import jax
 import jax.numpy as jnp
 from jax import lax
+from jax.experimental import pallas as pl
+from jax.experimental.pallas import tpu as pltpu
 from jax.sharding import PartitionSpec as P
+
+WIDEST = 8
+MIB = 1 << 20
+
+
+def call(body, out_shape, args, flops=0, scratch=(), vmem=40):
+    moved = sum(a.size * a.dtype.itemsize for a in jax.tree.leaves((args, out_shape)))
+    return pl.pallas_call(
+        body,
+        out_shape=out_shape,
+        scratch_shapes=scratch,
+        compiler_params=pltpu.CompilerParams(vmem_limit_bytes=vmem * MIB),
+        cost_estimate=pl.CostEstimate(flops=flops, bytes_accessed=moved, transcendentals=0),
+    )(*args)
+
+
+def as_row(column):
+    rows = column.shape[0]
+    diagonal = lax.broadcasted_iota(jnp.int32, (rows, rows), 0) == lax.broadcasted_iota(
+        jnp.int32, (rows, rows), 1
+    )
+    return jnp.sum(jnp.where(diagonal, column, 0.0), axis=0, keepdims=True)
+
+
+def slot_columns(named, experts, capacity):
+    tokens, picks = named.shape
+    lane = lax.broadcasted_iota(jnp.int32, (tokens, experts), 1)
+    onehots = [(named[:, k : k + 1] == lane).astype(jnp.float32) for k in range(picks)]
+    counted = functools.reduce(jnp.add, onehots)
+    earlier = lax.broadcasted_iota(jnp.int32, (tokens, tokens), 0) > lax.broadcasted_iota(
+        jnp.int32, (tokens, tokens), 1
+    )
+    before = jnp.dot(
+        earlier.astype(jnp.bfloat16),
+        counted.astype(jnp.bfloat16),
+        preferred_element_type=jnp.float32,
+    )
+    return [
+        named[:, k : k + 1].astype(jnp.float32) * capacity
+        + jnp.sum(before * onehots[k], axis=1, keepdims=True)
+        for k in range(picks)
+    ]
+
+
+def spread_body(experts, capacity, routing_ref, gates_ref, dout_ref, *block_refs):
+    me = lax.axis_index("expert")
+    tokens, picks = routing_ref.shape
+    slots = slot_columns(routing_ref[...] ^ me, experts, capacity)
+    gates = gates_ref[...]
+    slot_rows = [as_row(s) for s in slots]
+    gate_rows = [as_row(gates[:, k : k + 1]) for k in range(picks)]
+    for m, block in enumerate(block_refs):
+        here = lax.broadcasted_iota(jnp.int32, (capacity, tokens), 0).astype(jnp.float32) + m * capacity
+        hits = [here == row for row in slot_rows]
+        chosen = functools.reduce(jnp.logical_or, hits).astype(jnp.bfloat16)
+        gate = functools.reduce(
+            jnp.add,
+            [jnp.sum(jnp.where(h, g, 0.0), axis=1, keepdims=True) for h, g in zip(hits, gate_rows)],
+        )
+        rows = jnp.dot(chosen, dout_ref[...], preferred_element_type=jnp.float32)
+        block[...] = (rows * gate).astype(jnp.bfloat16)
+
+
+def expert_body(hidden_ref, weight_ref, *block_refs):
+    me = lax.axis_index("expert")
+    capacity = hidden_ref.shape[1]
+    rows = jnp.concatenate([hidden_ref[me ^ m] for m in range(len(block_refs))], axis=0)
+    out = jnp.dot(rows, weight_ref[...], preferred_element_type=jnp.float32).astype(jnp.bfloat16)
+    for m, block in enumerate(block_refs):
+        block[...] = out[m * capacity : (m + 1) * capacity]
+
+
+def hidden_grad_body(groups, *refs):
+    *block_refs, weight_ref, grad_ref = refs[: -groups]
+    slice_refs = refs[-groups:]
+    me = lax.axis_index("expert")
+    group = lax.axis_index("dp")
+    capacity = block_refs[0].shape[0]
+    rows = jnp.concatenate([b[...] for b in block_refs], axis=0)
+    grad = lax.dot_general(
+        rows, weight_ref[...], (((1,), (1,)), ((), ())), preferred_element_type=jnp.float32
+    ).astype(jnp.bfloat16)
+    for m in range(len(block_refs)):
+        grad_ref[me ^ m] = grad[m * capacity : (m + 1) * capacity]
+    width = slice_refs[0].shape[1]
+    for d, part in enumerate(slice_refs):
+        columns = pl.ds(pl.multiple_of((group ^ d) * width, width), width)
+        for m, b in enumerate(block_refs):
+            part[m * capacity : (m + 1) * capacity] = b[:, columns]
+
+
+def weight_grad_body(groups, *refs):
+    hidden_refs, slice_refs, out_ref = refs[:groups], refs[groups : 2 * groups], refs[-1]
+    me = lax.axis_index("expert")
+    experts = hidden_refs[0].shape[0]
+    total = jnp.zeros(out_ref.shape, jnp.float32)
+    for h, s in zip(hidden_refs, slice_refs):
+        rows = jnp.concatenate([h[me ^ m] for m in range(experts)], axis=0)
+        total += lax.dot_general(
+            rows, s[...], (((0,), (0,)), ((), ())), preferred_element_type=jnp.float32
+        )
+    out_ref[...] = total
+
+
+def combine_body(experts, capacity, routing_ref, gates_ref, dout_ref, *refs):
+    block_refs, combined_ref, grad_gates_ref = refs[:-2], refs[-2], refs[-1]
+    me = lax.axis_index("expert")
+    tokens, picks = routing_ref.shape
+    slots = slot_columns(routing_ref[...] ^ me, experts, capacity)
+    gates = gates_ref[...]
+    lane = lax.broadcasted_iota(jnp.int32, (tokens, experts * capacity), 1).astype(jnp.float32)
+    rows = jnp.concatenate([b[...] for b in block_refs], axis=0)
+    dout = dout_ref[...].astype(jnp.float32)
+    total = 0.0
+    for k in range(picks):
+        chosen = (lane == slots[k]).astype(jnp.bfloat16)
+        picked = jnp.dot(chosen, rows, preferred_element_type=jnp.float32)
+        total += gates[:, k : k + 1] * picked
+        grad_gates_ref[:, k : k + 1] = jnp.sum(picked * dout, axis=1, keepdims=True)
+    combined_ref[...] = total.astype(jnp.bfloat16)
+
+
+def pairs(size, m):
+    return [(i, i ^ m) for i in range(size)]
+
+
+def exchange(blocks, axis):
+    size = lax.axis_size(axis)
+    got = {0: blocks[0]}
+    for m in reversed(range(1, size)):
+        got[m] = lax.ppermute(blocks[m], axis, pairs(size, m))
+    return [got[m] for m in range(size)]
+
+
+def on_device(routing, gates, hidden, w_down, dout):
+    experts = lax.axis_size("expert")
+    groups = lax.axis_size("dp")
+    capacity, units = hidden.shape[3:]
+    width = w_down.shape[2]
+    tokens, picks = routing.shape
+    own = hidden[0, 0]
+    weight = w_down[0]
+    flops = 2 * experts * capacity * units * width
+    block = jax.ShapeDtypeStruct((capacity, width), jnp.bfloat16)
+
+    sent = call(
+        functools.partial(spread_body, experts, capacity), [block] * experts, (routing, gates, dout),
+        flops=2 * experts * capacity * tokens * width,
+    )
+    arrived = exchange(sent, "expert")
+    outputs = call(expert_body, [block] * experts, (own, weight), flops=flops)
+    returned = exchange(outputs, "expert")
+    peers = exchange([own] * groups, "dp")
+    grad_hidden, *slices = call(
+        functools.partial(hidden_grad_body, groups),
+        [jax.ShapeDtypeStruct(own.shape, jnp.bfloat16)]
+        + [jax.ShapeDtypeStruct((experts * capacity, width // groups), jnp.bfloat16)] * groups,
+        (*arrived, weight),
+        flops=flops,
+    )
+    gathered = exchange(slices, "dp")
+    grad_down = call(
+        functools.partial(weight_grad_body, groups),
+        jax.ShapeDtypeStruct((units, width // groups), jnp.float32),
+        (*peers, *gathered),
+        flops=flops,
+    )
+    combined, grad_gates = call(
+        functools.partial(combine_body, experts, capacity),
+        [
+            jax.ShapeDtypeStruct((tokens, width), jnp.bfloat16),
+            jax.ShapeDtypeStruct((tokens, picks), jnp.float32),
+        ],
+        (routing, gates, dout, *returned),
+        flops=2 * picks * experts * capacity * tokens * width,
+    )
+    return (combined, grad_gates, grad_hidden[None, None], grad_down[None])
 
 
 def slot_index(routing, experts, capacity):
@@ -12,7 +193,7 @@
     return flattened * capacity + ranking
 
 
-def on_device(routing, gates, hidden, w_down, dout):
+def on_device_wide(routing, gates, hidden, w_down, dout):
     experts = lax.axis_size("expert")
     capacity = hidden.shape[3]
     hidden_units = w_down.shape[1]
@@ -36,15 +217,13 @@
     slot_grads = jnp.zeros((experts * capacity, model_width), jnp.bfloat16).at[location].set(scaled)
     slot_grads = slot_grads.reshape(experts, capacity, model_width)
     received = lax.all_to_all(slot_grads, "expert", split_axis=0, concat_axis=0, tiled=True)
-    count_items = received.shape[1]
     flattened = received.reshape(-1, model_width)
     grad_rows = lax.dot_general(
         flattened, weight, (((1,), (1,)), ((), ())), preferred_element_type=jnp.float32
     )
-    grad_hidden = grad_rows.astype(jnp.bfloat16).reshape(experts, count_items, hidden_units)
-    arrived_rows = received.reshape(-1, model_width)
+    grad_hidden = grad_rows.astype(jnp.bfloat16).reshape(experts, capacity, hidden_units)
     partial_grad = lax.dot_general(
-        input_rows, arrived_rows, (((0,), (0,)), ((), ())), preferred_element_type=jnp.float32
+        input_rows, flattened, (((0,), (0,)), ((), ())), preferred_element_type=jnp.float32
     )
     grad_down = lax.psum_scatter(
         partial_grad.astype(jnp.bfloat16), "dp", scatter_dimension=1, tiled=True
@@ -60,8 +239,9 @@
         P("expert", None, None),
         P(("dp", "expert"), None),
     )
+    pairwise = all(size <= WIDEST and size & (size - 1) == 0 for size in mesh.shape.values())
     return jax.shard_map(
-        on_device,
+        on_device if pairwise else on_device_wide,
         mesh=mesh,
         in_specs=placed,
         out_specs=(

time: 150 us -> 108 us (0.72)
  blocking collectives: 44.3 us -> 0 us
  starting transfers between devices: 4.53 us -> 45.2 us
  local copies, waits for them, and re-layouts: 22.4 us -> 5.14 us
  other arithmetic: 16.2 us -> 0 us
  between operations: 14.1 us -> 0.69 us
  Pallas kernels: 0 us -> 12.3 us
  matrix products: 10.8 us -> 0 us
  waiting for transfers between devices: 37.3 us -> 44.1 us
    ppermute x0 -> x20, starting transfers between devices: none -> 45.2 us  [exchange(): got[m] = lax.ppermute(blocks[m], axis, pairs(size, m))]
    all_to_all x1 -> x0, blocking collectives: 44.3 us -> none  [on_device(): lax.all_to_all(slot_grads, 'expert', split_axis=0, concat_axis=0, tiled=T...]
    ppermute x0 -> x20, waiting for transfers between devices: none -> 44.1 us  [exchange(): got[m] = lax.ppermute(blocks[m], axis, pairs(size, m))]
    all_to_all x1 -> x0, waiting for transfers between devices: 37.3 us -> none  [on_device(): lax.all_to_all(outputs, 'expert', split_axis=0, concat_axis=0, tiled=True)]
    pallas_call x0 -> x5, Pallas kernels: none -> 12.3 us  [call(): pl.pallas_call(body, out_shape=out_shape, scratch_shapes=scratch, compile...]
    dot_general x3 -> x0, matrix products: 10.8 us -> none  [the longest x1 3.65 us: on_device(): lax.dot_general(flattened, weight, (((1,), (1,)), ((), ())), preferred_el...]
    reduce_sum x3 -> x0, other arithmetic: 8.61 us -> none  [the longest x1 6.24 us: on_device(): combined = jnp.sum(gates[..., None] * picked, axis=1).astype(jnp.bfloat16)]
    gather x2 -> x0, local copies, waits for them, and re-layouts: 7.46 us -> none  [on_device(): jnp.take(returned.reshape(experts * capacity, model_width), location, axi...]
  transfers between devices with their start and end apart: 2 -> 20, of which waited for: 1 -> 7; matrix products, arithmetic and copies ran while one was open for 16% -> 1% of each run, Pallas kernels for 0% -> 7%
where the time goes in v1:
time: 108 us
  starting transfers between devices  45.2 us (42%)
  waiting for transfers between devices  44.1 us (41%)
  Pallas kernels  12.3 us (11%)
  local copies, waits for them, and re-layouts  5.14 us (5%)
    ppermute x20, starting transfers between devices, exchange(): got[m] = lax.ppermute(blocks[m], axis, pairs(size, m))  45.2 us
    ppermute x20, waiting for transfers between devices, exchange(): got[m] = lax.ppermute(blocks[m], axis, pairs(size, m))  44.1 us
    pallas_call x5, Pallas kernels, call(): pl.pallas_call(body, out_shape=out_shape, scratch_shapes=scratch, compile...  12.3 us
    unnamed x11, local copies, waits for them, and re-layouts  5.14 us
  transfers between devices with their start and end apart: 20, of which 7 were waited for; matrix products, arithmetic and copies ran while one was open for 1% of the time, Pallas kernels for 7%

profile of v1, /device:TPU:0, one launch (start us, length us, event | category | flops | bytes accessed | tf_op | source)
XLA Modules:
  0.0 107.5 jit_solution(12205606815761569421)
XLA Ops:
  0.6 0.8 copy.9.routing_ref
  1.4 0.8 copy.10.gates_ref
  2.2 1.0 copy-done.2
  3.2 1.1 %shard_map.86 = (bf16[48,2048]{1,0:T(8,128)(2,1)S(1)}, bf16[48,2048]{1,0:T(8,128)(2,1)S(1)}, bf16[48,2048]{1,0:T(8,128)(2,1)S(1)}, bf16[48,2048]{1,0:T(8,128)(2,...) custom-call(s32[128,2]{1,0:T(8,128)S(1)} %copy.9.routing_ref, ...), custom_call_target="tpu_custom_call" | custom-call | flops 201326592 | bytes 2099200 | tf_op jit(solution)/shard_map/pallas_call | solution.py:16
  4.4 0.5 collective-permute-start.7
  4.9 2.7 %collective-permute-start.8 = (bf16[48,2048]{1,0:T(8,128)(2,1)S(1)}, bf16[48,2048]{1,0:T(8,128)(2,1)S(1)}, u32[]{:S(2)}, u32[]{:S(2)}) collective-permute-start(bf16[48,2048]{1,0:T(8,128)(2,1)S(1)} %get-tuple-element.39), channel_id=1, source_target_pairs={{0,2},{1,3},{2,0},{3,1},{4,6},{5,7},{6,4},{7,5},{8,10},{9,11},{10,... | collective-permute-start | bytes 589832 | tf_op jit(solution)/shard_map/ppermute | solution.py:139
  7.6 2.8 %collective-permute-start.10 = (bf16[48,2048]{1,0:T(8,128)(2,1)S(1)}, bf16[48,2048]{1,0:T(8,128)(2,1)S(1)}, u32[]{:S(2)}, u32[]{:S(2)}) collective-permute-start(bf16[48,2048]{1,0:T(8,128)(2,1)S(1)} %get-tuple-element.41), channel_id=1, source_target_pairs={{0,4},{1,5},{2,6},{3,7},{4,0},{5,1},{6,2},{7,3},{8,12},{9,13},{10,... | collective-permute-start | bytes 589832 | tf_op jit(solution)/shard_map/ppermute | solution.py:139
  10.4 1.9 %copy-done = bf16[1,768,2048]{2,1,0:T(8,128)(2,1)S(1)} copy-done((bf16[1,768,2048]{2,1,0:T(8,128)(2,1)S(1)}, bf16[1,768,2048]{2,1,0:T(8,128)(2,1)}, u32[]{:S(2)}) %copy-start) | copy-done | bytes 3145752
  12.3 2.6 %shard_map.84 = (bf16[48,2048]{1,0:T(8,128)(2,1)S(1)}, bf16[48,2048]{1,0:T(8,128)(2,1)S(1)}, bf16[48,2048]{1,0:T(8,128)(2,1)S(1)}, bf16[48,2048]{1,0:T(8,128)(2,...) custom-call(bf16[8,48,768]{2,1,0:T(8,128)(2,1)} %bitcast.hidden_ref., ...), custom_call_target="tpu_custom_call" | custom-call | flops 1207959552 | bytes 5308416 | tf_op jit(solution)/shard_map/pallas_call | solution.py:16
  14.9 3.7 %collective-permute-start.12 = (bf16[48,2048]{1,0:T(8,128)(2,1)S(1)}, bf16[48,2048]{1,0:T(8,128)(2,1)S(1)}, u32[]{:S(2)}, u32[]{:S(2)}) collective-permute-start(bf16[48,2048]{1,0:T(8,128)(2,1)S(1)} %get-tuple-element.43), channel_id=1, source_target_pairs={{0,6},{1,7},{2,4},{3,5},{4,2},{5,3},{6,0},{7,1},{8,14},{9,15},{10,... | collective-permute-start | bytes 589832 | tf_op jit(solution)/shard_map/ppermute | solution.py:139
  18.6 2.7 %collective-permute-done.8.refs_2_ = bf16[48,2048]{1,0:T(8,128)(2,1)S(1)} collective-permute-done((bf16[48,2048]{1,0:T(8,128)(2,1)S(1)}, bf16[48,2048]{1,0:T(8,128)(2,1)S(1)}, u32[]{:S(2)}, u32[]{:S(2)}) %collective-permute-start.8) | collective-permute-done | bytes 196640 | tf_op jit(solution)/shard_map/ppermute | solution.py:139
  21.3 0.5 collective-permute-start.13
  21.8 3.2 %collective-permute-done.9.refs_3_ = bf16[48,2048]{1,0:T(8,128)(2,1)S(1)} collective-permute-done((bf16[48,2048]{1,0:T(8,128)(2,1)S(1)}, bf16[48,2048]{1,0:T(8,128)(2,1)S(1)}, u32[]{:S(2)}, u32[]{:S(2)}) %collective-permute-start.9) | collective-permute-done | bytes 196640 | tf_op jit(solution)/shard_map/ppermute | solution.py:139
  25.1 2.5 %collective-permute-start.16 = (bf16[8,48,768]{2,1,0:T(8,128)(2,1)}, bf16[8,48,768]{2,1,0:T(8,128)(2,1)S(1)}, u32[]{:S(2)}, u32[]{:S(2)}) collective-permute-start(bf16[8,48,768]{2,1,0:T(8,128)(2,1)} %bitcast.hidden_ref.refs_0_), channel_id=1, source_target_pairs={{0,24},{8,16},{16,8},{24,0},{1,25},{9,17},{17,9},{25,1},{2,26},{10... | collective-permute-start | bytes 1769480 | tf_op jit(solution)/shard_map/ppermute | solution.py:139
  27.6 10.7 %collective-permute-start.1 = (bf16[48,2048]{1,0:T(8,128)(2,1)S(1)}, bf16[48,2048]{1,0:T(8,128)(2,1)S(1)}, u32[]{:S(2)}, u32[]{:S(2)}) collective-permute-start(bf16[48,2048]{1,0:T(8,128)(2,1)S(1)} %get-tuple-element.29), channel_id=1, source_target_pairs={{0,2},{1,3},{2,0},{3,1},{4,6},{5,7},{6,4},{7,5},{8,10},{9,11},{10,... | collective-permute-start | bytes 589832 | tf_op jit(solution)/shard_map/ppermute | solution.py:139
  38.3 2.8 %collective-permute-start.2 = (bf16[48,2048]{1,0:T(8,128)(2,1)S(1)}, bf16[48,2048]{1,0:T(8,128)(2,1)S(1)}, u32[]{:S(2)}, u32[]{:S(2)}) collective-permute-start(bf16[48,2048]{1,0:T(8,128)(2,1)S(1)} %get-tuple-element.30), channel_id=1, source_target_pairs={{0,3},{1,2},{2,1},{3,0},{4,7},{5,6},{6,5},{7,4},{8,11},{9,10},{10,... | collective-permute-start | bytes 589832 | tf_op jit(solution)/shard_map/ppermute | solution.py:139
  41.1 6.4 %collective-permute-start.3 = (bf16[48,2048]{1,0:T(8,128)(2,1)S(1)}, bf16[48,2048]{1,0:T(8,128)(2,1)S(1)}, u32[]{:S(2)}, u32[]{:S(2)}) collective-permute-start(bf16[48,2048]{1,0:T(8,128)(2,1)S(1)} %get-tuple-element.31), channel_id=1, source_target_pairs={{0,4},{1,5},{2,6},{3,7},{4,0},{5,1},{6,2},{7,3},{8,12},{9,13},{10,... | collective-permute-start | bytes 589832 | tf_op jit(solution)/shard_map/ppermute | solution.py:139
  47.8 1.5 %collective-permute-start.15 = (bf16[8,48,768]{2,1,0:T(8,128)(2,1)}, bf16[8,48,768]{2,1,0:T(8,128)(2,1)S(1)}, u32[]{:S(2)}, u32[]{:S(2)}) collective-permute-start(bf16[8,48,768]{2,1,0:T(8,128)(2,1)} %bitcast.hidden_ref.refs_0_), channel_id=1, source_target_pairs={{0,16},{8,24},{16,0},{24,8},{1,17},{9,25},{17,1},{25,9},{2,18},{10... | collective-permute-start | bytes 1769480 | tf_op jit(solution)/shard_map/ppermute | solution.py:139
  49.4 5.7 %collective-permute-start.5 = (bf16[48,2048]{1,0:T(8,128)(2,1)S(1)}, bf16[48,2048]{1,0:T(8,128)(2,1)S(1)}, u32[]{:S(2)}, u32[]{:S(2)}) collective-permute-start(bf16[48,2048]{1,0:T(8,128)(2,1)S(1)} %get-tuple-element.33), channel_id=1, source_target_pairs={{0,6},{1,7},{2,4},{3,5},{4,2},{5,3},{6,0},{7,1},{8,14},{9,15},{10,... | collective-permute-start | bytes 589832 | tf_op jit(solution)/shard_map/ppermute | solution.py:139
  55.1 10.8 %collective-permute-done.3.refs_4_ = bf16[48,2048]{1,0:T(8,128)(2,1)S(1)} collective-permute-done((bf16[48,2048]{1,0:T(8,128)(2,1)S(1)}, bf16[48,2048]{1,0:T(8,128)(2,1)S(1)}, u32[]{:S(2)}, u32[]{:S(2)}) %collective-permute-start.3) | collective-permute-done | bytes 196640 | tf_op jit(solution)/shard_map/ppermute | solution.py:139
  65.9 4.2 %collective-permute-done.4.refs_5_ = bf16[48,2048]{1,0:T(8,128)(2,1)S(1)} collective-permute-done((bf16[48,2048]{1,0:T(8,128)(2,1)S(1)}, bf16[48,2048]{1,0:T(8,128)(2,1)S(1)}, u32[]{:S(2)}, u32[]{:S(2)}) %collective-permute-start.4) | collective-permute-done | bytes 196640 | tf_op jit(solution)/shard_map/ppermute | solution.py:139
  70.1 1.5 %collective-permute-start.14 = (bf16[8,48,768]{2,1,0:T(8,128)(2,1)}, bf16[8,48,768]{2,1,0:T(8,128)(2,1)S(1)}, u32[]{:S(2)}, u32[]{:S(2)}) collective-permute-start(bf16[8,48,768]{2,1,0:T(8,128)(2,1)} %bitcast.hidden_ref.refs_0_), channel_id=1, source_target_pairs={{0,8},{8,0},{16,24},{24,16},{1,9},{9,1},{17,25},{25,17},{2,10},{10... | collective-permute-start | bytes 1769480 | tf_op jit(solution)/shard_map/ppermute | solution.py:139
  71.6 2.6 %shard_map.87 = (bf16[8,48,768]{2,1,0:T(8,128)(2,1)}, bf16[384,512]{1,0:T(8,128)(2,1)S(1)}, bf16[384,512]{1,0:T(8,128)(2,1)}, bf16[384,512]{1,0:T(8,128)(2,1)}, bf16[384,512]{1,0:T(8,128)(2,1)}) custom-call(bf16[48,2048]{1,0:T(8,128)(2,1)S(1)} %get-tuple-element.37.refs_0_, bf16[48,2048]{1,0:T(8,128)(2,1)S(1)} %collective-permute-done.7.refs_1_, ...), custom_call_target="tpu_custom_call" | custom-call | flops 1207959552 | bytes 6881280 | tf_op jit(solution)/shard_map/pallas_call | solution.py:16
  74.2 0.5 collective-permute-start.17
  74.8 1.5 %collective-permute-start.18 = (bf16[384,512]{1,0:T(8,128)(2,1)}, bf16[384,512]{1,0:T(8,128)(2,1)S(1)}, u32[]{:S(2)}, u32[]{:S(2)}) collective-permute-start(bf16[384,512]{1,0:T(8,128)(2,1)} %get-tuple-element.48), channel_id=1, source_target_pairs={{0,16},{8,24},{16,0},{24,8},{1,17},{9,25},{17,1},{25,9},{2,18},{10... | collective-permute-start | bytes 1179656 | tf_op jit(solution)/shard_map/ppermute | solution.py:139
  76.3 1.4 %collective-permute-start.19 = (bf16[384,512]{1,0:T(8,128)(2,1)}, bf16[384,512]{1,0:T(8,128)(2,1)S(1)}, u32[]{:S(2)}, u32[]{:S(2)}) collective-permute-start(bf16[384,512]{1,0:T(8,128)(2,1)} %get-tuple-element.49), channel_id=1, source_target_pairs={{0,24},{8,16},{16,8},{24,0},{1,25},{9,17},{17,9},{25,1},{2,26},{10... | collective-permute-start | bytes 1179656 | tf_op jit(solution)/shard_map/ppermute | solution.py:139
  77.7 1.9 %shard_map.85 = (bf16[128,2048]{1,0:T(8,128)(2,1)}, f32[128,2]{1,0:T(8,128)S(1)}) custom-call(s32[128,2]{1,0:T(8,128)S(1)} %copy.9.routing_ref, f32[128,2]{1,0:T(8,128)S(1)} %copy.10.gates_ref, bf16[128,2048]{1,0:T(8,128)(2,1)S(1)} %copy-done.3, bf16[48,2048]{1,0:T(8,128)(2,1)S(1)} %get-tuple-element.27.refs_0_, ...), custom_call_target="tpu_custom_call" | custom-call | flops 402653184 | bytes 2624512 | tf_op jit(solution)/shard_map/pallas_call | solution.py:16
  79.6 0.6 copy.13
  80.3 6.2 %collective-permute-done.14.refs_1_ = bf16[8,48,768]{2,1,0:T(8,128)(2,1)S(1)} collective-permute-done((bf16[8,48,768]{2,1,0:T(8,128)(2,1)}, bf16[8,48,768]{2,1,0:T(8,128)(2,1)S(1)}, u32[]{:S(2)}, u32[]{:S(2)}) %collective-permute-start.14) | collective-permute-done | bytes 589856 | tf_op jit(solution)/shard_map/ppermute | solution.py:139
  86.5 8.4 %collective-permute-done.17.refs_5_ = bf16[384,512]{1,0:T(8,128)(2,1)S(1)} collective-permute-done((bf16[384,512]{1,0:T(8,128)(2,1)}, bf16[384,512]{1,0:T(8,128)(2,1)S(1)}, u32[]{:S(2)}, u32[]{:S(2)}) %collective-permute-start.17) | collective-permute-done | bytes 393248 | tf_op jit(solution)/shard_map/ppermute | solution.py:139
  94.9 8.6 %collective-permute-done.19.refs_7_ = bf16[384,512]{1,0:T(8,128)(2,1)S(1)} collective-permute-done((bf16[384,512]{1,0:T(8,128)(2,1)}, bf16[384,512]{1,0:T(8,128)(2,1)S(1)}, u32[]{:S(2)}, u32[]{:S(2)}) %collective-permute-start.19) | collective-permute-done | bytes 393248 | tf_op jit(solution)/shard_map/ppermute | solution.py:139
  103.5 4.0 %shard_map.88 = f32[768,512]{1,0:T(8,128)} custom-call(bf16[8,48,768]{2,1,0:T(8,128)(2,1)} %bitcast.hidden_ref.refs_0_, bf16[8,48,768]{2,1,0:T(8,128)(2,1)S(1)} %collective-permute-done.14.refs_1_, bf16[8,48,768]{2,1,0:T(8,128)(2,1)S(1)} %collective-permute-done.15.refs_2_, bf16[8,48,768]{2,1,0:T(8,128)(2,1)S(1)} %collective-permute-done.16.refs_3_, ...), custom_call_target="tpu_custom_call" | custom-call | flops 1207959552 | bytes 5505024 | tf_op jit(solution)/shard_map/pallas_call | solution.py:16
  (24 shorter events, 0.6 us)
Async XLA Ops:
  2.2 1.0 copy-start.2
  4.4 10.5 %collective-permute-start.7 = (bf16[48,2048]{1,0:T(8,128)(2,1)S(1)}, bf16[48,2048]{1,0:T(8,128)(2,1)S(1)}, u32[]{:S(2)}, u32[]{:S(2)}) collective-permute-start(bf16[48,2048]{1,0:T(8,128)(2,1)S(1)} %get-tuple-element.38), channel_id=1, source_target_pairs={{0,1},{1,0},{2,3},{3,2},{4,5},{5,4},{6,7},{7,6},{8,9},{9,8},{10,11... | collective-permute-start | bytes 589832 | tf_op jit(solution)/shard_map/ppermute | solution.py:139
  4.9 16.4 %collective-permute-start.8 = (bf16[48,2048]{1,0:T(8,128)(2,1)S(1)}, bf16[48,2048]{1,0:T(8,128)(2,1)S(1)}, u32[]{:S(2)}, u32[]{:S(2)}) collective-permute-start(bf16[48,2048]{1,0:T(8,128)(2,1)S(1)} %get-tuple-element.39), channel_id=1, source_target_pairs={{0,2},{1,3},{2,0},{3,1},{4,6},{5,7},{6,4},{7,5},{8,10},{9,11},{10,... | collective-permute-start | bytes 589832 | tf_op jit(solution)/shard_map/ppermute | solution.py:139
  7.6 17.4 %collective-permute-start.9 = (bf16[48,2048]{1,0:T(8,128)(2,1)S(1)}, bf16[48,2048]{1,0:T(8,128)(2,1)S(1)}, u32[]{:S(2)}, u32[]{:S(2)}) collective-permute-start(bf16[48,2048]{1,0:T(8,128)(2,1)S(1)} %get-tuple-element.40), channel_id=1, source_target_pairs={{0,3},{1,2},{2,1},{3,0},{4,7},{5,6},{6,5},{7,4},{8,11},{9,10},{10,... | collective-permute-start | bytes 589832 | tf_op jit(solution)/shard_map/ppermute | solution.py:139
  7.6 17.5 %collective-permute-start.10 = (bf16[48,2048]{1,0:T(8,128)(2,1)S(1)}, bf16[48,2048]{1,0:T(8,128)(2,1)S(1)}, u32[]{:S(2)}, u32[]{:S(2)}) collective-permute-start(bf16[48,2048]{1,0:T(8,128)(2,1)S(1)} %get-tuple-element.41), channel_id=1, source_target_pairs={{0,4},{1,5},{2,6},{3,7},{4,0},{5,1},{6,2},{7,3},{8,12},{9,13},{10,... | collective-permute-start | bytes 589832 | tf_op jit(solution)/shard_map/ppermute | solution.py:139
  10.4 17.2 %collective-permute-start.11 = (bf16[48,2048]{1,0:T(8,128)(2,1)S(1)}, bf16[48,2048]{1,0:T(8,128)(2,1)S(1)}, u32[]{:S(2)}, u32[]{:S(2)}) collective-permute-start(bf16[48,2048]{1,0:T(8,128)(2,1)S(1)} %get-tuple-element.42), channel_id=1, source_target_pairs={{0,5},{1,4},{2,7},{3,6},{4,1},{5,0},{6,3},{7,2},{8,13},{9,12},{10,... | collective-permute-start | bytes 589832 | tf_op jit(solution)/shard_map/ppermute | solution.py:139
  10.4 1.9 %copy-start = (bf16[1,768,2048]{2,1,0:T(8,128)(2,1)S(1)}, bf16[1,768,2048]{2,1,0:T(8,128)(2,1)}, u32[]{:S(2)}) copy-start(bf16[1,768,2048]{2,1,0:T(8,128)(2,1)} %param.8) | copy-start | bytes 9437188
  12.3 59.3 %copy-start.1 = (bf16[1,768,2048]{2,1,0:T(8,128)(2,1)S(1)}, bf16[1,768,2048]{2,1,0:T(8,128)(2,1)}, u32[]{:S(2)}) copy-start(bf16[1,768,2048]{2,1,0:T(8,128)(2,1)} %param.8) | copy-start | bytes 9437188
  14.9 62.8 %copy-start.3 = (bf16[128,2048]{1,0:T(8,128)(2,1)S(1)}, bf16[128,2048]{1,0:T(8,128)(2,1)}, u32[]{:S(2)}) copy-start(bf16[128,2048]{1,0:T(8,128)(2,1)} %dout_ref.3) | copy-start | bytes 1572868
  14.9 23.4 %collective-permute-start.12 = (bf16[48,2048]{1,0:T(8,128)(2,1)S(1)}, bf16[48,2048]{1,0:T(8,128)(2,1)S(1)}, u32[]{:S(2)}, u32[]{:S(2)}) collective-permute-start(bf16[48,2048]{1,0:T(8,128)(2,1)S(1)} %get-tuple-element.43), channel_id=1, source_target_pairs={{0,6},{1,7},{2,4},{3,5},{4,2},{5,3},{6,0},{7,1},{8,14},{9,15},{10,... | collective-permute-start | bytes 589832 | tf_op jit(solution)/shard_map/ppermute | solution.py:139
  21.3 19.8 %collective-permute-start.13 = (bf16[48,2048]{1,0:T(8,128)(2,1)S(1)}, bf16[48,2048]{1,0:T(8,128)(2,1)S(1)}, u32[]{:S(2)}, u32[]{:S(2)}) collective-permute-start(bf16[48,2048]{1,0:T(8,128)(2,1)S(1)} %get-tuple-element.44), channel_id=1, source_target_pairs={{0,7},{1,6},{2,5},{3,4},{4,3},{5,2},{6,1},{7,0},{8,15},{9,14},{10,... | collective-permute-start | bytes 589832 | tf_op jit(solution)/shard_map/ppermute | solution.py:139
  25.0 22.5 %collective-permute-start = (bf16[48,2048]{1,0:T(8,128)(2,1)S(1)}, bf16[48,2048]{1,0:T(8,128)(2,1)S(1)}, u32[]{:S(2)}, u32[]{:S(2)}) collective-permute-start(bf16[48,2048]{1,0:T(8,128)(2,1)S(1)} %get-tuple-element.28), channel_id=1, source_target_pairs={{0,1},{1,0},{2,3},{3,2},{4,5},{5,4},{6,7},{7,6},{8,9},{9,8},{10,11... | collective-permute-start | bytes 589832 | tf_op jit(solution)/shard_map/ppermute | solution.py:139
  25.1 51.2 %collective-permute-start.16 = (bf16[8,48,768]{2,1,0:T(8,128)(2,1)}, bf16[8,48,768]{2,1,0:T(8,128)(2,1)S(1)}, u32[]{:S(2)}, u32[]{:S(2)}) collective-permute-start(bf16[8,48,768]{2,1,0:T(8,128)(2,1)} %bitcast.hidden_ref.refs_0_), channel_id=1, source_target_pairs={{0,24},{8,16},{16,8},{24,0},{1,25},{9,17},{17,9},{25,1},{2,26},{10... | collective-permute-start | bytes 1769480 | tf_op jit(solution)/shard_map/ppermute | solution.py:139
  27.6 20.2 %collective-permute-start.1 = (bf16[48,2048]{1,0:T(8,128)(2,1)S(1)}, bf16[48,2048]{1,0:T(8,128)(2,1)S(1)}, u32[]{:S(2)}, u32[]{:S(2)}) collective-permute-start(bf16[48,2048]{1,0:T(8,128)(2,1)S(1)} %get-tuple-element.29), channel_id=1, source_target_pairs={{0,2},{1,3},{2,0},{3,1},{4,6},{5,7},{6,4},{7,5},{8,10},{9,11},{10,... | collective-permute-start | bytes 589832 | tf_op jit(solution)/shard_map/ppermute | solution.py:139
  38.3 11.1 %collective-permute-start.2 = (bf16[48,2048]{1,0:T(8,128)(2,1)S(1)}, bf16[48,2048]{1,0:T(8,128)(2,1)S(1)}, u32[]{:S(2)}, u32[]{:S(2)}) collective-permute-start(bf16[48,2048]{1,0:T(8,128)(2,1)S(1)} %get-tuple-element.30), channel_id=1, source_target_pairs={{0,3},{1,2},{2,1},{3,0},{4,7},{5,6},{6,5},{7,4},{8,11},{9,10},{10,... | collective-permute-start | bytes 589832 | tf_op jit(solution)/shard_map/ppermute | solution.py:139
  41.1 24.8 %collective-permute-start.3 = (bf16[48,2048]{1,0:T(8,128)(2,1)S(1)}, bf16[48,2048]{1,0:T(8,128)(2,1)S(1)}, u32[]{:S(2)}, u32[]{:S(2)}) collective-permute-start(bf16[48,2048]{1,0:T(8,128)(2,1)S(1)} %get-tuple-element.31), channel_id=1, source_target_pairs={{0,4},{1,5},{2,6},{3,7},{4,0},{5,1},{6,2},{7,3},{8,12},{9,13},{10,... | collective-permute-start | bytes 589832 | tf_op jit(solution)/shard_map/ppermute | solution.py:139
  47.5 22.6 %collective-permute-start.4 = (bf16[48,2048]{1,0:T(8,128)(2,1)S(1)}, bf16[48,2048]{1,0:T(8,128)(2,1)S(1)}, u32[]{:S(2)}, u32[]{:S(2)}) collective-permute-start(bf16[48,2048]{1,0:T(8,128)(2,1)S(1)} %get-tuple-element.32), channel_id=1, source_target_pairs={{0,5},{1,4},{2,7},{3,6},{4,1},{5,0},{6,3},{7,2},{8,13},{9,12},{10,... | collective-permute-start | bytes 589832 | tf_op jit(solution)/shard_map/ppermute | solution.py:139
  47.8 32.4 %collective-permute-start.15 = (bf16[8,48,768]{2,1,0:T(8,128)(2,1)}, bf16[8,48,768]{2,1,0:T(8,128)(2,1)S(1)}, u32[]{:S(2)}, u32[]{:S(2)}) collective-permute-start(bf16[8,48,768]{2,1,0:T(8,128)(2,1)} %bitcast.hidden_ref.refs_0_), channel_id=1, source_target_pairs={{0,16},{8,24},{16,0},{24,8},{1,17},{9,25},{17,1},{25,9},{2,18},{10... | collective-permute-start | bytes 1769480 | tf_op jit(solution)/shard_map/ppermute | solution.py:139
  49.4 24.9 %collective-permute-start.5 = (bf16[48,2048]{1,0:T(8,128)(2,1)S(1)}, bf16[48,2048]{1,0:T(8,128)(2,1)S(1)}, u32[]{:S(2)}, u32[]{:S(2)}) collective-permute-start(bf16[48,2048]{1,0:T(8,128)(2,1)S(1)} %get-tuple-element.33), channel_id=1, source_target_pairs={{0,6},{1,7},{2,4},{3,5},{4,2},{5,3},{6,0},{7,1},{8,14},{9,15},{10,... | collective-permute-start | bytes 589832 | tf_op jit(solution)/shard_map/ppermute | solution.py:139
  65.9 8.9 %collective-permute-start.6 = (bf16[48,2048]{1,0:T(8,128)(2,1)S(1)}, bf16[48,2048]{1,0:T(8,128)(2,1)S(1)}, u32[]{:S(2)}, u32[]{:S(2)}) collective-permute-start(bf16[48,2048]{1,0:T(8,128)(2,1)S(1)} %get-tuple-element.34), channel_id=1, source_target_pairs={{0,7},{1,6},{2,5},{3,4},{4,3},{5,2},{6,1},{7,0},{8,15},{9,14},{10,... | collective-permute-start | bytes 589832 | tf_op jit(solution)/shard_map/ppermute | solution.py:139
  70.1 16.4 %collective-permute-start.14 = (bf16[8,48,768]{2,1,0:T(8,128)(2,1)}, bf16[8,48,768]{2,1,0:T(8,128)(2,1)S(1)}, u32[]{:S(2)}, u32[]{:S(2)}) collective-permute-start(bf16[8,48,768]{2,1,0:T(8,128)(2,1)} %bitcast.hidden_ref.refs_0_), channel_id=1, source_target_pairs={{0,8},{8,0},{16,24},{24,16},{1,9},{9,1},{17,25},{25,17},{2,10},{10... | collective-permute-start | bytes 1769480 | tf_op jit(solution)/shard_map/ppermute | solution.py:139
  74.2 20.7 %collective-permute-start.17 = (bf16[384,512]{1,0:T(8,128)(2,1)}, bf16[384,512]{1,0:T(8,128)(2,1)S(1)}, u32[]{:S(2)}, u32[]{:S(2)}) collective-permute-start(bf16[384,512]{1,0:T(8,128)(2,1)} %get-tuple-element.47), channel_id=1, source_target_pairs={{0,8},{8,0},{16,24},{24,16},{1,9},{9,1},{17,25},{25,17},{2,10},{10... | collective-permute-start | bytes 1179656 | tf_op jit(solution)/shard_map/ppermute | solution.py:139
  74.8 20.2 %collective-permute-start.18 = (bf16[384,512]{1,0:T(8,128)(2,1)}, bf16[384,512]{1,0:T(8,128)(2,1)S(1)}, u32[]{:S(2)}, u32[]{:S(2)}) collective-permute-start(bf16[384,512]{1,0:T(8,128)(2,1)} %get-tuple-element.48), channel_id=1, source_target_pairs={{0,16},{8,24},{16,0},{24,8},{1,17},{9,25},{17,1},{25,9},{2,18},{10... | collective-permute-start | bytes 1179656 | tf_op jit(solution)/shard_map/ppermute | solution.py:139
  76.3 27.2 %collective-permute-start.19 = (bf16[384,512]{1,0:T(8,128)(2,1)}, bf16[384,512]{1,0:T(8,128)(2,1)S(1)}, u32[]{:S(2)}, u32[]{:S(2)}) collective-permute-start(bf16[384,512]{1,0:T(8,128)(2,1)} %get-tuple-element.49), channel_id=1, source_target_pairs={{0,24},{8,16},{16,8},{24,0},{1,25},{9,17},{17,9},{25,1},{2,26},{10... | collective-permute-start | bytes 1179656 | tf_op jit(solution)/shard_map/ppermute | solution.py:139

commit v2 on v0

--- a/solution.py
+++ b/solution.py
@@ -1,7 +1,436 @@
+import functools
+
 import jax
 import jax.numpy as jnp
 from jax import lax
+from jax.experimental import pallas as pl
+from jax.experimental.pallas import tpu as pltpu
 from jax.sharding import PartitionSpec as P
+
+LINE = 8
+SQUARE = 4
+LANES = 128
+PIECES = 3
+MIB = 1 << 20
+VMEM_ALL = 60
+f32, bf16 = jnp.float32, jnp.bfloat16
+
+
+class Steps:
+    def __init__(self):
+        self.token = None
+
+    def __call__(self, body, outs, args, scratch=(), vmem=40, aliases=None, anywhere=(), anywhere_out=(), pinned=()):
+        aliases = aliases or {}
+        whole = pl.BlockSpec(memory_space=pltpu.VMEM)
+        free = pl.BlockSpec(memory_space=pl.ANY)
+        fixed = pl.BlockSpec(memory_space=pltpu.HBM)
+        in_specs = [
+            fixed if i in pinned else free if i in aliases or i in anywhere else whole
+            for i in range(len(args))
+        ]
+        out_specs = [free if o in aliases.values() or o in anywhere_out else whole for o in range(len(outs))]
+        n_args, n_outs = len(args), len(outs)
+        chained = () if self.token is None else (self.token,)
+
+        def kernel(*refs):
+            rest = refs[n_args + len(chained) :]
+            body(*refs[:n_args], *rest[:n_outs], *rest[n_outs + 1 :])
+
+        *results, self.token = pl.pallas_call(
+            kernel,
+            out_shape=[*outs, jax.ShapeDtypeStruct((8, LANES), f32)],
+            in_specs=in_specs + [free] * len(chained),
+            out_specs=out_specs + [free],
+            scratch_shapes=scratch,
+            input_output_aliases=aliases,
+            compiler_params=pltpu.CompilerParams(vmem_limit_bytes=vmem * MIB),
+            cost_estimate=pl.CostEstimate(flops=0, bytes_accessed=0, transcendentals=0),
+        )(*args, *chained)
+        return results
+
+
+def bf16_like(*shape):
+    return jax.ShapeDtypeStruct(shape, bf16)
+
+
+def f32_like(*shape):
+    return jax.ShapeDtypeStruct(shape, f32)
+
+
+def as_column(row):
+    size = row.shape[1]
+    diagonal = lax.broadcasted_iota(jnp.int32, (size, size), 0) == lax.broadcasted_iota(
+        jnp.int32, (size, size), 1
+    )
+    return jnp.sum(jnp.where(diagonal, row, 0.0), axis=1, keepdims=True)
+
+
+def as_row(column):
+    size = column.shape[0]
+    diagonal = lax.broadcasted_iota(jnp.int32, (size, size), 0) == lax.broadcasted_iota(
+        jnp.int32, (size, size), 1
+    )
+    return jnp.sum(jnp.where(diagonal, column, 0.0), axis=0, keepdims=True)
+
+
+def slot_rows(routing, experts, capacity):
+    picks, tokens = routing.shape
+    line = lax.broadcasted_iota(jnp.int32, (experts, tokens), 0)
+    onehots = [(routing[k : k + 1] == line).astype(f32) for k in range(picks)]
+    counted = functools.reduce(jnp.add, onehots)
+    earlier = lax.broadcasted_iota(jnp.int32, (tokens, tokens), 0) < lax.broadcasted_iota(
+        jnp.int32, (tokens, tokens), 1
+    )
+    before = jnp.dot(counted.astype(bf16), earlier.astype(bf16), preferred_element_type=f32)
+    return [
+        routing[k : k + 1].astype(f32) * capacity + jnp.sum(before * onehots[k], axis=0, keepdims=True)
+        for k in range(picks)
+    ]
+
+
+def rows_for(first, count, slots, gates, dout):
+    tokens = dout.shape[0]
+    here = lax.broadcasted_iota(jnp.int32, (count, tokens), 0).astype(f32) + first
+    hits = [here == row for row in slots]
+    chosen = functools.reduce(jnp.logical_or, hits).astype(bf16)
+    gate = functools.reduce(
+        jnp.add, [jnp.sum(jnp.where(h, g, 0.0), axis=1, keepdims=True) for h, g in zip(hits, gates)]
+    )
+    return (jnp.dot(chosen, dout, preferred_element_type=f32) * gate).astype(bf16)
+
+
+def pick_rows(first, slots_column, rows):
+    lane = lax.broadcasted_iota(jnp.int32, (slots_column.shape[0], rows.shape[0]), 1).astype(f32)
+    return jnp.dot((lane == slots_column - first).astype(bf16), rows, preferred_element_type=f32)
+
+
+def message_body(capacity, routing_at, gates_at, dout_at, *refs):
+    message_ref, *slot_refs = refs[:5]
+    routing_ref, gates_ref, dout_ref, sems = refs[5:]
+    moves = [
+        pltpu.make_async_copy(a, b, sems.at[i])
+        for i, (a, b) in enumerate(
+            (
+                (routing_at, routing_ref),
+                (gates_at, gates_ref),
+                (dout_at, dout_ref),
+            )
+        )
+    ]
+    for move in moves:
+        move.start()
+    for move in moves:
+        move.wait()
+    me = lax.axis_index("expert")
+    picks, tokens = routing_ref.shape
+    routing = routing_ref[...]
+    slots = slot_rows(routing, LINE, capacity)
+    gates = [gates_ref[k : k + 1] for k in range(picks)]
+    dout = dout_ref[...]
+    for m, ref in enumerate(slot_refs):
+        first = ((me ^ m) * capacity).astype(f32)
+        ref[...] = rows_for(first, capacity, slots, gates, dout)
+    lines = []
+    for k in range(picks):
+        expert = routing[k : k + 1].astype(f32)
+        lines += [expert, slots[k] - expert * capacity]
+        left = gates[k]
+        for _ in range(PIECES):
+            piece = left.astype(bf16).astype(f32)
+            lines.append(piece)
+            left = left - piece
+    lines.append(jnp.zeros((LANES - len(lines), tokens), f32))
+    width = dout.shape[1]
+    message_ref[:, :width] = dout
+    message_ref[:, width:] = jnp.concatenate(lines, axis=0).T.astype(bf16)
+
+
+def read_message(message_ref, picks, capacity):
+    width = message_ref.shape[1] - LANES
+    lines = message_ref[:, width:].astype(f32).T
+    slots, gates = [], []
+    for k in range(picks):
+        at = k * (2 + PIECES)
+        slots.append(lines[at : at + 1] * capacity + lines[at + 1 : at + 2])
+        gates.append(jnp.sum(lines[at + 2 : at + 2 + PIECES], axis=0, keepdims=True))
+    return slots, gates, message_ref[:, :width]
+
+
+def rows_body(capacity, hidden_ref, weight_ref, *out_refs):
+    me = lax.axis_index("expert")
+    rows = jnp.concatenate([hidden_ref[me ^ m] for m in range(LINE)], axis=0)
+    out = jnp.dot(rows, weight_ref[...], preferred_element_type=f32).astype(bf16)
+    at = 0
+    for ref in out_refs:
+        ref[...] = out[at : at + ref.shape[0]]
+        at += ref.shape[0]
+
+
+def swap_body(*refs):
+    own_ref, *arrived_refs, out_ref = refs
+    count = own_ref.shape[0]
+    out_ref[:count] = own_ref[...]
+    for at, ref in enumerate(arrived_refs, 1):
+        out_ref[at * count : (at + 1) * count] = ref[count:]
+
+
+def relay_body(capacity, picks, message_ref, *out_refs):
+    me = lax.axis_index("expert")
+    slots, gates, dout = read_message(message_ref, picks, capacity)
+    m = 0
+    for ref in out_refs:
+        for at in range(0, ref.shape[0], capacity):
+            first = ((me ^ m) * capacity).astype(f32)
+            ref[at : at + capacity] = rows_for(first, capacity, slots, gates, dout)
+            m += 1
+
+
+def rows_to_hidden(rows, weight_ref, grad_part):
+    grad = lax.dot_general(
+        rows, weight_ref[...], (((1,), (1,)), ((), ())), preferred_element_type=f32
+    ).astype(bf16)
+    capacity = grad_part[0][0].shape[1]
+    for at, (ref, block) in enumerate(grad_part):
+        ref[block] = grad[at * capacity : (at + 1) * capacity]
+
+
+def cut_slices(rows, slice_refs):
+    group = lax.axis_index("dp")
+    width = slice_refs[0].shape[1]
+    for d, part in enumerate(slice_refs):
+        part[...] = rows[:, pl.ds(pl.multiple_of((group ^ d) * width, width), width)]
+
+
+def near_body(capacity, weight_ref, *refs):
+    block_refs, grad_ref, slice_refs, rows = refs[:-6], refs[-6], refs[-5:-1], refs[-1]
+    gather_blocks(capacity, block_refs, rows)
+    rows_to_hidden(rows[...], weight_ref, [(grad_ref, m) for m in range(4)])
+    cut_slices(rows, slice_refs)
+
+
+def gather_blocks(capacity, refs, rows):
+    if len(refs) == 4:
+        parts = [(ref, 0) for ref in refs]
+    else:
+        own, hop, pair = refs
+        parts = [(own, 0), (pair, 0), (hop, 0), (pair, capacity)]
+    for at, (ref, start) in enumerate(parts):
+        rows[at * capacity : (at + 1) * capacity] = ref[start : start + capacity]
+
+
+def far_body(capacity, weight_ref, near_grad_ref, *refs):
+    block_refs, grad_ref, slice_refs, rows = refs[:-6], refs[-6], refs[-5:-1], refs[-1]
+    me = lax.axis_index("expert")
+    gather_blocks(capacity, block_refs, rows)
+    for m in range(4):
+        grad_ref[me ^ m] = near_grad_ref[m]
+    rows_to_hidden(rows[...], weight_ref, [(grad_ref, me ^ m) for m in range(4, LINE)])
+    cut_slices(rows, slice_refs)
+
+
+def pack_body(*refs):
+    hidden_refs, (near_ref, far_ref) = refs[:SQUARE], refs[-2:]
+    me = lax.axis_index("expert")
+    for ref, first in ((near_ref, 0), (far_ref, 4)):
+        rows = jnp.concatenate([h[me ^ (first + m)] for h in hidden_refs for m in range(4)], axis=0)
+        ref[...] = rows.T
+
+
+def weight_body(columns_ref, *refs):
+    slice_refs, others, out_ref = refs[:SQUARE], refs[SQUARE : SQUARE + 1], refs[-1]
+    rows = jnp.concatenate([s[...] for s in slice_refs], axis=0)
+    total = jnp.dot(columns_ref[...], rows, preferred_element_type=f32)
+    for other in others if len(refs) > SQUARE + 1 else ():
+        total = total + other[...]
+    out_ref[...] = total
+
+
+def combine_body(capacity, routing_ref, gates_ref, dout_ref, *refs):
+    *block_refs, combined_ref, grad_gates_ref, rows = refs
+    me = lax.axis_index("expert")
+    picks = gates_ref.shape[0]
+    c = capacity
+    slots = slot_rows(routing_ref[...] ^ me, LINE, c)
+    if len(block_refs) == LINE:
+        parts = [(ref, 0) for ref in block_refs]
+    else:
+        own, *hops, pair = block_refs
+        parts = [(own, 0), (pair, 0)]
+        for at, ref in enumerate(hops, 1):
+            parts += [(ref, 0), (pair, at * c)]
+    for at, (ref, start) in enumerate(parts):
+        rows[at * c : (at + 1) * c] = ref[start : start + c]
+    dout = dout_ref[...].astype(f32)
+    total = 0.0
+    for k in range(picks):
+        picked = pick_rows(0.0, as_column(slots[k]), rows[...])
+        total += as_column(gates_ref[k : k + 1]) * picked
+        grad_gates_ref[k : k + 1] = as_row(jnp.sum(picked * dout, axis=1, keepdims=True))
+    combined_ref[...] = total.astype(bf16)
+
+
+class Plan:
+    def __init__(self, **values):
+        self.values = values
+        self.moves = {}
+        self.run = Steps()
+
+    def move(self, name, source, axis, m):
+        self.moves[name] = (source, axis, m)
+
+    def value(self, name):
+        if name not in self.values:
+            source, axis, m = self.moves[name]
+            size = lax.axis_size(axis)
+            self.values[name] = lax.ppermute(
+                self.value(source), axis, [(i, i ^ m) for i in range(size)]
+            )
+        return self.values[name]
+
+    def step(self, body, outs, ins, waits=(), held=(), **options):
+        n, w, h, o = len(ins), len(waits), len(held), len(outs)
+        args = [self.value(name) for name in (*ins, *waits, *held)]
+
+        def whole(*refs):
+            rest = refs[n + w + h :]
+            body(*refs[:n], *rest[:o], *rest[o + h :])
+
+        results = self.run(
+            whole,
+            [*outs.values(), *(jax.ShapeDtypeStruct(a.shape, a.dtype) for a in args[n + w :])],
+            args,
+            anywhere=tuple(range(n, n + w)),
+            aliases={n + w + k: o + k for k in range(h)},
+            **options,
+        )
+        self.values.update(zip((*outs, *held), results))
+
+
+def on_device(routing, gates, hidden, w_down, dout):
+    capacity, units = hidden.shape[3:]
+    width = w_down.shape[2]
+    tokens, picks = routing.shape
+    part = width // SQUARE
+    plan = Plan(
+        routing=routing.T, gates=gates.T, hidden=hidden[0, 0], weight=w_down[0], dout=dout
+    )
+    step, move = plan.step, plan.move
+
+    def block(count):
+        return bf16_like(count * capacity, width)
+
+    slices = bf16_like(4 * capacity, part)
+    rows_scratch = [pltpu.VMEM((4 * capacity, width), bf16)]
+
+    move("peer1", "hidden", "dp", 1)
+    move("peer2", "hidden", "dp", 2)
+    move("peer3", "peer1", "dp", 2)
+    move("from_afar", "message", "expert", 4)
+    for m in (1, 2, 3):
+        move(f"near{m}", f"slots{m}", "expert", m)
+        move(f"far{m}", f"relay{m}", "expert", m)
+        move(f"near_slice{m}", f"near_cut{m}", "dp", m)
+        move(f"far_slice{m}", f"far_cut{m}", "dp", m)
+    for m in (2, 4, 6):
+        move(f"got{m}", f"rows{m}", "expert", m)
+    move("last", "last_swap", "expert", 1)
+
+    step(
+        functools.partial(message_body, capacity),
+        dict(message=bf16_like(tokens, width + LANES), **{f"slots{m}": block(1) for m in range(4)}),
+        ["routing", "gates", "dout"],
+        scratch=[
+            pltpu.VMEM((picks, tokens), jnp.int32),
+            pltpu.VMEM((picks, tokens), f32),
+            pltpu.VMEM((tokens, width), bf16),
+            pltpu.SemaphoreType.DMA((3,)),
+        ],
+        pinned=(0, 1, 2),
+        vmem=VMEM_ALL,
+    )
+
+    def rows(**o):
+        step(
+            functools.partial(rows_body, capacity),
+            dict(rows0=block(1), rows1=block(1), rows2=block(2), rows4=block(2), rows6=block(2)),
+            ["hidden", "weight"],
+            **o,
+        )
+
+    def near(**o):
+        step(
+            functools.partial(near_body, capacity),
+            dict(near_grad=bf16_like(4, capacity, units), **{f"near_cut{d}": slices for d in range(SQUARE)}),
+            ["weight", "slots0", "near1", "near2", "near3"],
+            scratch=rows_scratch,
+            **o,
+        )
+
+    def relay(**o):
+        step(
+            functools.partial(relay_body, capacity, picks),
+            {f"relay{m}": block(1) for m in range(4)},
+            ["from_afar"],
+            **o,
+        )
+
+    def pack(**o):
+        step(
+            pack_body,
+            dict(near_columns=bf16_like(units, SQUARE * 4 * capacity), far_columns=bf16_like(units, SQUARE * 4 * capacity)),
+            ["hidden", "peer1", "peer2", "peer3"],
+            **o,
+        )
+
+    def near_weight(**o):
+        step(
+            weight_body,
+            dict(near_weight=f32_like(units, part)),
+            ["near_columns", "near_cut0", "near_slice1", "near_slice2", "near_slice3"],
+            **o,
+        )
+
+    def far(**o):
+        step(
+            functools.partial(far_body, capacity),
+            dict(grad_hidden=bf16_like(LINE, capacity, units), **{f"far_cut{d}": slices for d in range(SQUARE)}),
+            ["weight", "near_grad", "relay0", "far1", "far2", "far3"],
+            scratch=rows_scratch,
+            **o,
+        )
+
+    def far_weight(**o):
+        step(
+            weight_body,
+            dict(grad_down=f32_like(units, part)),
+            ["far_columns", "far_cut0", "far_slice1", "far_slice2", "far_slice3", "near_weight"],
+            **o,
+        )
+
+    def last_swap(**o):
+        step(swap_body, dict(last_swap=block(4)), ["rows1", "got2", "got4", "got6"], **o)
+
+    def combine(**o):
+        step(
+            functools.partial(combine_body, capacity),
+            dict(combined=bf16_like(tokens, width), grad_gates=f32_like(picks, tokens)),
+            ["routing", "gates", "dout", "rows0", "got2", "got4", "got6", "last"],
+            scratch=[pltpu.VMEM((LINE * capacity, width), bf16)],
+            **o,
+        )
+
+    rows()
+    near()
+    relay(waits=["near_slice1", "near_slice2"], held=["rows4", "rows6"])
+    far(waits=["got6", "got2"])
+    pack()
+    near_weight()
+    far_weight(waits=["got4"])
+    last_swap()
+    combine()
+    v = plan.values
+    return (v["combined"], v["grad_gates"].T, v["grad_hidden"][None, None], v["grad_down"][None])
 
 
 def slot_index(routing, experts, capacity):
@@ -12,7 +441,7 @@
     return flattened * capacity + ranking
 
 
-def on_device(routing, gates, hidden, w_down, dout):
+def on_device_any(routing, gates, hidden, w_down, dout):
     experts = lax.axis_size("expert")
     capacity = hidden.shape[3]
     hidden_units = w_down.shape[1]
@@ -60,8 +489,9 @@
         P("expert", None, None),
         P(("dp", "expert"), None),
     )
+    planned = mesh.shape["expert"] == LINE and mesh.shape["dp"] == SQUARE
     return jax.shard_map(
-        on_device,
+        on_device if planned else on_device_any,
         mesh=mesh,
         in_specs=placed,
         out_specs=(

time: 150 us -> 82.5 us (0.55)
  blocking collectives: 44.3 us -> 0 us
  starting transfers between devices: 4.53 us -> 24.7 us
  local copies, waits for them, and re-layouts: 22.4 us -> 3.65 us
  other arithmetic: 16.2 us -> 0 us
  between operations: 14.1 us -> 0.74 us
  Pallas kernels: 0 us -> 12.9 us
  matrix products: 10.8 us -> 0 us
  waiting for transfers between devices: 37.3 us -> 40.2 us
    all_to_all x1 -> x0, blocking collectives: 44.3 us -> none  [on_device(): lax.all_to_all(slot_grads, 'expert', split_axis=0, concat_axis=0, tiled=T...]
    ppermute x0 -> x20, waiting for transfers between devices: none -> 40.2 us  [value(): lax.ppermute(self.value(source), axis, [(i, i ^ m) for i in range(size)])]
    all_to_all x1 -> x0, waiting for transfers between devices: 37.3 us -> none  [on_device(): lax.all_to_all(outputs, 'expert', split_axis=0, concat_axis=0, tiled=True)]
    ppermute x0 -> x20, starting transfers between devices: none -> 24.7 us  [value(): lax.ppermute(self.value(source), axis, [(i, i ^ m) for i in range(size)])]
    pallas_call x0 -> x10, Pallas kernels: none -> 12.9 us  [__call__(): pl.pallas_call(kernel, out_shape=[*outs, jax.ShapeDtypeStruct((8, LANES),...]
    dot_general x3 -> x0, matrix products: 10.8 us -> none  [the longest x1 3.65 us: on_device(): lax.dot_general(flattened, weight, (((1,), (1,)), ((), ())), preferred_el...]
    reduce_sum x3 -> x0, other arithmetic: 8.61 us -> none  [the longest x1 6.24 us: on_device(): combined = jnp.sum(gates[..., None] * picked, axis=1).astype(jnp.bfloat16)]
    gather x2 -> x0, local copies, waits for them, and re-layouts: 7.46 us -> none  [on_device(): jnp.take(returned.reshape(experts * capacity, model_width), location, axi...]
  transfers between devices with their start and end apart: 2 -> 20, of which waited for: 1 -> 9; matrix products, arithmetic and copies ran while one was open for 16% -> 0% of each run, Pallas kernels for 0% -> 11%
where the time goes in v2:
time: 82.5 us; the launch traced here: 82.3 us
  waiting for transfers between devices  40.2 us (49%)
  starting transfers between devices  24.7 us (30%)
  Pallas kernels  12.9 us (16%)
  local copies, waits for them, and re-layouts  3.65 us (4%)
    ppermute x20, waiting for transfers between devices, value(): lax.ppermute(self.value(source), axis, [(i, i ^ m) for i in range(size)])  40.2 us
    ppermute x20, starting transfers between devices, value(): lax.ppermute(self.value(source), axis, [(i, i ^ m) for i in range(size)])  24.7 us
    pallas_call x10, Pallas kernels, __call__(): pl.pallas_call(kernel, out_shape=[*outs, jax.ShapeDtypeStruct((8, LANES),...  12.9 us
    unnamed x18, local copies, waits for them, and re-layouts  3.65 us
  transfers between devices with their start and end apart: 20, of which 9 were waited for; matrix products, arithmetic and copies ran while one was open for 0% of the time, Pallas kernels for 11%

profile of v2, /device:TPU:0, one launch (start us, length us, event | category | flops | bytes accessed | tf_op | source)
XLA Modules:
  0.0 82.3 jit_solution(12615674314857415338)
XLA Ops:
  0.6 3.0 %collective-permute-start.9 = (bf16[8,48,768]{2,1,0:T(8,128)(2,1)}, bf16[8,48,768]{2,1,0:T(8,128)(2,1)S(1)}, u32[]{:S(2)}, u32[]{:S(2)}) collective-permute-start(bf16[8,48,768]{2,1,0:T(8,128)(2,1)} %bitcast.10), channel_id=1, source_target_pairs={{0,8},{8,0},{16,24},{24,16},{1,9},{9,1},{17,25},{25,17},{2,10},{10... | collective-permute-start | bytes 1769480 | tf_op jit(solution)/shard_map/ppermute | solution.py:286
  3.6 2.5 %shard_map.84 = (bf16[128,2176]{1,0:T(8,128)(2,1)}, bf16[48,2048]{1,0:T(8,128)(2,1)}, bf16[48,2048]{1,0:T(8,128)(2,1)}, bf16[48,2048]{1,0:T(8,128)(2,1)}, bf16[48,2048]{1,0:T(8,128)(2,1)}, /*index=5*/f32[8,128]{1,0:T(8,128)}) custom-call(s32[2,128]{1,0:T(2,128)} %bitcast.14, f32[2,128]{1,0:T(2,128)} %bitcast.16, bf16[128,2048]{1,0:T(8,128)(2,1)} %refs_2_.3), custom_call_target="tpu_custom_call" | custom-call | tf_op jit(solution)/shard_map/pallas_call | solution.py:40
  6.3 1.6 %collective-permute-start.3 = (bf16[48,2048]{1,0:T(8,128)(2,1)}, bf16[48,2048]{1,0:T(8,128)(2,1)S(1)}, u32[]{:S(2)}, u32[]{:S(2)}) collective-permute-start(bf16[48,2048]{1,0:T(8,128)(2,1)} %get-tuple-element.52), channel_id=1, source_target_pairs={{0,2},{1,3},{2,0},{3,1},{4,6},{5,7},{6,4},{7,5},{8,10},{9,11},{10,... | collective-permute-start | bytes 589832 | tf_op jit(solution)/shard_map/ppermute | solution.py:286
  8.1 2.6 %collective-permute-start.1 = (bf16[128,2176]{1,0:T(8,128)(2,1)}, bf16[128,2176]{1,0:T(8,128)(2,1)S(1)}, u32[]{:S(2)}, u32[]{:S(2)}) collective-permute-start(bf16[128,2176]{1,0:T(8,128)(2,1)} %get-tuple-element.49), channel_id=1, source_target_pairs={{0,4},{1,5},{2,6},{3,7},{4,0},{5,1},{6,2},{7,3},{8,12},{9,13},{10,... | collective-permute-start | bytes 1671176 | tf_op jit(solution)/shard_map/ppermute | solution.py:286
  10.7 1.9 %copy-done = bf16[1,768,2048]{2,1,0:T(8,128)(2,1)S(1)} copy-done((bf16[1,768,2048]{2,1,0:T(8,128)(2,1)S(1)}, bf16[1,768,2048]{2,1,0:T(8,128)(2,1)}, u32[]{:S(2)}) %copy-start) | copy-done | bytes 3145752
  12.6 1.1 %copy-done.2 = bf16[1,1,8,48,768]{4,3,2,1,0:T(8,128)(2,1)S(1)} copy-done((bf16[1,1,8,48,768]{4,3,2,1,0:T(8,128)(2,1)S(1)}, bf16[1,1,8,48,768]{4,3,2,1,0:T(8,128)(2,1)}, u32[]{:S(2)}) %copy-start.2) | copy-done | bytes 589848
  13.7 0.7 copy-done.8
  14.3 1.4 %shard_map.85 = (bf16[48,2048]{1,0:T(8,128)(2,1)S(1)}, bf16[48,2048]{1,0:T(8,128)(2,1)S(1)}, bf16[96,2048]{1,0:T(8,128)(2,1)S(1)}, bf16[96,2048]{1,0:T(8,128)(2,...) custom-call(bf16[8,48,768]{2,1,0:T(8,128)(2,1)S(1)} %bitcast.11, bf16[768,2048]{1,0:T(8,128)(2,1)S(1)} %bitcast.7, ...), custom_call_target="tpu_custom_call" | custom-call | tf_op jit(solution)/shard_map/pallas_call | solution.py:40
  15.8 1.6 %collective-permute-start = (bf16[96,2048]{1,0:T(8,128)(2,1)S(1)}, bf16[96,2048]{1,0:T(8,128)(2,1)S(1)}, u32[]{:S(2)}, u32[]{:S(2)}) collective-permute-start(bf16[96,2048]{1,0:T(8,128)(2,1)S(1)} %get-tuple-element.48), channel_id=1, source_target_pairs={{0,2},{1,3},{2,0},{3,1},{4,6},{5,7},{6,4},{7,5},{8,10},{9,11},{10,... | collective-permute-start | bytes 1179656 | tf_op jit(solution)/shard_map/ppermute | solution.py:286
  17.4 4.8 %collective-permute-done.3.refs_3_ = bf16[48,2048]{1,0:T(8,128)(2,1)S(1)} collective-permute-done((bf16[48,2048]{1,0:T(8,128)(2,1)}, bf16[48,2048]{1,0:T(8,128)(2,1)S(1)}, u32[]{:S(2)}, u32[]{:S(2)}) %collective-permute-start.3) | collective-permute-done | bytes 196640 | tf_op jit(solution)/shard_map/ppermute | solution.py:286
  22.1 3.3 %collective-permute-done.4.refs_4_ = bf16[48,2048]{1,0:T(8,128)(2,1)S(1)} collective-permute-done((bf16[48,2048]{1,0:T(8,128)(2,1)}, bf16[48,2048]{1,0:T(8,128)(2,1)S(1)}, u32[]{:S(2)}, u32[]{:S(2)}) %collective-permute-start.4) | collective-permute-done | bytes 196640 | tf_op jit(solution)/shard_map/ppermute | solution.py:286
  25.5 1.2 %shard_map.86 = (bf16[4,48,768]{2,1,0:T(8,128)(2,1)S(1)}, bf16[192,512]{1,0:T(8,128)(2,1)S(1)}, bf16[192,512]{1,0:T(8,128)(2,1)S(1)}, bf16[192,512]{1,0:T(8,128)...) custom-call(bf16[768,2048]{1,0:T(8,128)(2,1)S(1)} %bitcast.8, bf16[48,2048]{1,0:T(8,128)(2,1)S(1)} %copy-done.5, ...), custom_call_target="tpu_custom_call" | custom-call | tf_op jit(solution)/shard_map/pallas_call | solution.py:40
  26.7 0.7 collective-permute-start.5
  27.4 1.5 %collective-permute-start.6 = (bf16[192,512]{1,0:T(8,128)(2,1)S(1)}, bf16[192,512]{1,0:T(8,128)(2,1)S(1)}, u32[]{:S(2)}, u32[]{:S(2)}) collective-permute-start(bf16[192,512]{1,0:T(8,128)(2,1)S(1)} %get-tuple-element.56), channel_id=1, source_target_pairs={{0,16},{8,24},{16,0},{24,8},{1,17},{9,25},{17,1},{25,9},{2,18},{10... | collective-permute-start | bytes 589832 | tf_op jit(solution)/shard_map/ppermute | solution.py:286
  28.8 5.6 %collective-permute-done.5.refs_1_.refs_2_ = bf16[192,512]{1,0:T(8,128)(2,1)S(1)} collective-permute-done((bf16[192,512]{1,0:T(8,128)(2,1)S(1)}, bf16[192,512]{1,0:T(8,128)(2,1)S(1)}, u32[]{:S(2)}, u32[]{:S(2)}) %collective-permute-start.5) | collective-permute-done | bytes 196640 | tf_op jit(solution)/shard_map/ppermute | solution.py:286
  34.5 1.6 %collective-permute-start.10 = (bf16[8,48,768]{2,1,0:T(8,128)(2,1)S(1)}, bf16[8,48,768]{2,1,0:T(8,128)(2,1)S(1)}, u32[]{:S(2)}, u32[]{:S(2)}) collective-permute-start(bf16[8,48,768]{2,1,0:T(8,128)(2,1)S(1)} %bitcast.12), channel_id=1, source_target_pairs={{0,16},{8,24},{16,0},{24,8},{1,17},{9,25},{17,1},{25,9},{2,18},{10... | collective-permute-start | bytes 1769480 | tf_op jit(solution)/shard_map/ppermute | solution.py:286
  37.1 3.3 %collective-permute-start.8 = (bf16[96,2048]{1,0:T(8,128)(2,1)S(1)}, bf16[96,2048]{1,0:T(8,128)(2,1)S(1)}, u32[]{:S(2)}, u32[]{:S(2)}) collective-permute-start(bf16[96,2048]{1,0:T(8,128)(2,1)S(1)} %get-tuple-element.61), channel_id=1, source_target_pairs={{0,6},{1,7},{2,4},{3,5},{4,2},{5,3},{6,0},{7,1},{8,14},{9,15},{10,... | collective-permute-start | bytes 1179656 | tf_op jit(solution)/shard_map/ppermute | solution.py:286
  40.4 1.5 %collective-permute-start.14 = (bf16[48,2048]{1,0:T(8,128)(2,1)S(1)}, bf16[48,2048]{1,0:T(8,128)(2,1)S(1)}, u32[]{:S(2)}, u32[]{:S(2)}) collective-permute-start(bf16[48,2048]{1,0:T(8,128)(2,1)S(1)} %get-tuple-element.67), channel_id=1, source_target_pairs={{0,3},{1,2},{2,1},{3,0},{4,7},{5,6},{6,5},{7,4},{8,11},{9,10},{10,... | collective-permute-start | bytes 589832 | tf_op jit(solution)/shard_map/ppermute | solution.py:286
  41.9 12.9 %collective-permute-done.13.refs_4_ = bf16[48,2048]{1,0:T(8,128)(2,1)S(1)} collective-permute-done((bf16[48,2048]{1,0:T(8,128)(2,1)S(1)}, bf16[48,2048]{1,0:T(8,128)(2,1)S(1)}, u32[]{:S(2)}, u32[]{:S(2)}) %collective-permute-start.13) | collective-permute-done | bytes 196640 | tf_op jit(solution)/shard_map/ppermute | solution.py:286
  54.8 1.3 %collective-permute-start.7 = (bf16[96,2048]{1,0:T(8,128)(2,1)S(1)}, bf16[96,2048]{1,0:T(8,128)(2,1)S(1)}, u32[]{:S(2)}, u32[]{:S(2)}) collective-permute-start(bf16[96,2048]{1,0:T(8,128)(2,1)S(1)} %get-tuple-element.60), channel_id=1, source_target_pairs={{0,4},{1,5},{2,6},{3,7},{4,0},{5,1},{6,2},{7,3},{8,12},{9,13},{10,... | collective-permute-start | bytes 1179656 | tf_op jit(solution)/shard_map/ppermute | solution.py:286
  56.1 3.5 %collective-permute-done.14.refs_5_ = bf16[48,2048]{1,0:T(8,128)(2,1)S(1)} collective-permute-done((bf16[48,2048]{1,0:T(8,128)(2,1)S(1)}, bf16[48,2048]{1,0:T(8,128)(2,1)S(1)}, u32[]{:S(2)}, u32[]{:S(2)}) %collective-permute-start.14) | collective-permute-done | bytes 196640 | tf_op jit(solution)/shard_map/ppermute | solution.py:286
  59.6 1.5 %collective-permute-start.18 = (bf16[192,512]{1,0:T(8,128)(2,1)S(1)}, bf16[192,512]{1,0:T(8,128)(2,1)S(1)}, u32[]{:S(2)}, u32[]{:S(2)}) collective-permute-start(bf16[192,512]{1,0:T(8,128)(2,1)S(1)} %get-tuple-element.77), channel_id=1, source_target_pairs={{0,24},{8,16},{16,8},{24,0},{1,25},{9,17},{17,9},{25,1},{2,26},{10... | collective-permute-start | bytes 589832 | tf_op jit(solution)/shard_map/ppermute | solution.py:286
  61.2 2.1 %shard_map.88 = (bf16[8,48,768]{2,1,0:T(8,128)(2,1)}, bf16[192,512]{1,0:T(8,128)(2,1)S(1)}, bf16[192,512]{1,0:T(8,128)(2,1)S(1)}, bf16[192,512]{1,0:T(8,128)(2,1...) custom-call(bf16[768,2048]{1,0:T(8,128)(2,1)S(1)} %bitcast.9, ...), custom_call_target="tpu_custom_call" | custom-call | tf_op jit(solution)/shard_map/pallas_call | solution.py:40
  63.2 1.5 %collective-permute-start.15 = (bf16[192,512]{1,0:T(8,128)(2,1)S(1)}, bf16[192,512]{1,0:T(8,128)(2,1)S(1)}, u32[]{:S(2)}, u32[]{:S(2)}) collective-permute-start(bf16[192,512]{1,0:T(8,128)(2,1)S(1)} %get-tuple-element.72), channel_id=1, source_target_pairs={{0,8},{8,0},{16,24},{24,16},{1,9},{9,1},{17,25},{25,17},{2,10},{10... | collective-permute-start | bytes 589832 | tf_op jit(solution)/shard_map/ppermute | solution.py:286
  65.2 1.5 %collective-permute-start.17 = (bf16[192,512]{1,0:T(8,128)(2,1)S(1)}, bf16[192,512]{1,0:T(8,128)(2,1)S(1)}, u32[]{:S(2)}, u32[]{:S(2)}) collective-permute-start(bf16[192,512]{1,0:T(8,128)(2,1)S(1)} %get-tuple-element.74), channel_id=1, source_target_pairs={{0,24},{8,16},{16,8},{24,0},{1,25},{9,17},{17,9},{25,1},{2,26},{10... | collective-permute-start | bytes 589832 | tf_op jit(solution)/shard_map/ppermute | solution.py:286
  67.4 0.9 %collective-permute-done.18.refs_4_ = bf16[192,512]{1,0:T(8,128)(2,1)S(1)} collective-permute-done((bf16[192,512]{1,0:T(8,128)(2,1)S(1)}, bf16[192,512]{1,0:T(8,128)(2,1)S(1)}, u32[]{:S(2)}, u32[]{:S(2)}) %collective-permute-start.18) | collective-permute-done | bytes 196640 | tf_op jit(solution)/shard_map/ppermute | solution.py:286
  68.3 0.8 shard_map.90
  69.0 6.1 %collective-permute-done.7.refs_6_.refs_2_.refs_5_ = bf16[96,2048]{1,0:T(8,128)(2,1)S(1)} collective-permute-done((bf16[96,2048]{1,0:T(8,128)(2,1)S(1)}, bf16[96,2048]{1,0:T(8,128)(2,1)S(1)}, u32[]{:S(2)}, u32[]{:S(2)}) %collective-permute-start.7) | collective-permute-done | bytes 393248 | tf_op jit(solution)/shard_map/ppermute | solution.py:286
  75.1 0.9 %collective-permute-done.17.refs_4_ = bf16[192,512]{1,0:T(8,128)(2,1)S(1)} collective-permute-done((bf16[192,512]{1,0:T(8,128)(2,1)S(1)}, bf16[192,512]{1,0:T(8,128)(2,1)S(1)}, u32[]{:S(2)}, u32[]{:S(2)}) %collective-permute-start.17) | collective-permute-done | bytes 196640 | tf_op jit(solution)/shard_map/ppermute | solution.py:286
  76.1 1.9 %shard_map.91 = (f32[768,512]{1,0:T(8,128)}, f32[8,128]{1,0:T(8,128)S(1)}) custom-call(bf16[768,768]{1,0:T(8,128)(2,1)S(1)} %get-tuple-element.70.refs_0_, bf16[192,512]{1,0:T(8,128)(2,1)S(1)} %get-tuple-element.71.refs_1_, bf16[192,512]{1,0:T(8,128)(2,1)S(1)} %collective-permute-done.15.refs_2_, bf16[192,512]{1,0:T(8,128)(2,1)S(1)} %collective-permute-done.16.refs_3_, ...), custom_call_target="tpu_custom_call" | custom-call | tf_op jit(solution)/shard_map/pallas_call | solution.py:40
  78.1 2.3 %collective-permute-done.19.refs_7_ = bf16[192,2048]{1,0:T(8,128)(2,1)S(1)} collective-permute-done((bf16[192,2048]{1,0:T(8,128)(2,1)S(1)}, bf16[192,2048]{1,0:T(8,128)(2,1)S(1)}, u32[]{:S(2)}, u32[]{:S(2)}) %collective-permute-start.19) | collective-permute-done | bytes 786464 | tf_op jit(solution)/shard_map/ppermute | solution.py:286
  80.4 1.9 %shard_map.93 = (bf16[128,2048]{1,0:T(8,128)(2,1)}, f32[2,128]{1,0:T(2,128)}, f32[8,128]{1,0:T(8,128)}) custom-call(s32[2,128]{1,0:T(2,128)S(1)} %bitcast.15, f32[2,128]{1,0:T(2,128)S(1)} %bitcast.17, bf16[128,2048]{1,0:T(8,128)(2,1)S(1)} %copy-done.4, bf16[48,2048]{1,0:T(8,128)(2,1)S(1)} %get-tuple-element.47.refs_3_, ...), custom_call_target="tpu_custom_call" | custom-call | tf_op jit(solution)/shard_map/pallas_call | solution.py:40
  (36 shorter events, 2.6 us)
Async XLA Ops:
  0.6 35.4 %collective-permute-start.9 = (bf16[8,48,768]{2,1,0:T(8,128)(2,1)}, bf16[8,48,768]{2,1,0:T(8,128)(2,1)S(1)}, u32[]{:S(2)}, u32[]{:S(2)}) collective-permute-start(bf16[8,48,768]{2,1,0:T(8,128)(2,1)} %bitcast.10), channel_id=1, source_target_pairs={{0,8},{8,0},{16,24},{24,16},{1,9},{9,1},{17,25},{25,17},{2,10},{10... | collective-permute-start | bytes 1769480 | tf_op jit(solution)/shard_map/ppermute | solution.py:286
  6.2 9.6 %collective-permute-start.2 = (bf16[48,2048]{1,0:T(8,128)(2,1)}, bf16[48,2048]{1,0:T(8,128)(2,1)S(1)}, u32[]{:S(2)}, u32[]{:S(2)}) collective-permute-start(bf16[48,2048]{1,0:T(8,128)(2,1)} %get-tuple-element.51), channel_id=1, source_target_pairs={{0,1},{1,0},{2,3},{3,2},{4,5},{5,4},{6,7},{7,6},{8,9},{9,8},{10,11... | collective-permute-start | bytes 589832 | tf_op jit(solution)/shard_map/ppermute | solution.py:286
  6.3 15.9 %collective-permute-start.3 = (bf16[48,2048]{1,0:T(8,128)(2,1)}, bf16[48,2048]{1,0:T(8,128)(2,1)S(1)}, u32[]{:S(2)}, u32[]{:S(2)}) collective-permute-start(bf16[48,2048]{1,0:T(8,128)(2,1)} %get-tuple-element.52), channel_id=1, source_target_pairs={{0,2},{1,3},{2,0},{3,1},{4,6},{5,7},{6,4},{7,5},{8,10},{9,11},{10,... | collective-permute-start | bytes 589832 | tf_op jit(solution)/shard_map/ppermute | solution.py:286
  7.9 17.6 %collective-permute-start.4 = (bf16[48,2048]{1,0:T(8,128)(2,1)}, bf16[48,2048]{1,0:T(8,128)(2,1)S(1)}, u32[]{:S(2)}, u32[]{:S(2)}) collective-permute-start(bf16[48,2048]{1,0:T(8,128)(2,1)} %get-tuple-element.53), channel_id=1, source_target_pairs={{0,3},{1,2},{2,1},{3,0},{4,7},{5,6},{6,5},{7,4},{8,11},{9,10},{10,... | collective-permute-start | bytes 589832 | tf_op jit(solution)/shard_map/ppermute | solution.py:286
  8.1 28.4 %collective-permute-start.1 = (bf16[128,2176]{1,0:T(8,128)(2,1)}, bf16[128,2176]{1,0:T(8,128)(2,1)S(1)}, u32[]{:S(2)}, u32[]{:S(2)}) collective-permute-start(bf16[128,2176]{1,0:T(8,128)(2,1)} %get-tuple-element.49), channel_id=1, source_target_pairs={{0,4},{1,5},{2,6},{3,7},{4,0},{5,1},{6,2},{7,3},{8,12},{9,13},{10,... | collective-permute-start | bytes 1671176 | tf_op jit(solution)/shard_map/ppermute | solution.py:286
  10.7 1.9 %copy-start = (bf16[1,768,2048]{2,1,0:T(8,128)(2,1)S(1)}, bf16[1,768,2048]{2,1,0:T(8,128)(2,1)}, u32[]{:S(2)}) copy-start(bf16[1,768,2048]{2,1,0:T(8,128)(2,1)} %param.8) | copy-start | bytes 9437188
  12.6 1.1 %copy-start.2 = (bf16[1,1,8,48,768]{4,3,2,1,0:T(8,128)(2,1)S(1)}, bf16[1,1,8,48,768]{4,3,2,1,0:T(8,128)(2,1)}, u32[]{:S(2)}) copy-start(bf16[1,1,8,48,768]{4,3,2,1,0:T(8,128)(2,1)} %param.7) | copy-start | bytes 1769476
  13.7 0.7 copy-start.8
  14.3 11.1 %copy-start.1 = (bf16[1,768,2048]{2,1,0:T(8,128)(2,1)S(1)}, bf16[1,768,2048]{2,1,0:T(8,128)(2,1)}, u32[]{:S(2)}) copy-start(bf16[1,768,2048]{2,1,0:T(8,128)(2,1)} %param.8) | copy-start | bytes 9437188
  14.3 11.1 %copy-start.5 = (bf16[48,2048]{1,0:T(8,128)(2,1)S(1)}, bf16[48,2048]{1,0:T(8,128)(2,1)}, u32[]{:S(2)}) copy-start(bf16[48,2048]{1,0:T(8,128)(2,1)} %get-tuple-element.50.refs_1_) | copy-start | bytes 589828
  15.8 24.7 %collective-permute-start = (bf16[96,2048]{1,0:T(8,128)(2,1)S(1)}, bf16[96,2048]{1,0:T(8,128)(2,1)S(1)}, u32[]{:S(2)}, u32[]{:S(2)}) collective-permute-start(bf16[96,2048]{1,0:T(8,128)(2,1)S(1)} %get-tuple-element.48), channel_id=1, source_target_pairs={{0,2},{1,3},{2,0},{3,1},{4,6},{5,7},{6,4},{7,5},{8,10},{9,11},{10,... | collective-permute-start | bytes 1179656 | tf_op jit(solution)/shard_map/ppermute | solution.py:286
  25.5 9.0 %copy-start.3 = (bf16[1,1,8,48,768]{4,3,2,1,0:T(8,128)(2,1)S(1)}, bf16[1,1,8,48,768]{4,3,2,1,0:T(8,128)(2,1)}, u32[]{:S(2)}) copy-start(bf16[1,1,8,48,768]{4,3,2,1,0:T(8,128)(2,1)} %param.7) | copy-start | bytes 1769476
  26.7 7.8 %collective-permute-start.5 = (bf16[192,512]{1,0:T(8,128)(2,1)S(1)}, bf16[192,512]{1,0:T(8,128)(2,1)S(1)}, u32[]{:S(2)}, u32[]{:S(2)}) collective-permute-start(bf16[192,512]{1,0:T(8,128)(2,1)S(1)} %get-tuple-element.55), channel_id=1, source_target_pairs={{0,8},{8,0},{16,24},{24,16},{1,9},{9,1},{17,25},{25,17},{2,10},{10... | collective-permute-start | bytes 589832 | tf_op jit(solution)/shard_map/ppermute | solution.py:286
  27.4 9.2 %collective-permute-start.6 = (bf16[192,512]{1,0:T(8,128)(2,1)S(1)}, bf16[192,512]{1,0:T(8,128)(2,1)S(1)}, u32[]{:S(2)}, u32[]{:S(2)}) collective-permute-start(bf16[192,512]{1,0:T(8,128)(2,1)S(1)} %get-tuple-element.56), channel_id=1, source_target_pairs={{0,16},{8,24},{16,0},{24,8},{1,17},{9,25},{17,1},{25,9},{2,18},{10... | collective-permute-start | bytes 589832 | tf_op jit(solution)/shard_map/ppermute | solution.py:286
  34.5 30.3 %collective-permute-start.10 = (bf16[8,48,768]{2,1,0:T(8,128)(2,1)S(1)}, bf16[8,48,768]{2,1,0:T(8,128)(2,1)S(1)}, u32[]{:S(2)}, u32[]{:S(2)}) collective-permute-start(bf16[8,48,768]{2,1,0:T(8,128)(2,1)S(1)} %bitcast.12), channel_id=1, source_target_pairs={{0,16},{8,24},{16,0},{24,8},{1,17},{9,25},{17,1},{25,9},{2,18},{10... | collective-permute-start | bytes 1769480 | tf_op jit(solution)/shard_map/ppermute | solution.py:286
  36.0 29.2 %collective-permute-start.11 = (bf16[8,48,768]{2,1,0:T(8,128)(2,1)S(1)}, bf16[8,48,768]{2,1,0:T(8,128)(2,1)S(1)}, u32[]{:S(2)}, u32[]{:S(2)}) collective-permute-start(bf16[8,48,768]{2,1,0:T(8,128)(2,1)S(1)} %collective-permute-done.9.refs_1_), channel_id=1, source_target_pairs={{0,16},{8,24},{16,0},{24,8},{1,17},{9,25},{17,1},{25,9},{2,18},{10... | collective-permute-start | bytes 1769480 | tf_op jit(solution)/shard_map/ppermute | solution.py:286
  37.0 3.4 %collective-permute-start.12 = (bf16[48,2048]{1,0:T(8,128)(2,1)S(1)}, bf16[48,2048]{1,0:T(8,128)(2,1)S(1)}, u32[]{:S(2)}, u32[]{:S(2)}) collective-permute-start(bf16[48,2048]{1,0:T(8,128)(2,1)S(1)} %get-tuple-element.65), channel_id=1, source_target_pairs={{0,1},{1,0},{2,3},{3,2},{4,5},{5,4},{6,7},{7,6},{8,9},{9,8},{10,11... | collective-permute-start | bytes 589832 | tf_op jit(solution)/shard_map/ppermute | solution.py:286
  37.1 24.1 %collective-permute-start.8 = (bf16[96,2048]{1,0:T(8,128)(2,1)S(1)}, bf16[96,2048]{1,0:T(8,128)(2,1)S(1)}, u32[]{:S(2)}, u32[]{:S(2)}) collective-permute-start(bf16[96,2048]{1,0:T(8,128)(2,1)S(1)} %get-tuple-element.61), channel_id=1, source_target_pairs={{0,6},{1,7},{2,4},{3,5},{4,2},{5,3},{6,0},{7,1},{8,14},{9,15},{10,... | collective-permute-start | bytes 1179656 | tf_op jit(solution)/shard_map/ppermute | solution.py:286
  40.4 14.4 %collective-permute-start.13 = (bf16[48,2048]{1,0:T(8,128)(2,1)S(1)}, bf16[48,2048]{1,0:T(8,128)(2,1)S(1)}, u32[]{:S(2)}, u32[]{:S(2)}) collective-permute-start(bf16[48,2048]{1,0:T(8,128)(2,1)S(1)} %get-tuple-element.66), channel_id=1, source_target_pairs={{0,2},{1,3},{2,0},{3,1},{4,6},{5,7},{6,4},{7,5},{8,10},{9,11},{10,... | collective-permute-start | bytes 589832 | tf_op jit(solution)/shard_map/ppermute | solution.py:286
  40.4 19.2 %collective-permute-start.14 = (bf16[48,2048]{1,0:T(8,128)(2,1)S(1)}, bf16[48,2048]{1,0:T(8,128)(2,1)S(1)}, u32[]{:S(2)}, u32[]{:S(2)}) collective-permute-start(bf16[48,2048]{1,0:T(8,128)(2,1)S(1)} %get-tuple-element.67), channel_id=1, source_target_pairs={{0,3},{1,2},{2,1},{3,0},{4,7},{5,6},{6,5},{7,4},{8,11},{9,10},{10,... | collective-permute-start | bytes 589832 | tf_op jit(solution)/shard_map/ppermute | solution.py:286
  54.8 20.3 %collective-permute-start.7 = (bf16[96,2048]{1,0:T(8,128)(2,1)S(1)}, bf16[96,2048]{1,0:T(8,128)(2,1)S(1)}, u32[]{:S(2)}, u32[]{:S(2)}) collective-permute-start(bf16[96,2048]{1,0:T(8,128)(2,1)S(1)} %get-tuple-element.60), channel_id=1, source_target_pairs={{0,4},{1,5},{2,6},{3,7},{4,0},{5,1},{6,2},{7,3},{8,12},{9,13},{10,... | collective-permute-start | bytes 1179656 | tf_op jit(solution)/shard_map/ppermute | solution.py:286
  59.6 8.6 %collective-permute-start.18 = (bf16[192,512]{1,0:T(8,128)(2,1)S(1)}, bf16[192,512]{1,0:T(8,128)(2,1)S(1)}, u32[]{:S(2)}, u32[]{:S(2)}) collective-permute-start(bf16[192,512]{1,0:T(8,128)(2,1)S(1)} %get-tuple-element.77), channel_id=1, source_target_pairs={{0,24},{8,16},{16,8},{24,0},{1,25},{9,17},{17,9},{25,1},{2,26},{10... | collective-permute-start | bytes 589832 | tf_op jit(solution)/shard_map/ppermute | solution.py:286
  63.2 11.9 %collective-permute-start.15 = (bf16[192,512]{1,0:T(8,128)(2,1)S(1)}, bf16[192,512]{1,0:T(8,128)(2,1)S(1)}, u32[]{:S(2)}, u32[]{:S(2)}) collective-permute-start(bf16[192,512]{1,0:T(8,128)(2,1)S(1)} %get-tuple-element.72), channel_id=1, source_target_pairs={{0,8},{8,0},{16,24},{24,16},{1,9},{9,1},{17,25},{25,17},{2,10},{10... | collective-permute-start | bytes 589832 | tf_op jit(solution)/shard_map/ppermute | solution.py:286
  64.7 10.4 %collective-permute-start.16 = (bf16[192,512]{1,0:T(8,128)(2,1)S(1)}, bf16[192,512]{1,0:T(8,128)(2,1)S(1)}, u32[]{:S(2)}, u32[]{:S(2)}) collective-permute-start(bf16[192,512]{1,0:T(8,128)(2,1)S(1)} %get-tuple-element.73), channel_id=1, source_target_pairs={{0,16},{8,24},{16,0},{24,8},{1,17},{9,25},{17,1},{25,9},{2,18},{10... | collective-permute-start | bytes 589832 | tf_op jit(solution)/shard_map/ppermute | solution.py:286
  65.2 10.8 %collective-permute-start.17 = (bf16[192,512]{1,0:T(8,128)(2,1)S(1)}, bf16[192,512]{1,0:T(8,128)(2,1)S(1)}, u32[]{:S(2)}, u32[]{:S(2)}) collective-permute-start(bf16[192,512]{1,0:T(8,128)(2,1)S(1)} %get-tuple-element.74), channel_id=1, source_target_pairs={{0,24},{8,16},{16,8},{24,0},{1,25},{9,17},{17,9},{25,1},{2,26},{10... | collective-permute-start | bytes 589832 | tf_op jit(solution)/shard_map/ppermute | solution.py:286
  76.0 4.3 %copy-start.6 = (s32[128,2]{0,1:T(2,128)S(1)}, s32[128,2]{0,1:T(2,128)}, u32[]{:S(2)}) copy-start(s32[128,2]{0,1:T(2,128)} %param.5) | copy-start | bytes 3076
  76.1 4.3 %copy-start.7 = (f32[128,2]{0,1:T(2,128)S(1)}, f32[128,2]{0,1:T(2,128)}, u32[]{:S(2)}) copy-start(f32[128,2]{0,1:T(2,128)} %param.6) | copy-start | bytes 3076
  78.0 2.4 %copy-start.4 = (bf16[128,2048]{1,0:T(8,128)(2,1)S(1)}, bf16[128,2048]{1,0:T(8,128)(2,1)}, u32[]{:S(2)}) copy-start(bf16[128,2048]{1,0:T(8,128)(2,1)} %refs_2_.3) | copy-start | bytes 1572868
  78.0 2.4 %collective-permute-start.19 = (bf16[192,2048]{1,0:T(8,128)(2,1)S(1)}, bf16[192,2048]{1,0:T(8,128)(2,1)S(1)}, u32[]{:S(2)}, u32[]{:S(2)}) collective-permute-start(bf16[192,2048]{1,0:T(8,128)(2,1)S(1)} %get-tuple-element.82), channel_id=1, source_target_pairs={{0,1},{1,0},{2,3},{3,2},{4,5},{5,4},{6,7},{7,6},{8,9},{9,8},{10,11... | collective-permute-start | bytes 2359304 | tf_op jit(solution)/shard_map/ppermute | solution.py:286

commit v3 on v2

--- a/solution.py
+++ b/solution.py
@@ -105,9 +105,9 @@
     return jnp.dot((lane == slots_column - first).astype(bf16), rows, preferred_element_type=f32)
 
 
-def message_body(capacity, routing_at, gates_at, dout_at, *refs):
-    message_ref, *slot_refs = refs[:5]
-    routing_ref, gates_ref, dout_ref, sems = refs[5:]
+def start_body(capacity, routing_at, gates_at, dout_at, hidden_at, weight_at, *refs):
+    message_ref, give_refs, (near_own, near_pair, near_two, hidden_copy) = refs[0], refs[1:5], refs[5:9]
+    routing_ref, gates_ref, dout_ref, hidden_ref, weight_ref, sems = refs[9:]
     moves = [
         pltpu.make_async_copy(a, b, sems.at[i])
         for i, (a, b) in enumerate(
@@ -115,26 +115,26 @@
                 (routing_at, routing_ref),
                 (gates_at, gates_ref),
                 (dout_at, dout_ref),
+                (hidden_at, hidden_ref),
+                (weight_at, weight_ref),
             )
         )
     ]
     for move in moves:
         move.start()
-    for move in moves:
+    me = lax.axis_index("expert")
+    c = capacity
+    picks, tokens = routing_ref.shape
+    for move in moves[:3]:
         move.wait()
-    me = lax.axis_index("expert")
-    picks, tokens = routing_ref.shape
     routing = routing_ref[...]
-    slots = slot_rows(routing, LINE, capacity)
+    slots = slot_rows(routing, LINE, c)
     gates = [gates_ref[k : k + 1] for k in range(picks)]
     dout = dout_ref[...]
-    for m, ref in enumerate(slot_refs):
-        first = ((me ^ m) * capacity).astype(f32)
-        ref[...] = rows_for(first, capacity, slots, gates, dout)
     lines = []
     for k in range(picks):
         expert = routing[k : k + 1].astype(f32)
-        lines += [expert, slots[k] - expert * capacity]
+        lines += [expert, slots[k] - expert * c]
         left = gates[k]
         for _ in range(PIECES):
             piece = left.astype(bf16).astype(f32)
@@ -144,35 +144,36 @@
     width = dout.shape[1]
     message_ref[:, :width] = dout
     message_ref[:, width:] = jnp.concatenate(lines, axis=0).T.astype(bf16)
-
-
-def read_message(message_ref, picks, capacity):
+    for m, ref in enumerate(give_refs):
+        first = ((me ^ m) * c).astype(f32)
+        ref[:c] = rows_for(first, c, slots, gates, dout)
+    moves[3].wait()
+    hidden_copy[...] = hidden_ref[...]
+    rows = jnp.concatenate([hidden_ref[me ^ m] for m in (4, 5, 6, 7, 0, 1, 3, 2)], axis=0)
+    moves[4].wait()
+    out = jnp.dot(rows, weight_ref[...], preferred_element_type=f32).astype(bf16)
+    for m, ref in enumerate(give_refs):
+        ref[c:] = out[m * c : (m + 1) * c]
+    near_own[...] = out[4 * c : 5 * c]
+    near_pair[...] = out[5 * c : 7 * c]
+    near_two[...] = out[7 * c :]
+
+
+def message_lines(message_ref, picks):
     width = message_ref.shape[1] - LANES
     lines = message_ref[:, width:].astype(f32).T
-    slots, gates = [], []
+    experts, ranks, gates = [], [], []
     for k in range(picks):
         at = k * (2 + PIECES)
-        slots.append(lines[at : at + 1] * capacity + lines[at + 1 : at + 2])
+        experts.append(lines[at : at + 1])
+        ranks.append(lines[at + 1 : at + 2])
         gates.append(jnp.sum(lines[at + 2 : at + 2 + PIECES], axis=0, keepdims=True))
-    return slots, gates, message_ref[:, :width]
-
-
-def rows_body(capacity, hidden_ref, weight_ref, *out_refs):
-    me = lax.axis_index("expert")
-    rows = jnp.concatenate([hidden_ref[me ^ m] for m in range(LINE)], axis=0)
-    out = jnp.dot(rows, weight_ref[...], preferred_element_type=f32).astype(bf16)
-    at = 0
-    for ref in out_refs:
-        ref[...] = out[at : at + ref.shape[0]]
-        at += ref.shape[0]
-
-
-def swap_body(*refs):
-    own_ref, *arrived_refs, out_ref = refs
-    count = own_ref.shape[0]
-    out_ref[:count] = own_ref[...]
-    for at, ref in enumerate(arrived_refs, 1):
-        out_ref[at * count : (at + 1) * count] = ref[count:]
+    return experts, ranks, gates, message_ref[:, :width]
+
+
+def read_message(message_ref, picks, capacity):
+    experts, ranks, gates, dout = message_lines(message_ref, picks)
+    return [e * capacity + r for e, r in zip(experts, ranks)], gates, dout
 
 
 def relay_body(capacity, picks, message_ref, *out_refs):
@@ -209,13 +210,8 @@
     cut_slices(rows, slice_refs)
 
 
-def gather_blocks(capacity, refs, rows):
-    if len(refs) == 4:
-        parts = [(ref, 0) for ref in refs]
-    else:
-        own, hop, pair = refs
-        parts = [(own, 0), (pair, 0), (hop, 0), (pair, capacity)]
-    for at, (ref, start) in enumerate(parts):
+def gather_blocks(capacity, refs, rows, start=0):
+    for at, ref in enumerate(refs):
         rows[at * capacity : (at + 1) * capacity] = ref[start : start + capacity]
 
 
@@ -246,28 +242,57 @@
     out_ref[...] = total
 
 
-def combine_body(capacity, routing_ref, gates_ref, dout_ref, *refs):
-    *block_refs, combined_ref, grad_gates_ref, rows = refs
+def share_body(capacity, own_ref, pair_ref, out_ref):
+    out_ref[:capacity] = own_ref[...]
+    out_ref[capacity:] = pair_ref[capacity:]
+
+
+def blend(capacity, experts, ranks, gates, dout, rows):
     me = lax.axis_index("expert")
-    picks = gates_ref.shape[0]
+    dout = dout.astype(f32)
+    total, products = 0.0, []
+    for expert, rank, gate in zip(experts, ranks, gates):
+        block = (expert.astype(jnp.int32) ^ me).astype(f32)
+        picked = pick_rows(0.0, as_column(block * capacity + rank), rows)
+        total += as_column(gate) * picked
+        products.append(jnp.sum(picked * dout, axis=1, keepdims=True))
+    return total, products
+
+
+def blend_body(capacity, picks, message_ref, *refs):
+    *block_refs, out_ref, rows = refs
+    gather_blocks(capacity, block_refs, rows, capacity)
+    experts, ranks, gates, dout = message_lines(message_ref, picks)
+    total, products = blend(capacity, experts, ranks, gates, dout, rows[...])
+    width = dout.shape[1]
+    out_ref[:, :width] = total.astype(bf16)
+    lane = lax.broadcasted_iota(jnp.int32, (total.shape[0], LANES), 1)
+    beside = jnp.zeros(lane.shape, f32)
+    at = 0
+    for left in products:
+        for _ in range(PIECES):
+            piece = left.astype(bf16).astype(f32)
+            beside = jnp.where(lane == at, piece, beside)
+            left = left - piece
+            at += 1
+    out_ref[:, width:] = beside.astype(bf16)
+
+
+def combine_body(capacity, message_ref, own_ref, pair_ref, hop_ref, far_ref, *refs):
+    combined_ref, grad_gates_ref, rows = refs
     c = capacity
-    slots = slot_rows(routing_ref[...] ^ me, LINE, c)
-    if len(block_refs) == LINE:
-        parts = [(ref, 0) for ref in block_refs]
-    else:
-        own, *hops, pair = block_refs
-        parts = [(own, 0), (pair, 0)]
-        for at, ref in enumerate(hops, 1):
-            parts += [(ref, 0), (pair, at * c)]
-    for at, (ref, start) in enumerate(parts):
-        rows[at * c : (at + 1) * c] = ref[start : start + c]
-    dout = dout_ref[...].astype(f32)
-    total = 0.0
-    for k in range(picks):
-        picked = pick_rows(0.0, as_column(slots[k]), rows[...])
-        total += as_column(gates_ref[k : k + 1]) * picked
-        grad_gates_ref[k : k + 1] = as_row(jnp.sum(picked * dout, axis=1, keepdims=True))
-    combined_ref[...] = total.astype(bf16)
+    picks = grad_gates_ref.shape[0]
+    rows[:c] = own_ref[...]
+    rows[c : 2 * c] = pair_ref[:c]
+    rows[2 * c :] = hop_ref[...]
+    experts, ranks, gates, dout = message_lines(message_ref, picks)
+    total, products = blend(c, experts, ranks, gates, dout, rows[...])
+    width = dout.shape[1]
+    combined_ref[...] = (total + far_ref[:, :width].astype(f32)).astype(bf16)
+    beside = far_ref[:, width:].astype(f32)
+    for k, near in enumerate(products):
+        far = jnp.sum(beside[:, k * PIECES : (k + 1) * PIECES], axis=1, keepdims=True)
+        grad_gates_ref[k : k + 1] = as_row(near + far)
 
 
 class Plan:
@@ -323,46 +348,47 @@
     slices = bf16_like(4 * capacity, part)
     rows_scratch = [pltpu.VMEM((4 * capacity, width), bf16)]
 
-    move("peer1", "hidden", "dp", 1)
-    move("peer2", "hidden", "dp", 2)
+    move("peer1", "hidden_copy", "dp", 1)
+    move("peer2", "hidden_copy", "dp", 2)
     move("peer3", "peer1", "dp", 2)
     move("from_afar", "message", "expert", 4)
     for m in (1, 2, 3):
-        move(f"near{m}", f"slots{m}", "expert", m)
+        move(f"near{m}", f"give{m}", "expert", m)
         move(f"far{m}", f"relay{m}", "expert", m)
         move(f"near_slice{m}", f"near_cut{m}", "dp", m)
         move(f"far_slice{m}", f"far_cut{m}", "dp", m)
-    for m in (2, 4, 6):
-        move(f"got{m}", f"rows{m}", "expert", m)
-    move("last", "last_swap", "expert", 1)
+    move("pair_near", "rows_near", "expert", 1)
+    move("hop_near", "share_near", "expert", 2)
+    move("blended", "blend", "expert", 4)
 
     step(
-        functools.partial(message_body, capacity),
-        dict(message=bf16_like(tokens, width + LANES), **{f"slots{m}": block(1) for m in range(4)}),
-        ["routing", "gates", "dout"],
+        functools.partial(start_body, capacity),
+        dict(
+            message=bf16_like(tokens, width + LANES),
+            **{f"give{m}": block(2) for m in range(4)},
+            rows0=block(1),
+            rows_near=block(2),
+            rows2=block(1),
+            hidden_copy=bf16_like(LINE, capacity, units),
+        ),
+        ["routing", "gates", "dout", "hidden", "weight"],
         scratch=[
             pltpu.VMEM((picks, tokens), jnp.int32),
             pltpu.VMEM((picks, tokens), f32),
             pltpu.VMEM((tokens, width), bf16),
-            pltpu.SemaphoreType.DMA((3,)),
+            pltpu.VMEM((LINE, capacity, units), bf16),
+            pltpu.VMEM((units, width), bf16),
+            pltpu.SemaphoreType.DMA((5,)),
         ],
-        pinned=(0, 1, 2),
+        pinned=(0, 1, 2, 3, 4),
         vmem=VMEM_ALL,
     )
-
-    def rows(**o):
-        step(
-            functools.partial(rows_body, capacity),
-            dict(rows0=block(1), rows1=block(1), rows2=block(2), rows4=block(2), rows6=block(2)),
-            ["hidden", "weight"],
-            **o,
-        )
 
     def near(**o):
         step(
             functools.partial(near_body, capacity),
             dict(near_grad=bf16_like(4, capacity, units), **{f"near_cut{d}": slices for d in range(SQUARE)}),
-            ["weight", "slots0", "near1", "near2", "near3"],
+            ["weight", "give0", "near1", "near2", "near3"],
             scratch=rows_scratch,
             **o,
         )
@@ -408,26 +434,44 @@
             **o,
         )
 
-    def last_swap(**o):
-        step(swap_body, dict(last_swap=block(4)), ["rows1", "got2", "got4", "got6"], **o)
+    def share(name, own, **o):
+        step(
+            functools.partial(share_body, capacity),
+            {f"share_{name}": block(2)},
+            [own, f"pair_{name}"],
+            **o,
+        )
+
+    def gate(*waits, held=()):
+        step(lambda *_: None, {}, [], waits=waits, held=held)
+
+    def blend(**o):
+        step(
+            functools.partial(blend_body, capacity, picks),
+            dict(blend=bf16_like(tokens, width + LANES)),
+            ["from_afar", "give0", "near1", "near2", "near3"],
+            scratch=rows_scratch,
+            **o,
+        )
 
     def combine(**o):
         step(
             functools.partial(combine_body, capacity),
             dict(combined=bf16_like(tokens, width), grad_gates=f32_like(picks, tokens)),
-            ["routing", "gates", "dout", "rows0", "got2", "got4", "got6", "last"],
-            scratch=[pltpu.VMEM((LINE * capacity, width), bf16)],
-            **o,
-        )
-
-    rows()
+            ["message", "rows0", "pair_near", "hop_near", "blended"],
+            scratch=rows_scratch,
+            **o,
+        )
+
+    gate("near1")
+    relay(waits=["peer1", "peer2"])
     near()
-    relay(waits=["near_slice1", "near_slice2"], held=["rows4", "rows6"])
-    far(waits=["got6", "got2"])
+    blend()
+    share("near", "rows2")
+    far()
     pack()
     near_weight()
-    far_weight(waits=["got4"])
-    last_swap()
+    far_weight()
     combine()
     v = plan.values
     return (v["combined"], v["grad_gates"].T, v["grad_hidden"][None, None], v["grad_down"][None])

time: 82.5 us -> 77.4 us (0.938)
  waiting for transfers between devices: 40.2 us -> 34.8 us
  local copies, waits for them, and re-layouts: 3.65 us -> 0.71 us
  Pallas kernels: 12.9 us -> 15.1 us
  starting transfers between devices: 24.7 us -> 25.9 us
    ppermute x20 -> x19, waiting for transfers between devices: 40.2 us -> 34.8 us  [value(): lax.ppermute(self.value(source), axis, [(i, i ^ m) for i in range(size)])]
    unnamed x18 -> x14, local copies, waits for them, and re-layouts: 3.65 us -> 0.71 us
    pallas_call x10 -> x11, Pallas kernels: 12.9 us -> 15.1 us  [__call__(): pl.pallas_call(kernel, out_shape=[*outs, jax.ShapeDtypeStruct((8, LANES),...]
    ppermute x20 -> x19, starting transfers between devices: 24.7 us -> 25.9 us  [value(): lax.ppermute(self.value(source), axis, [(i, i ^ m) for i in range(size)])]
  transfers between devices with their start and end apart: 20 -> 19, of which waited for: 9 -> 6; matrix products, arithmetic and copies ran while one was open for 0% -> 0% of each run, Pallas kernels for 11% -> 10%
where the time goes in v3:
time: 77.4 us; the launch traced here: 77.2 us
  waiting for transfers between devices  34.8 us (45%)
  starting transfers between devices  25.9 us (33%)
  Pallas kernels  15.1 us (20%)
    ppermute x19, waiting for transfers between devices, value(): lax.ppermute(self.value(source), axis, [(i, i ^ m) for i in range(size)])  34.8 us
    ppermute x19, starting transfers between devices, value(): lax.ppermute(self.value(source), axis, [(i, i ^ m) for i in range(size)])  25.9 us
    pallas_call x11, Pallas kernels, __call__(): pl.pallas_call(kernel, out_shape=[*outs, jax.ShapeDtypeStruct((8, LANES),...  15.1 us
  transfers between devices with their start and end apart: 19, of which 6 were waited for; matrix products, arithmetic and copies ran while one was open for 0% of the time, Pallas kernels for 10%

profile of v3, /device:TPU:0, one launch (start us, length us, event | category | flops | bytes accessed | tf_op | source)
XLA Modules:
  0.0 77.2 jit_solution(16156433530580411976)
XLA Ops:
  0.6 5.5 %shard_map.84 = (bf16[128,2176]{1,0:T(8,128)(2,1)}, bf16[96,2048]{1,0:T(8,128)(2,1)}, bf16[96,2048]{1,0:T(8,128)(2,1)}, bf16[96,2048]{1,0:T(8,128)(2,1)}, bf16[9...) custom-call(s32[2,128]{1,0:T(2,128)} %bitcast.12, ...), custom_call_target="tpu_custom_call" | custom-call | tf_op jit(solution)/shard_map/pallas_call | solution.py:40
  6.2 0.0 copy-start.2
  6.2 4.1 %collective-permute-start.1 = (bf16[128,2176]{1,0:T(8,128)(2,1)}, bf16[128,2176]{1,0:T(8,128)(2,1)S(1)}, u32[]{:S(2)}, u32[]{:S(2)}) collective-permute-start(bf16[128,2176]{1,0:T(8,128)(2,1)} %get-tuple-element.44.refs_0_), channel_id=1, source_target_pairs={{0,4},{1,5},{2,6},{3,7},{4,0},{5,1},{6,2},{7,3},{8,12},{9,13},{10,... | collective-permute-start | bytes 1671176 | tf_op jit(solution)/shard_map/ppermute | solution.py:311
  10.3 1.5 %collective-permute-start.5 = (bf16[8,48,768]{2,1,0:T(8,128)(2,1)}, bf16[8,48,768]{2,1,0:T(8,128)(2,1)S(1)}, u32[]{:S(2)}, u32[]{:S(2)}) collective-permute-start(bf16[8,48,768]{2,1,0:T(8,128)(2,1)} %get-tuple-element.52), channel_id=1, source_target_pairs={{0,8},{8,0},{16,24},{24,16},{1,9},{9,1},{17,25},{25,17},{2,10},{10... | collective-permute-start | bytes 1769480 | tf_op jit(solution)/shard_map/ppermute | solution.py:311
  11.8 1.5 %collective-permute-start.6 = (bf16[8,48,768]{2,1,0:T(8,128)(2,1)}, bf16[8,48,768]{2,1,0:T(8,128)(2,1)S(1)}, u32[]{:S(2)}, u32[]{:S(2)}) collective-permute-start(bf16[8,48,768]{2,1,0:T(8,128)(2,1)} %get-tuple-element.52), channel_id=1, source_target_pairs={{0,16},{8,24},{16,0},{24,8},{1,17},{9,25},{17,1},{25,9},{2,18},{10... | collective-permute-start | bytes 1769480 | tf_op jit(solution)/shard_map/ppermute | solution.py:311
  13.3 1.6 %collective-permute-start.3 = (bf16[96,2048]{1,0:T(8,128)(2,1)}, bf16[96,2048]{1,0:T(8,128)(2,1)S(1)}, u32[]{:S(2)}, u32[]{:S(2)}) collective-permute-start(bf16[96,2048]{1,0:T(8,128)(2,1)} %get-tuple-element.50), channel_id=1, source_target_pairs={{0,2},{1,3},{2,0},{3,1},{4,6},{5,7},{6,4},{7,5},{8,10},{9,11},{10,... | collective-permute-start | bytes 1179656 | tf_op jit(solution)/shard_map/ppermute | solution.py:311
  14.9 20.3 %collective-permute-done.1.refs_0_ = bf16[128,2176]{1,0:T(8,128)(2,1)S(1)} collective-permute-done((bf16[128,2176]{1,0:T(8,128)(2,1)}, bf16[128,2176]{1,0:T(8,128)(2,1)S(1)}, u32[]{:S(2)}, u32[]{:S(2)}) %collective-permute-start.1) | collective-permute-done | bytes 557088 | tf_op jit(solution)/shard_map/ppermute | solution.py:311
  35.2 1.6 %collective-permute-start.9 = (bf16[8,48,768]{2,1,0:T(8,128)(2,1)S(1)}, bf16[8,48,768]{2,1,0:T(8,128)(2,1)S(1)}, u32[]{:S(2)}, u32[]{:S(2)}) collective-permute-start(bf16[8,48,768]{2,1,0:T(8,128)(2,1)S(1)} %collective-permute-done.5.refs_1_), channel_id=1, source_target_pairs={{0,16},{8,24},{16,0},{24,8},{1,17},{9,25},{17,1},{25,9},{2,18},{10... | collective-permute-start | bytes 1769480 | tf_op jit(solution)/shard_map/ppermute | solution.py:311
  36.7 0.7 copy-done.6
  37.4 0.5 shard_map.86
  37.9 0.3 collective-permute-start.10
  38.2 0.7 collective-permute-start.11
  38.9 3.7 %collective-permute-done.4.refs_4_ = bf16[96,2048]{1,0:T(8,128)(2,1)S(1)} collective-permute-done((bf16[96,2048]{1,0:T(8,128)(2,1)}, bf16[96,2048]{1,0:T(8,128)(2,1)S(1)}, u32[]{:S(2)}, u32[]{:S(2)}) %collective-permute-start.4) | collective-permute-done | bytes 393248 | tf_op jit(solution)/shard_map/ppermute | solution.py:311
  42.7 1.2 %shard_map.87 = (bf16[4,48,768]{2,1,0:T(8,128)(2,1)S(1)}, bf16[192,512]{1,0:T(8,128)(2,1)S(1)}, bf16[192,512]{1,0:T(8,128)(2,1)S(1)}, bf16[192,512]{1,0:T(8,128)...) custom-call(bf16[768,2048]{1,0:T(8,128)(2,1)S(1)} %bitcast.8, bf16[96,2048]{1,0:T(8,128)(2,1)S(1)} %copy-done.2, ...), custom_call_target="tpu_custom_call" | custom-call | tf_op jit(solution)/shard_map/pallas_call | solution.py:40
  43.9 0.7 collective-permute-start.16
  44.6 0.8 shard_map.88
  45.4 4.2 %collective-permute-start.8 = (bf16[128,2176]{1,0:T(8,128)(2,1)S(1)}, bf16[128,2176]{1,0:T(8,128)(2,1)S(1)}, u32[]{:S(2)}, u32[]{:S(2)}) collective-permute-start(bf16[128,2176]{1,0:T(8,128)(2,1)S(1)} %get-tuple-element.58), channel_id=1, source_target_pairs={{0,4},{1,5},{2,6},{3,7},{4,0},{5,1},{6,2},{7,3},{8,12},{9,13},{10,... | collective-permute-start | bytes 1671176 | tf_op jit(solution)/shard_map/ppermute | solution.py:311
  49.6 0.6 collective-permute-start.17
  50.2 1.5 %collective-permute-done.12.refs_5_ = bf16[48,2048]{1,0:T(8,128)(2,1)S(1)} collective-permute-done((bf16[48,2048]{1,0:T(8,128)(2,1)S(1)}, bf16[48,2048]{1,0:T(8,128)(2,1)S(1)}, u32[]{:S(2)}, u32[]{:S(2)}) %collective-permute-start.12) | collective-permute-done | bytes 196640 | tf_op jit(solution)/shard_map/ppermute | solution.py:311
  51.7 1.4 %collective-permute-start.18 = (bf16[192,512]{1,0:T(8,128)(2,1)S(1)}, bf16[192,512]{1,0:T(8,128)(2,1)S(1)}, u32[]{:S(2)}, u32[]{:S(2)}) collective-permute-start(bf16[192,512]{1,0:T(8,128)(2,1)S(1)} %get-tuple-element.75), channel_id=1, source_target_pairs={{0,24},{8,16},{16,8},{24,0},{1,25},{9,17},{17,9},{25,1},{2,26},{10... | collective-permute-start | bytes 589832 | tf_op jit(solution)/shard_map/ppermute | solution.py:311
  53.1 0.3 collective-permute-start.7
  53.5 2.1 %shard_map.90 = (bf16[8,48,768]{2,1,0:T(8,128)(2,1)}, bf16[192,512]{1,0:T(8,128)(2,1)S(1)}, bf16[192,512]{1,0:T(8,128)(2,1)S(1)}, bf16[192,512]{1,0:T(8,128)(2,1...) custom-call(bf16[768,2048]{1,0:T(8,128)(2,1)S(1)} %bitcast.9, ...), custom_call_target="tpu_custom_call" | custom-call | tf_op jit(solution)/shard_map/pallas_call | solution.py:40
  55.5 6.0 %collective-permute-start.13 = (bf16[192,512]{1,0:T(8,128)(2,1)S(1)}, bf16[192,512]{1,0:T(8,128)(2,1)S(1)}, u32[]{:S(2)}, u32[]{:S(2)}) collective-permute-start(bf16[192,512]{1,0:T(8,128)(2,1)S(1)} %get-tuple-element.68), channel_id=1, source_target_pairs={{0,8},{8,0},{16,24},{24,16},{1,9},{9,1},{17,25},{25,17},{2,10},{10... | collective-permute-start | bytes 589832 | tf_op jit(solution)/shard_map/ppermute | solution.py:311
  61.5 0.9 %collective-permute-start.14 = (bf16[192,512]{1,0:T(8,128)(2,1)S(1)}, bf16[192,512]{1,0:T(8,128)(2,1)S(1)}, u32[]{:S(2)}, u32[]{:S(2)}) collective-permute-start(bf16[192,512]{1,0:T(8,128)(2,1)S(1)} %get-tuple-element.69), channel_id=1, source_target_pairs={{0,16},{8,24},{16,0},{24,8},{1,17},{9,25},{17,1},{25,9},{2,18},{10... | collective-permute-start | bytes 589832 | tf_op jit(solution)/shard_map/ppermute | solution.py:311
  62.4 0.5 collective-permute-start.15
  63.0 0.7 shard_map.91
  63.6 0.8 shard_map.92
  64.4 2.1 %collective-permute-done.13.refs_2_ = bf16[192,512]{1,0:T(8,128)(2,1)S(1)} collective-permute-done((bf16[192,512]{1,0:T(8,128)(2,1)S(1)}, bf16[192,512]{1,0:T(8,128)(2,1)S(1)}, u32[]{:S(2)}, u32[]{:S(2)}) %collective-permute-start.13) | collective-permute-done | bytes 196640 | tf_op jit(solution)/shard_map/ppermute | solution.py:311
  66.5 5.0 %collective-permute-done.14.refs_3_ = bf16[192,512]{1,0:T(8,128)(2,1)S(1)} collective-permute-done((bf16[192,512]{1,0:T(8,128)(2,1)S(1)}, bf16[192,512]{1,0:T(8,128)(2,1)S(1)}, u32[]{:S(2)}, u32[]{:S(2)}) %collective-permute-start.14) | collective-permute-done | bytes 196640 | tf_op jit(solution)/shard_map/ppermute | solution.py:311
  71.5 1.9 %shard_map.93 = (f32[768,512]{1,0:T(8,128)}, f32[8,128]{1,0:T(8,128)S(1)}) custom-call(bf16[768,768]{1,0:T(8,128)(2,1)S(1)} %get-tuple-element.66.refs_0_, bf16[192,512]{1,0:T(8,128)(2,1)S(1)} %get-tuple-element.67.refs_1_, bf16[192,512]{1,0:T(8,128)(2,1)S(1)} %collective-permute-done.13.refs_2_, bf16[192,512]{1,0:T(8,128)(2,1)S(1)} %collective-permute-done.14.refs_3_, ...), custom_call_target="tpu_custom_call" | custom-call | tf_op jit(solution)/shard_map/pallas_call | solution.py:40
  73.4 2.2 %collective-permute-done.7.refs_3_ = bf16[96,2048]{1,0:T(8,128)(2,1)S(1)} collective-permute-done((bf16[96,2048]{1,0:T(8,128)(2,1)S(1)}, bf16[96,2048]{1,0:T(8,128)(2,1)S(1)}, u32[]{:S(2)}, u32[]{:S(2)}) %collective-permute-start.7) | collective-permute-done | bytes 393248 | tf_op jit(solution)/shard_map/ppermute | solution.py:311
  75.6 1.7 %shard_map.94 = (bf16[128,2048]{1,0:T(8,128)(2,1)}, f32[2,128]{1,0:T(2,128)}, f32[8,128]{1,0:T(8,128)}) custom-call(bf16[128,2176]{1,0:T(8,128)(2,1)S(1)} %copy-done.3, bf16[48,2048]{1,0:T(8,128)(2,1)S(1)} %copy-done.4, bf16[96,2048]{1,0:T(8,128)(2,1)S(1)} %collective-permute-done.refs_1_.refs_2_, bf16[96,2048]{1,0:T(8,128)(2,1)S(1)} %collective-permute-done.7.refs_3_, ...), custom_call_target="tpu_custom_call" | custom-call | tf_op jit(solution)/shard_map/pallas_call | solution.py:40
  (31 shorter events, 0.1 us)
Async XLA Ops:
  0.6 42.0 %copy-start = (bf16[1,768,2048]{2,1,0:T(8,128)(2,1)S(1)}, bf16[1,768,2048]{2,1,0:T(8,128)(2,1)}, u32[]{:S(2)}) copy-start(bf16[1,768,2048]{2,1,0:T(8,128)(2,1)} %param.8) | copy-start | bytes 9437188
  6.2 36.5 %copy-start.2 = (bf16[96,2048]{1,0:T(8,128)(2,1)S(1)}, bf16[96,2048]{1,0:T(8,128)(2,1)}, u32[]{:S(2)}) copy-start(bf16[96,2048]{1,0:T(8,128)(2,1)} %get-tuple-element.48.refs_1_) | copy-start | bytes 1179652
  6.2 29.0 %collective-permute-start.1 = (bf16[128,2176]{1,0:T(8,128)(2,1)}, bf16[128,2176]{1,0:T(8,128)(2,1)S(1)}, u32[]{:S(2)}, u32[]{:S(2)}) collective-permute-start(bf16[128,2176]{1,0:T(8,128)(2,1)} %get-tuple-element.44.refs_0_), channel_id=1, source_target_pairs={{0,4},{1,5},{2,6},{3,7},{4,0},{5,1},{6,2},{7,3},{8,12},{9,13},{10,... | collective-permute-start | bytes 1671176 | tf_op jit(solution)/shard_map/ppermute | solution.py:311
  10.3 4.6 %collective-permute-start.2 = (bf16[96,2048]{1,0:T(8,128)(2,1)}, bf16[96,2048]{1,0:T(8,128)(2,1)S(1)}, u32[]{:S(2)}, u32[]{:S(2)}) collective-permute-start(bf16[96,2048]{1,0:T(8,128)(2,1)} %get-tuple-element.49), channel_id=1, source_target_pairs={{0,1},{1,0},{2,3},{3,2},{4,5},{5,4},{6,7},{7,6},{8,9},{9,8},{10,11... | collective-permute-start | bytes 1179656 | tf_op jit(solution)/shard_map/ppermute | solution.py:311
  10.3 24.9 %collective-permute-start.5 = (bf16[8,48,768]{2,1,0:T(8,128)(2,1)}, bf16[8,48,768]{2,1,0:T(8,128)(2,1)S(1)}, u32[]{:S(2)}, u32[]{:S(2)}) collective-permute-start(bf16[8,48,768]{2,1,0:T(8,128)(2,1)} %get-tuple-element.52), channel_id=1, source_target_pairs={{0,8},{8,0},{16,24},{24,16},{1,9},{9,1},{17,25},{25,17},{2,10},{10... | collective-permute-start | bytes 1769480 | tf_op jit(solution)/shard_map/ppermute | solution.py:311
  11.8 25.7 %collective-permute-start.6 = (bf16[8,48,768]{2,1,0:T(8,128)(2,1)}, bf16[8,48,768]{2,1,0:T(8,128)(2,1)S(1)}, u32[]{:S(2)}, u32[]{:S(2)}) collective-permute-start(bf16[8,48,768]{2,1,0:T(8,128)(2,1)} %get-tuple-element.52), channel_id=1, source_target_pairs={{0,16},{8,24},{16,0},{24,8},{1,17},{9,25},{17,1},{25,9},{2,18},{10... | collective-permute-start | bytes 1769480 | tf_op jit(solution)/shard_map/ppermute | solution.py:311
  13.3 24.9 %collective-permute-start.3 = (bf16[96,2048]{1,0:T(8,128)(2,1)}, bf16[96,2048]{1,0:T(8,128)(2,1)S(1)}, u32[]{:S(2)}, u32[]{:S(2)}) collective-permute-start(bf16[96,2048]{1,0:T(8,128)(2,1)} %get-tuple-element.50), channel_id=1, source_target_pairs={{0,2},{1,3},{2,0},{3,1},{4,6},{5,7},{6,4},{7,5},{8,10},{9,11},{10,... | collective-permute-start | bytes 1179656 | tf_op jit(solution)/shard_map/ppermute | solution.py:311
  14.9 27.8 %collective-permute-start.4 = (bf16[96,2048]{1,0:T(8,128)(2,1)}, bf16[96,2048]{1,0:T(8,128)(2,1)S(1)}, u32[]{:S(2)}, u32[]{:S(2)}) collective-permute-start(bf16[96,2048]{1,0:T(8,128)(2,1)} %get-tuple-element.51), channel_id=1, source_target_pairs={{0,3},{1,2},{2,1},{3,0},{4,7},{5,6},{6,5},{7,4},{8,11},{9,10},{10,... | collective-permute-start | bytes 1179656 | tf_op jit(solution)/shard_map/ppermute | solution.py:311
  35.2 8.8 %collective-permute-start = (bf16[96,2048]{1,0:T(8,128)(2,1)}, bf16[96,2048]{1,0:T(8,128)(2,1)S(1)}, u32[]{:S(2)}, u32[]{:S(2)}) collective-permute-start(bf16[96,2048]{1,0:T(8,128)(2,1)} %get-tuple-element.46), channel_id=1, source_target_pairs={{0,1},{1,0},{2,3},{3,2},{4,5},{5,4},{6,7},{7,6},{8,9},{9,8},{10,11... | collective-permute-start | bytes 1179656 | tf_op jit(solution)/shard_map/ppermute | solution.py:311
  35.2 27.2 %collective-permute-start.9 = (bf16[8,48,768]{2,1,0:T(8,128)(2,1)S(1)}, bf16[8,48,768]{2,1,0:T(8,128)(2,1)S(1)}, u32[]{:S(2)}, u32[]{:S(2)}) collective-permute-start(bf16[8,48,768]{2,1,0:T(8,128)(2,1)S(1)} %collective-permute-done.5.refs_1_), channel_id=1, source_target_pairs={{0,16},{8,24},{16,0},{24,8},{1,17},{9,25},{17,1},{25,9},{2,18},{10... | collective-permute-start | bytes 1769480 | tf_op jit(solution)/shard_map/ppermute | solution.py:311
  36.7 0.7 copy-start.6
  37.9 7.4 %collective-permute-start.10 = (bf16[48,2048]{1,0:T(8,128)(2,1)S(1)}, bf16[48,2048]{1,0:T(8,128)(2,1)S(1)}, u32[]{:S(2)}, u32[]{:S(2)}) collective-permute-start(bf16[48,2048]{1,0:T(8,128)(2,1)S(1)} %get-tuple-element.61), channel_id=1, source_target_pairs={{0,1},{1,0},{2,3},{3,2},{4,5},{5,4},{6,7},{7,6},{8,9},{9,8},{10,11... | collective-permute-start | bytes 589832 | tf_op jit(solution)/shard_map/ppermute | solution.py:311
  38.2 11.4 %collective-permute-start.11 = (bf16[48,2048]{1,0:T(8,128)(2,1)S(1)}, bf16[48,2048]{1,0:T(8,128)(2,1)S(1)}, u32[]{:S(2)}, u32[]{:S(2)}) collective-permute-start(bf16[48,2048]{1,0:T(8,128)(2,1)S(1)} %get-tuple-element.62), channel_id=1, source_target_pairs={{0,2},{1,3},{2,0},{3,1},{4,6},{5,7},{6,4},{7,5},{8,10},{9,11},{10,... | collective-permute-start | bytes 589832 | tf_op jit(solution)/shard_map/ppermute | solution.py:311
  42.7 9.0 %collective-permute-start.12 = (bf16[48,2048]{1,0:T(8,128)(2,1)S(1)}, bf16[48,2048]{1,0:T(8,128)(2,1)S(1)}, u32[]{:S(2)}, u32[]{:S(2)}) collective-permute-start(bf16[48,2048]{1,0:T(8,128)(2,1)S(1)} %get-tuple-element.63), channel_id=1, source_target_pairs={{0,3},{1,2},{2,1},{3,0},{4,7},{5,6},{6,5},{7,4},{8,11},{9,10},{10,... | collective-permute-start | bytes 589832 | tf_op jit(solution)/shard_map/ppermute | solution.py:311
  43.9 9.2 %copy-start.5 = (bf16[48,2048]{1,0:T(8,128)(2,1)S(1)}, bf16[48,2048]{1,0:T(8,128)(2,1)}, u32[]{:S(2)}) copy-start(bf16[48,2048]{1,0:T(8,128)(2,1)} %get-tuple-element.47.refs_0_) | copy-start | bytes 589828
  43.9 9.2 %collective-permute-start.16 = (bf16[192,512]{1,0:T(8,128)(2,1)S(1)}, bf16[192,512]{1,0:T(8,128)(2,1)S(1)}, u32[]{:S(2)}, u32[]{:S(2)}) collective-permute-start(bf16[192,512]{1,0:T(8,128)(2,1)S(1)} %get-tuple-element.73), channel_id=1, source_target_pairs={{0,8},{8,0},{16,24},{24,16},{1,9},{9,1},{17,25},{25,17},{2,10},{10... | collective-permute-start | bytes 589832 | tf_op jit(solution)/shard_map/ppermute | solution.py:311
  45.4 30.2 %collective-permute-start.8 = (bf16[128,2176]{1,0:T(8,128)(2,1)S(1)}, bf16[128,2176]{1,0:T(8,128)(2,1)S(1)}, u32[]{:S(2)}, u32[]{:S(2)}) collective-permute-start(bf16[128,2176]{1,0:T(8,128)(2,1)S(1)} %get-tuple-element.58), channel_id=1, source_target_pairs={{0,4},{1,5},{2,6},{3,7},{4,0},{5,1},{6,2},{7,3},{8,12},{9,13},{10,... | collective-permute-start | bytes 1671176 | tf_op jit(solution)/shard_map/ppermute | solution.py:311
  49.6 5.9 %collective-permute-start.17 = (bf16[192,512]{1,0:T(8,128)(2,1)S(1)}, bf16[192,512]{1,0:T(8,128)(2,1)S(1)}, u32[]{:S(2)}, u32[]{:S(2)}) collective-permute-start(bf16[192,512]{1,0:T(8,128)(2,1)S(1)} %get-tuple-element.74), channel_id=1, source_target_pairs={{0,16},{8,24},{16,0},{24,8},{1,17},{9,25},{17,1},{25,9},{2,18},{10... | collective-permute-start | bytes 589832 | tf_op jit(solution)/shard_map/ppermute | solution.py:311
  51.7 9.8 %collective-permute-start.18 = (bf16[192,512]{1,0:T(8,128)(2,1)S(1)}, bf16[192,512]{1,0:T(8,128)(2,1)S(1)}, u32[]{:S(2)}, u32[]{:S(2)}) collective-permute-start(bf16[192,512]{1,0:T(8,128)(2,1)S(1)} %get-tuple-element.75), channel_id=1, source_target_pairs={{0,24},{8,16},{16,8},{24,0},{1,25},{9,17},{17,9},{25,1},{2,26},{10... | collective-permute-start | bytes 589832 | tf_op jit(solution)/shard_map/ppermute | solution.py:311
  53.1 22.5 %collective-permute-start.7 = (bf16[96,2048]{1,0:T(8,128)(2,1)S(1)}, bf16[96,2048]{1,0:T(8,128)(2,1)S(1)}, u32[]{:S(2)}, u32[]{:S(2)}) collective-permute-start(bf16[96,2048]{1,0:T(8,128)(2,1)S(1)} %get-tuple-element.57), channel_id=1, source_target_pairs={{0,2},{1,3},{2,0},{3,1},{4,6},{5,7},{6,4},{7,5},{8,10},{9,11},{10,... | collective-permute-start | bytes 1179656 | tf_op jit(solution)/shard_map/ppermute | solution.py:311
  53.4 9.5 %copy-start.1 = (bf16[1,1,8,48,768]{4,3,2,1,0:T(8,128)(2,1)S(1)}, bf16[1,1,8,48,768]{4,3,2,1,0:T(8,128)(2,1)}, u32[]{:S(2)}) copy-start(bf16[1,1,8,48,768]{4,3,2,1,0:T(8,128)(2,1)} %param.7) | copy-start | bytes 1769476
  55.5 10.9 %collective-permute-start.13 = (bf16[192,512]{1,0:T(8,128)(2,1)S(1)}, bf16[192,512]{1,0:T(8,128)(2,1)S(1)}, u32[]{:S(2)}, u32[]{:S(2)}) collective-permute-start(bf16[192,512]{1,0:T(8,128)(2,1)S(1)} %get-tuple-element.68), channel_id=1, source_target_pairs={{0,8},{8,0},{16,24},{24,16},{1,9},{9,1},{17,25},{25,17},{2,10},{10... | collective-permute-start | bytes 589832 | tf_op jit(solution)/shard_map/ppermute | solution.py:311
  61.5 10.0 %collective-permute-start.14 = (bf16[192,512]{1,0:T(8,128)(2,1)S(1)}, bf16[192,512]{1,0:T(8,128)(2,1)S(1)}, u32[]{:S(2)}, u32[]{:S(2)}) collective-permute-start(bf16[192,512]{1,0:T(8,128)(2,1)S(1)} %get-tuple-element.69), channel_id=1, source_target_pairs={{0,16},{8,24},{16,0},{24,8},{1,17},{9,25},{17,1},{25,9},{2,18},{10... | collective-permute-start | bytes 589832 | tf_op jit(solution)/shard_map/ppermute | solution.py:311
  62.4 9.1 %collective-permute-start.15 = (bf16[192,512]{1,0:T(8,128)(2,1)S(1)}, bf16[192,512]{1,0:T(8,128)(2,1)S(1)}, u32[]{:S(2)}, u32[]{:S(2)}) collective-permute-start(bf16[192,512]{1,0:T(8,128)(2,1)S(1)} %get-tuple-element.70), channel_id=1, source_target_pairs={{0,24},{8,16},{16,8},{24,0},{1,25},{9,17},{17,9},{25,1},{2,26},{10... | collective-permute-start | bytes 589832 | tf_op jit(solution)/shard_map/ppermute | solution.py:311
  71.5 4.1 %copy-start.3 = (bf16[128,2176]{1,0:T(8,128)(2,1)S(1)}, bf16[128,2176]{1,0:T(8,128)(2,1)}, u32[]{:S(2)}) copy-start(bf16[128,2176]{1,0:T(8,128)(2,1)} %get-tuple-element.44.refs_0_) | copy-start | bytes 1671172
  71.5 4.1 %copy-start.4 = (bf16[48,2048]{1,0:T(8,128)(2,1)S(1)}, bf16[48,2048]{1,0:T(8,128)(2,1)}, u32[]{:S(2)}) copy-start(bf16[48,2048]{1,0:T(8,128)(2,1)} %get-tuple-element.45.refs_1_) | copy-start | bytes 589828

commit v4 on v3

--- a/solution.py
+++ b/solution.py
@@ -20,7 +20,7 @@
     def __init__(self):
         self.token = None
 
-    def __call__(self, body, outs, args, scratch=(), vmem=40, aliases=None, anywhere=(), anywhere_out=(), pinned=()):
+    def __call__(self, body, outs, args, scratch=(), vmem=40, aliases=None, anywhere=(), pinned=()):
         aliases = aliases or {}
         whole = pl.BlockSpec(memory_space=pltpu.VMEM)
         free = pl.BlockSpec(memory_space=pl.ANY)
@@ -29,7 +29,7 @@
             fixed if i in pinned else free if i in aliases or i in anywhere else whole
             for i in range(len(args))
         ]
-        out_specs = [free if o in aliases.values() or o in anywhere_out else whole for o in range(len(outs))]
+        out_specs = [free if o in aliases.values() else whole for o in range(len(outs))]
         n_args, n_outs = len(args), len(outs)
         chained = () if self.token is None else (self.token,)
 
@@ -106,8 +106,8 @@
 
 
 def start_body(capacity, routing_at, gates_at, dout_at, hidden_at, weight_at, *refs):
-    message_ref, give_refs, (near_own, near_pair, near_two, hidden_copy) = refs[0], refs[1:5], refs[5:9]
-    routing_ref, gates_ref, dout_ref, hidden_ref, weight_ref, sems = refs[9:]
+    message_ref, give_refs = refs[0], refs[1:5]
+    routing_ref, gates_ref, dout_ref, hidden_ref, weight_ref, sems = refs[5:]
     moves = [
         pltpu.make_async_copy(a, b, sems.at[i])
         for i, (a, b) in enumerate(
@@ -148,15 +148,23 @@
         first = ((me ^ m) * c).astype(f32)
         ref[:c] = rows_for(first, c, slots, gates, dout)
     moves[3].wait()
-    hidden_copy[...] = hidden_ref[...]
-    rows = jnp.concatenate([hidden_ref[me ^ m] for m in (4, 5, 6, 7, 0, 1, 3, 2)], axis=0)
+    rows = jnp.concatenate([hidden_ref[me ^ m] for m in range(4, LINE)], axis=0)
     moves[4].wait()
     out = jnp.dot(rows, weight_ref[...], preferred_element_type=f32).astype(bf16)
     for m, ref in enumerate(give_refs):
         ref[c:] = out[m * c : (m + 1) * c]
-    near_own[...] = out[4 * c : 5 * c]
-    near_pair[...] = out[5 * c : 7 * c]
-    near_two[...] = out[7 * c :]
+
+
+def rest_body(hidden_ref, weight_ref, *refs):
+    *out_refs, hidden_copy = refs
+    me = lax.axis_index("expert")
+    rows = jnp.concatenate([hidden_ref[me ^ m] for m in (0, 1, 3, 2)], axis=0)
+    out = jnp.dot(rows, weight_ref[...], preferred_element_type=f32).astype(bf16)
+    at = 0
+    for ref in out_refs:
+        ref[...] = out[at : at + ref.shape[0]]
+        at += ref.shape[0]
+    hidden_copy[...] = hidden_ref[...]
 
 
 def message_lines(message_ref, picks):
@@ -366,10 +374,6 @@
         dict(
             message=bf16_like(tokens, width + LANES),
             **{f"give{m}": block(2) for m in range(4)},
-            rows0=block(1),
-            rows_near=block(2),
-            rows2=block(1),
-            hidden_copy=bf16_like(LINE, capacity, units),
         ),
         ["routing", "gates", "dout", "hidden", "weight"],
         scratch=[
@@ -384,6 +388,19 @@
         vmem=VMEM_ALL,
     )
 
+    def rest(**o):
+        step(
+            rest_body,
+            dict(
+                rows0=block(1),
+                rows_near=block(2),
+                rows2=block(1),
+                hidden_copy=bf16_like(LINE, capacity, units),
+            ),
+            ["hidden", "weight"],
+            **o,
+        )
+
     def near(**o):
         step(
             functools.partial(near_body, capacity),
@@ -463,7 +480,7 @@
             **o,
         )
 
-    gate("near1")
+    rest(waits=["near1"])
     relay(waits=["peer1", "peer2"])
     near()
     blend()

time: 77.4 us -> 76.9 us (level)
  transfers between devices with their start and end apart: 19 -> 19, of which waited for: 6 -> 6; matrix products, arithmetic and copies ran while one was open for 0% -> 0% of each run, Pallas kernels for 10% -> 11%
where the time goes in v4:
time: 76.9 us; the launch traced here: 76.7 us
  waiting for transfers between devices  34.8 us (45%)
  starting transfers between devices  25.7 us (33%)
  Pallas kernels  14.7 us (19%)
  between operations  0.78 us (1%)
    ppermute x19, waiting for transfers between devices, value(): lax.ppermute(self.value(source), axis, [(i, i ^ m) for i in range(size)])  34.8 us
    ppermute x19, starting transfers between devices, value(): lax.ppermute(self.value(source), axis, [(i, i ^ m) for i in range(size)])  25.7 us
    pallas_call x11, Pallas kernels, __call__(): pl.pallas_call(kernel, out_shape=[*outs, jax.ShapeDtypeStruct((8, LANES),...  14.7 us
  transfers between devices with their start and end apart: 19, of which 6 were waited for; matrix products, arithmetic and copies ran while one was open for 0% of the time, Pallas kernels for 11%

profile of v4, /device:TPU:0, one launch (start us, length us, event | category | flops | bytes accessed | tf_op | source)
XLA Modules:
  0.0 76.7 jit_solution(8753551403780518150)
XLA Ops:
  0.7 4.4 %shard_map.84 = (bf16[128,2176]{1,0:T(8,128)(2,1)}, bf16[96,2048]{1,0:T(8,128)(2,1)}, bf16[96,2048]{1,0:T(8,128)(2,1)}, bf16[96,2048]{1,0:T(8,128)(2,1)}, bf16[96,2048]{1,0:T(8,128)(2,1)}, /*index=5*/f32[8,128]{1,0:T(8,128)}) custom-call(s32[2,128]{1,0:T(2,128)} %bitcast.14, f32[2,128]{1,0:T(2,128)} %bitcast.15, bf16[128,2048]{1,0:T(8,128)(2,1)} %refs_2_.1, ...), custom_call_target="tpu_custom_call" | custom-call | tf_op jit(solution)/shard_map/pallas_call | solution.py:40
  5.0 0.5 collective-permute-start
  5.5 3.7 %collective-permute-start.2 = (bf16[128,2176]{1,0:T(8,128)(2,1)}, bf16[128,2176]{1,0:T(8,128)(2,1)S(1)}, u32[]{:S(2)}, u32[]{:S(2)}) collective-permute-start(bf16[128,2176]{1,0:T(8,128)(2,1)} %get-tuple-element.45.refs_0_), channel_id=1, source_target_pairs={{0,4},{1,5},{2,6},{3,7},{4,0},{5,1},{6,2},{7,3},{8,12},{9,13},{10,... | collective-permute-start | bytes 1671176 | tf_op jit(solution)/shard_map/ppermute | solution.py:319
  9.2 0.7 copy-done.4
  9.9 0.8 %shard_map.85 = (bf16[48,2048]{1,0:T(8,128)(2,1)S(1)}, bf16[96,2048]{1,0:T(8,128)(2,1)S(1)}, bf16[48,2048]{1,0:T(8,128)(2,1)S(1)}, bf16[8,48,768]{2,1,0:T(8,128)(2,1)S(1)}, f32[8,128]{1,0:T(8,128)S(1)}) custom-call(bf16[8,48,768]{2,1,0:T(8,128)(2,1)S(1)} %bitcast.12, bf16[768,2048]{1,0:T(8,128)(2,1)S(1)} %bitcast.8, ...), custom_call_target="tpu_custom_call" | custom-call | tf_op jit(solution)/shard_map/pallas_call | solution.py:40
  10.7 1.6 %collective-permute-start.5 = (bf16[8,48,768]{2,1,0:T(8,128)(2,1)S(1)}, bf16[8,48,768]{2,1,0:T(8,128)(2,1)S(1)}, u32[]{:S(2)}, u32[]{:S(2)}) collective-permute-start(bf16[8,48,768]{2,1,0:T(8,128)(2,1)S(1)} %get-tuple-element.54), channel_id=1, source_target_pairs={{0,8},{8,0},{16,24},{24,16},{1,9},{9,1},{17,25},{25,17},{2,10},{10... | collective-permute-start | bytes 1769480 | tf_op jit(solution)/shard_map/ppermute | solution.py:319
  12.3 1.5 %collective-permute-start.6 = (bf16[8,48,768]{2,1,0:T(8,128)(2,1)S(1)}, bf16[8,48,768]{2,1,0:T(8,128)(2,1)S(1)}, u32[]{:S(2)}, u32[]{:S(2)}) collective-permute-start(bf16[8,48,768]{2,1,0:T(8,128)(2,1)S(1)} %get-tuple-element.54), channel_id=1, source_target_pairs={{0,16},{8,24},{16,0},{24,8},{1,17},{9,25},{17,1},{25,9},{2,18},{10... | collective-permute-start | bytes 1769480 | tf_op jit(solution)/shard_map/ppermute | solution.py:319
  13.8 1.6 %collective-permute-start.3 = (bf16[96,2048]{1,0:T(8,128)(2,1)S(1)}, bf16[96,2048]{1,0:T(8,128)(2,1)S(1)}, u32[]{:S(2)}, u32[]{:S(2)}) collective-permute-start(bf16[96,2048]{1,0:T(8,128)(2,1)S(1)} %copy-done.6), channel_id=1, source_target_pairs={{0,2},{1,3},{2,0},{3,1},{4,6},{5,7},{6,4},{7,5},{8,10},{9,11},{10,... | collective-permute-start | bytes 1179656 | tf_op jit(solution)/shard_map/ppermute | solution.py:319
  15.4 19.3 %collective-permute-done.2.refs_0_ = bf16[128,2176]{1,0:T(8,128)(2,1)S(1)} collective-permute-done((bf16[128,2176]{1,0:T(8,128)(2,1)}, bf16[128,2176]{1,0:T(8,128)(2,1)S(1)}, u32[]{:S(2)}, u32[]{:S(2)}) %collective-permute-start.2) | collective-permute-done | bytes 557088 | tf_op jit(solution)/shard_map/ppermute | solution.py:319
  34.7 1.6 %collective-permute-start.9 = (bf16[8,48,768]{2,1,0:T(8,128)(2,1)S(1)}, bf16[8,48,768]{2,1,0:T(8,128)(2,1)S(1)}, u32[]{:S(2)}, u32[]{:S(2)}) collective-permute-start(bf16[8,48,768]{2,1,0:T(8,128)(2,1)S(1)} %collective-permute-done.5.refs_1_), channel_id=1, source_target_pairs={{0,16},{8,24},{16,0},{24,8},{1,17},{9,25},{17,1},{25,9},{2,18},{10... | collective-permute-start | bytes 1769480 | tf_op jit(solution)/shard_map/ppermute | solution.py:319
  36.3 0.5 shard_map.86
  36.8 0.3 collective-permute-start.10
  37.0 0.7 collective-permute-start.11
  37.8 4.4 %collective-permute-done.4.refs_4_ = bf16[96,2048]{1,0:T(8,128)(2,1)S(1)} collective-permute-done((bf16[96,2048]{1,0:T(8,128)(2,1)S(1)}, bf16[96,2048]{1,0:T(8,128)(2,1)S(1)}, u32[]{:S(2)}, u32[]{:S(2)}) %collective-permute-start.4) | collective-permute-done | bytes 393248 | tf_op jit(solution)/shard_map/ppermute | solution.py:319
  42.2 1.2 %shard_map.87 = (bf16[4,48,768]{2,1,0:T(8,128)(2,1)S(1)}, bf16[192,512]{1,0:T(8,128)(2,1)S(1)}, bf16[192,512]{1,0:T(8,128)(2,1)S(1)}, bf16[192,512]{1,0:T(8,128)...) custom-call(bf16[768,2048]{1,0:T(8,128)(2,1)S(1)} %bitcast.9, bf16[96,2048]{1,0:T(8,128)(2,1)S(1)} %copy-done.2, ...), custom_call_target="tpu_custom_call" | custom-call | tf_op jit(solution)/shard_map/pallas_call | solution.py:40
  43.4 0.8 %collective-permute-start.16 = (bf16[192,512]{1,0:T(8,128)(2,1)S(1)}, bf16[192,512]{1,0:T(8,128)(2,1)S(1)}, u32[]{:S(2)}, u32[]{:S(2)}) collective-permute-start(bf16[192,512]{1,0:T(8,128)(2,1)S(1)} %get-tuple-element.75), channel_id=1, source_target_pairs={{0,8},{8,0},{16,24},{24,16},{1,9},{9,1},{17,25},{25,17},{2,10},{10... | collective-permute-start | bytes 589832 | tf_op jit(solution)/shard_map/ppermute | solution.py:319
  44.3 0.8 shard_map.88
  45.0 6.9 %collective-permute-start.8 = (bf16[128,2176]{1,0:T(8,128)(2,1)S(1)}, bf16[128,2176]{1,0:T(8,128)(2,1)S(1)}, u32[]{:S(2)}, u32[]{:S(2)}) collective-permute-start(bf16[128,2176]{1,0:T(8,128)(2,1)S(1)} %get-tuple-element.60), channel_id=1, source_target_pairs={{0,4},{1,5},{2,6},{3,7},{4,0},{5,1},{6,2},{7,3},{8,12},{9,13},{10,... | collective-permute-start | bytes 1671176 | tf_op jit(solution)/shard_map/ppermute | solution.py:319
  52.0 0.5 collective-permute-start.17
  52.5 2.4 %collective-permute-start.18 = (bf16[192,512]{1,0:T(8,128)(2,1)S(1)}, bf16[192,512]{1,0:T(8,128)(2,1)S(1)}, u32[]{:S(2)}, u32[]{:S(2)}) collective-permute-start(bf16[192,512]{1,0:T(8,128)(2,1)S(1)} %get-tuple-element.77), channel_id=1, source_target_pairs={{0,24},{8,16},{16,8},{24,0},{1,25},{9,17},{17,9},{25,1},{2,26},{10... | collective-permute-start | bytes 589832 | tf_op jit(solution)/shard_map/ppermute | solution.py:319
  55.0 2.1 %shard_map.90 = (bf16[8,48,768]{2,1,0:T(8,128)(2,1)}, bf16[192,512]{1,0:T(8,128)(2,1)S(1)}, bf16[192,512]{1,0:T(8,128)(2,1)S(1)}, bf16[192,512]{1,0:T(8,128)(2,1...) custom-call(bf16[768,2048]{1,0:T(8,128)(2,1)S(1)} %bitcast.10, ...), custom_call_target="tpu_custom_call" | custom-call | tf_op jit(solution)/shard_map/pallas_call | solution.py:40
  57.1 4.7 %collective-permute-done.17.refs_3_ = bf16[192,512]{1,0:T(8,128)(2,1)S(1)} collective-permute-done((bf16[192,512]{1,0:T(8,128)(2,1)S(1)}, bf16[192,512]{1,0:T(8,128)(2,1)S(1)}, u32[]{:S(2)}, u32[]{:S(2)}) %collective-permute-start.17) | collective-permute-done | bytes 196640 | tf_op jit(solution)/shard_map/ppermute | solution.py:319
  61.8 1.8 %collective-permute-start.13 = (bf16[192,512]{1,0:T(8,128)(2,1)S(1)}, bf16[192,512]{1,0:T(8,128)(2,1)S(1)}, u32[]{:S(2)}, u32[]{:S(2)}) collective-permute-start(bf16[192,512]{1,0:T(8,128)(2,1)S(1)} %get-tuple-element.70), channel_id=1, source_target_pairs={{0,8},{8,0},{16,24},{24,16},{1,9},{9,1},{17,25},{25,17},{2,10},{10... | collective-permute-start | bytes 589832 | tf_op jit(solution)/shard_map/ppermute | solution.py:319
  63.6 0.5 collective-permute-start.14
  64.1 1.2 %collective-permute-start.15 = (bf16[192,512]{1,0:T(8,128)(2,1)S(1)}, bf16[192,512]{1,0:T(8,128)(2,1)S(1)}, u32[]{:S(2)}, u32[]{:S(2)}) collective-permute-start(bf16[192,512]{1,0:T(8,128)(2,1)S(1)} %get-tuple-element.72), channel_id=1, source_target_pairs={{0,24},{8,16},{16,8},{24,0},{1,25},{9,17},{17,9},{25,1},{2,26},{10... | collective-permute-start | bytes 589832 | tf_op jit(solution)/shard_map/ppermute | solution.py:319
  65.3 0.7 shard_map.91
  66.0 0.8 shard_map.92
  66.8 1.9 %collective-permute-done.13.refs_2_ = bf16[192,512]{1,0:T(8,128)(2,1)S(1)} collective-permute-done((bf16[192,512]{1,0:T(8,128)(2,1)S(1)}, bf16[192,512]{1,0:T(8,128)(2,1)S(1)}, u32[]{:S(2)}, u32[]{:S(2)}) %collective-permute-start.13) | collective-permute-done | bytes 196640 | tf_op jit(solution)/shard_map/ppermute | solution.py:319
  68.7 3.0 %collective-permute-done.14.refs_3_ = bf16[192,512]{1,0:T(8,128)(2,1)S(1)} collective-permute-done((bf16[192,512]{1,0:T(8,128)(2,1)S(1)}, bf16[192,512]{1,0:T(8,128)(2,1)S(1)}, u32[]{:S(2)}, u32[]{:S(2)}) %collective-permute-start.14) | collective-permute-done | bytes 196640 | tf_op jit(solution)/shard_map/ppermute | solution.py:319
  71.7 1.9 %shard_map.93 = (f32[768,512]{1,0:T(8,128)}, f32[8,128]{1,0:T(8,128)S(1)}) custom-call(bf16[768,768]{1,0:T(8,128)(2,1)S(1)} %get-tuple-element.68.refs_0_, bf16[192,512]{1,0:T(8,128)(2,1)S(1)} %get-tuple-element.69.refs_1_, bf16[192,512]{1,0:T(8,128)(2,1)S(1)} %collective-permute-done.13.refs_2_, bf16[192,512]{1,0:T(8,128)(2,1)S(1)} %collective-permute-done.14.refs_3_, ...), custom_call_target="tpu_custom_call" | custom-call | tf_op jit(solution)/shard_map/pallas_call | solution.py:40
  73.7 1.4 %collective-permute-done.8.refs_4_ = bf16[128,2176]{1,0:T(8,128)(2,1)S(1)} collective-permute-done((bf16[128,2176]{1,0:T(8,128)(2,1)S(1)}, bf16[128,2176]{1,0:T(8,128)(2,1)S(1)}, u32[]{:S(2)}, u32[]{:S(2)}) %collective-permute-start.8) | collective-permute-done | bytes 557088 | tf_op jit(solution)/shard_map/ppermute | solution.py:319
  75.0 1.7 %shard_map.94 = (bf16[128,2048]{1,0:T(8,128)(2,1)}, f32[2,128]{1,0:T(2,128)}, f32[8,128]{1,0:T(8,128)}) custom-call(bf16[128,2176]{1,0:T(8,128)(2,1)S(1)} %copy-done.3, bf16[48,2048]{1,0:T(8,128)(2,1)S(1)} %get-tuple-element.48.refs_1_, bf16[96,2048]{1,0:T(8,128)(2,1)S(1)} %collective-permute-done.1.refs_1_.refs_2_, ...), custom_call_target="tpu_custom_call" | custom-call | tf_op jit(solution)/shard_map/pallas_call | solution.py:40
  (31 shorter events, 0.2 us)
Async XLA Ops:
  0.6 8.6 %copy-start = (bf16[1,768,2048]{2,1,0:T(8,128)(2,1)S(1)}, bf16[1,768,2048]{2,1,0:T(8,128)(2,1)}, u32[]{:S(2)}) copy-start(bf16[1,768,2048]{2,1,0:T(8,128)(2,1)} %param.8) | copy-start | bytes 9437188
  0.6 8.6 %copy-start.1 = (bf16[1,1,8,48,768]{4,3,2,1,0:T(8,128)(2,1)S(1)}, bf16[1,1,8,48,768]{4,3,2,1,0:T(8,128)(2,1)}, u32[]{:S(2)}) copy-start(bf16[1,1,8,48,768]{4,3,2,1,0:T(8,128)(2,1)} %param.7) | copy-start | bytes 1769476
  5.0 4.2 %collective-permute-start = (bf16[96,2048]{1,0:T(8,128)(2,1)}, bf16[96,2048]{1,0:T(8,128)(2,1)S(1)}, u32[]{:S(2)}, u32[]{:S(2)}) collective-permute-start(bf16[96,2048]{1,0:T(8,128)(2,1)} %get-tuple-element.46), channel_id=1, source_target_pairs={{0,1},{1,0},{2,3},{3,2},{4,5},{5,4},{6,7},{7,6},{8,9},{9,8},{10,11... | collective-permute-start | bytes 1179656 | tf_op jit(solution)/shard_map/ppermute | solution.py:319
  5.5 29.1 %collective-permute-start.2 = (bf16[128,2176]{1,0:T(8,128)(2,1)}, bf16[128,2176]{1,0:T(8,128)(2,1)S(1)}, u32[]{:S(2)}, u32[]{:S(2)}) collective-permute-start(bf16[128,2176]{1,0:T(8,128)(2,1)} %get-tuple-element.45.refs_0_), channel_id=1, source_target_pairs={{0,4},{1,5},{2,6},{3,7},{4,0},{5,1},{6,2},{7,3},{8,12},{9,13},{10,... | collective-permute-start | bytes 1671176 | tf_op jit(solution)/shard_map/ppermute | solution.py:319
  9.2 0.7 copy-start.4
  9.9 3.9 %copy-start.6 = (bf16[96,2048]{1,0:T(8,128)(2,1)S(1)}, bf16[96,2048]{1,0:T(8,128)(2,1)}, u32[]{:S(2)}) copy-start(bf16[96,2048]{1,0:T(8,128)(2,1)} %get-tuple-element.52) | copy-start | bytes 1179652
  9.9 5.5 %copy-start.5 = (bf16[96,2048]{1,0:T(8,128)(2,1)S(1)}, bf16[96,2048]{1,0:T(8,128)(2,1)}, u32[]{:S(2)}) copy-start(bf16[96,2048]{1,0:T(8,128)(2,1)} %get-tuple-element.53) | copy-start | bytes 1179652
  10.7 31.5 %copy-start.2 = (bf16[96,2048]{1,0:T(8,128)(2,1)S(1)}, bf16[96,2048]{1,0:T(8,128)(2,1)}, u32[]{:S(2)}) copy-start(bf16[96,2048]{1,0:T(8,128)(2,1)} %get-tuple-element.51.refs_1_) | copy-start | bytes 1179652
  10.7 23.9 %collective-permute-start.5 = (bf16[8,48,768]{2,1,0:T(8,128)(2,1)S(1)}, bf16[8,48,768]{2,1,0:T(8,128)(2,1)S(1)}, u32[]{:S(2)}, u32[]{:S(2)}) collective-permute-start(bf16[8,48,768]{2,1,0:T(8,128)(2,1)S(1)} %get-tuple-element.54), channel_id=1, source_target_pairs={{0,8},{8,0},{16,24},{24,16},{1,9},{9,1},{17,25},{25,17},{2,10},{10... | collective-permute-start | bytes 1769480 | tf_op jit(solution)/shard_map/ppermute | solution.py:319
  12.3 24.0 %collective-permute-start.6 = (bf16[8,48,768]{2,1,0:T(8,128)(2,1)S(1)}, bf16[8,48,768]{2,1,0:T(8,128)(2,1)S(1)}, u32[]{:S(2)}, u32[]{:S(2)}) collective-permute-start(bf16[8,48,768]{2,1,0:T(8,128)(2,1)S(1)} %get-tuple-element.54), channel_id=1, source_target_pairs={{0,16},{8,24},{16,0},{24,8},{1,17},{9,25},{17,1},{25,9},{2,18},{10... | collective-permute-start | bytes 1769480 | tf_op jit(solution)/shard_map/ppermute | solution.py:319
  13.8 23.2 %collective-permute-start.3 = (bf16[96,2048]{1,0:T(8,128)(2,1)S(1)}, bf16[96,2048]{1,0:T(8,128)(2,1)S(1)}, u32[]{:S(2)}, u32[]{:S(2)}) collective-permute-start(bf16[96,2048]{1,0:T(8,128)(2,1)S(1)} %copy-done.6), channel_id=1, source_target_pairs={{0,2},{1,3},{2,0},{3,1},{4,6},{5,7},{6,4},{7,5},{8,10},{9,11},{10,... | collective-permute-start | bytes 1179656 | tf_op jit(solution)/shard_map/ppermute | solution.py:319
  15.4 26.8 %collective-permute-start.4 = (bf16[96,2048]{1,0:T(8,128)(2,1)S(1)}, bf16[96,2048]{1,0:T(8,128)(2,1)S(1)}, u32[]{:S(2)}, u32[]{:S(2)}) collective-permute-start(bf16[96,2048]{1,0:T(8,128)(2,1)S(1)} %copy-done.5), channel_id=1, source_target_pairs={{0,3},{1,2},{2,1},{3,0},{4,7},{5,6},{6,5},{7,4},{8,11},{9,10},{10,... | collective-permute-start | bytes 1179656 | tf_op jit(solution)/shard_map/ppermute | solution.py:319
  34.7 8.8 %collective-permute-start.1 = (bf16[96,2048]{1,0:T(8,128)(2,1)S(1)}, bf16[96,2048]{1,0:T(8,128)(2,1)S(1)}, u32[]{:S(2)}, u32[]{:S(2)}) collective-permute-start(bf16[96,2048]{1,0:T(8,128)(2,1)S(1)} %get-tuple-element.49), channel_id=1, source_target_pairs={{0,1},{1,0},{2,3},{3,2},{4,5},{5,4},{6,7},{7,6},{8,9},{9,8},{10,11... | collective-permute-start | bytes 1179656 | tf_op jit(solution)/shard_map/ppermute | solution.py:319
  34.7 29.5 %collective-permute-start.9 = (bf16[8,48,768]{2,1,0:T(8,128)(2,1)S(1)}, bf16[8,48,768]{2,1,0:T(8,128)(2,1)S(1)}, u32[]{:S(2)}, u32[]{:S(2)}) collective-permute-start(bf16[8,48,768]{2,1,0:T(8,128)(2,1)S(1)} %collective-permute-done.5.refs_1_), channel_id=1, source_target_pairs={{0,16},{8,24},{16,0},{24,8},{1,17},{9,25},{17,1},{25,9},{2,18},{10... | collective-permute-start | bytes 1769480 | tf_op jit(solution)/shard_map/ppermute | solution.py:319
  36.8 8.3 %collective-permute-start.10 = (bf16[48,2048]{1,0:T(8,128)(2,1)S(1)}, bf16[48,2048]{1,0:T(8,128)(2,1)S(1)}, u32[]{:S(2)}, u32[]{:S(2)}) collective-permute-start(bf16[48,2048]{1,0:T(8,128)(2,1)S(1)} %get-tuple-element.63), channel_id=1, source_target_pairs={{0,1},{1,0},{2,3},{3,2},{4,5},{5,4},{6,7},{7,6},{8,9},{9,8},{10,11... | collective-permute-start | bytes 589832 | tf_op jit(solution)/shard_map/ppermute | solution.py:319
  37.0 14.9 %collective-permute-start.11 = (bf16[48,2048]{1,0:T(8,128)(2,1)S(1)}, bf16[48,2048]{1,0:T(8,128)(2,1)S(1)}, u32[]{:S(2)}, u32[]{:S(2)}) collective-permute-start(bf16[48,2048]{1,0:T(8,128)(2,1)S(1)} %get-tuple-element.64), channel_id=1, source_target_pairs={{0,2},{1,3},{2,0},{3,1},{4,6},{5,7},{6,4},{7,5},{8,10},{9,11},{10,... | collective-permute-start | bytes 589832 | tf_op jit(solution)/shard_map/ppermute | solution.py:319
  42.2 10.3 %collective-permute-start.12 = (bf16[48,2048]{1,0:T(8,128)(2,1)S(1)}, bf16[48,2048]{1,0:T(8,128)(2,1)S(1)}, u32[]{:S(2)}, u32[]{:S(2)}) collective-permute-start(bf16[48,2048]{1,0:T(8,128)(2,1)S(1)} %get-tuple-element.65), channel_id=1, source_target_pairs={{0,3},{1,2},{2,1},{3,0},{4,7},{5,6},{6,5},{7,4},{8,11},{9,10},{10,... | collective-permute-start | bytes 589832 | tf_op jit(solution)/shard_map/ppermute | solution.py:319
  43.4 11.5 %collective-permute-start.16 = (bf16[192,512]{1,0:T(8,128)(2,1)S(1)}, bf16[192,512]{1,0:T(8,128)(2,1)S(1)}, u32[]{:S(2)}, u32[]{:S(2)}) collective-permute-start(bf16[192,512]{1,0:T(8,128)(2,1)S(1)} %get-tuple-element.75), channel_id=1, source_target_pairs={{0,8},{8,0},{16,24},{24,16},{1,9},{9,1},{17,25},{25,17},{2,10},{10... | collective-permute-start | bytes 589832 | tf_op jit(solution)/shard_map/ppermute | solution.py:319
  45.0 30.0 %collective-permute-start.8 = (bf16[128,2176]{1,0:T(8,128)(2,1)S(1)}, bf16[128,2176]{1,0:T(8,128)(2,1)S(1)}, u32[]{:S(2)}, u32[]{:S(2)}) collective-permute-start(bf16[128,2176]{1,0:T(8,128)(2,1)S(1)} %get-tuple-element.60), channel_id=1, source_target_pairs={{0,4},{1,5},{2,6},{3,7},{4,0},{5,1},{6,2},{7,3},{8,12},{9,13},{10,... | collective-permute-start | bytes 1671176 | tf_op jit(solution)/shard_map/ppermute | solution.py:319
  52.0 9.9 %collective-permute-start.17 = (bf16[192,512]{1,0:T(8,128)(2,1)S(1)}, bf16[192,512]{1,0:T(8,128)(2,1)S(1)}, u32[]{:S(2)}, u32[]{:S(2)}) collective-permute-start(bf16[192,512]{1,0:T(8,128)(2,1)S(1)} %get-tuple-element.76), channel_id=1, source_target_pairs={{0,16},{8,24},{16,0},{24,8},{1,17},{9,25},{17,1},{25,9},{2,18},{10... | collective-permute-start | bytes 589832 | tf_op jit(solution)/shard_map/ppermute | solution.py:319
  52.5 11.1 %collective-permute-start.18 = (bf16[192,512]{1,0:T(8,128)(2,1)S(1)}, bf16[192,512]{1,0:T(8,128)(2,1)S(1)}, u32[]{:S(2)}, u32[]{:S(2)}) collective-permute-start(bf16[192,512]{1,0:T(8,128)(2,1)S(1)} %get-tuple-element.77), channel_id=1, source_target_pairs={{0,24},{8,16},{16,8},{24,0},{1,25},{9,17},{17,9},{25,1},{2,26},{10... | collective-permute-start | bytes 589832 | tf_op jit(solution)/shard_map/ppermute | solution.py:319
  55.0 18.7 %collective-permute-start.7 = (bf16[96,2048]{1,0:T(8,128)(2,1)S(1)}, bf16[96,2048]{1,0:T(8,128)(2,1)S(1)}, u32[]{:S(2)}, u32[]{:S(2)}) collective-permute-start(bf16[96,2048]{1,0:T(8,128)(2,1)S(1)} %get-tuple-element.59), channel_id=1, source_target_pairs={{0,2},{1,3},{2,0},{3,1},{4,6},{5,7},{6,4},{7,5},{8,10},{9,11},{10,... | collective-permute-start | bytes 1179656 | tf_op jit(solution)/shard_map/ppermute | solution.py:319
  61.8 6.9 %collective-permute-start.13 = (bf16[192,512]{1,0:T(8,128)(2,1)S(1)}, bf16[192,512]{1,0:T(8,128)(2,1)S(1)}, u32[]{:S(2)}, u32[]{:S(2)}) collective-permute-start(bf16[192,512]{1,0:T(8,128)(2,1)S(1)} %get-tuple-element.70), channel_id=1, source_target_pairs={{0,8},{8,0},{16,24},{24,16},{1,9},{9,1},{17,25},{25,17},{2,10},{10... | collective-permute-start | bytes 589832 | tf_op jit(solution)/shard_map/ppermute | solution.py:319
  63.6 8.1 %collective-permute-start.14 = (bf16[192,512]{1,0:T(8,128)(2,1)S(1)}, bf16[192,512]{1,0:T(8,128)(2,1)S(1)}, u32[]{:S(2)}, u32[]{:S(2)}) collective-permute-start(bf16[192,512]{1,0:T(8,128)(2,1)S(1)} %get-tuple-element.71), channel_id=1, source_target_pairs={{0,16},{8,24},{16,0},{24,8},{1,17},{9,25},{17,1},{25,9},{2,18},{10... | collective-permute-start | bytes 589832 | tf_op jit(solution)/shard_map/ppermute | solution.py:319
  64.1 7.6 %collective-permute-start.15 = (bf16[192,512]{1,0:T(8,128)(2,1)S(1)}, bf16[192,512]{1,0:T(8,128)(2,1)S(1)}, u32[]{:S(2)}, u32[]{:S(2)}) collective-permute-start(bf16[192,512]{1,0:T(8,128)(2,1)S(1)} %get-tuple-element.72), channel_id=1, source_target_pairs={{0,24},{8,16},{16,8},{24,0},{1,25},{9,17},{17,9},{25,1},{2,26},{10... | collective-permute-start | bytes 589832 | tf_op jit(solution)/shard_map/ppermute | solution.py:319
  71.7 3.3 %copy-start.3 = (bf16[128,2176]{1,0:T(8,128)(2,1)S(1)}, bf16[128,2176]{1,0:T(8,128)(2,1)}, u32[]{:S(2)}) copy-start(bf16[128,2176]{1,0:T(8,128)(2,1)} %get-tuple-element.45.refs_0_) | copy-start | bytes 1671172

commit v5 on v4

--- a/solution.py
+++ b/solution.py
@@ -10,6 +10,7 @@
 LINE = 8
 SQUARE = 4
 LANES = 128
+WEIGHT_PARTS = 3
 PIECES = 3
 MIB = 1 << 20
 VMEM_ALL = 60
@@ -108,6 +109,9 @@
 def start_body(capacity, routing_at, gates_at, dout_at, hidden_at, weight_at, *refs):
     message_ref, give_refs = refs[0], refs[1:5]
     routing_ref, gates_ref, dout_ref, hidden_ref, weight_ref, sems = refs[5:]
+    units = weight_ref.shape[0]
+    deep = units // WEIGHT_PARTS
+    parts = [slice(at, at + deep) for at in range(0, units, deep)]
     moves = [
         pltpu.make_async_copy(a, b, sems.at[i])
         for i, (a, b) in enumerate(
@@ -116,7 +120,7 @@
                 (gates_at, gates_ref),
                 (dout_at, dout_ref),
                 (hidden_at, hidden_ref),
-                (weight_at, weight_ref),
+                *((weight_at.at[part], weight_ref.at[part]) for part in parts),
             )
         )
     ]
@@ -149,8 +153,12 @@
         ref[:c] = rows_for(first, c, slots, gates, dout)
     moves[3].wait()
     rows = jnp.concatenate([hidden_ref[me ^ m] for m in range(4, LINE)], axis=0)
-    moves[4].wait()
-    out = jnp.dot(rows, weight_ref[...], preferred_element_type=f32).astype(bf16)
+    total = None
+    for part, move in zip(parts, moves[4:]):
+        move.wait()
+        product = jnp.dot(rows[:, part], weight_ref[part], preferred_element_type=f32)
+        total = product if total is None else total + product
+    out = total.astype(bf16)
     for m, ref in enumerate(give_refs):
         ref[c:] = out[m * c : (m + 1) * c]
 
@@ -382,7 +390,7 @@
             pltpu.VMEM((tokens, width), bf16),
             pltpu.VMEM((LINE, capacity, units), bf16),
             pltpu.VMEM((units, width), bf16),
-            pltpu.SemaphoreType.DMA((5,)),
+            pltpu.SemaphoreType.DMA((4 + WEIGHT_PARTS,)),
         ],
         pinned=(0, 1, 2, 3, 4),
         vmem=VMEM_ALL,

time: 76.9 us -> 76.7 us (level)
  no operation moved by 1% of the time
where the time goes in v5:
time: 76.7 us; the launch traced here: 76.5 us
  waiting for transfers between devices  34.8 us (45%)
  starting transfers between devices  25.7 us (34%)
  Pallas kernels  14.5 us (19%)
  between operations  0.78 us (1%)
    ppermute x19, waiting for transfers between devices, value(): lax.ppermute(self.value(source), axis, [(i, i ^ m) for i in range(size)])  34.8 us
    ppermute x19, starting transfers between devices, value(): lax.ppermute(self.value(source), axis, [(i, i ^ m) for i in range(size)])  25.7 us
    pallas_call x11, Pallas kernels, __call__(): pl.pallas_call(kernel, out_shape=[*outs, jax.ShapeDtypeStruct((8, LANES),...  14.5 us
  transfers between devices with their start and end apart: 19, of which 6 were waited for; matrix products, arithmetic and copies ran while one was open for 0% of the time, Pallas kernels for 11%

profile of v5, /device:TPU:0, one launch (start us, length us, event | category | flops | bytes accessed | tf_op | source)
XLA Modules:
  0.0 76.5 jit_solution(14832606212901774946)
XLA Ops:
  0.7 4.2 %shard_map.84 = (bf16[128,2176]{1,0:T(8,128)(2,1)}, bf16[96,2048]{1,0:T(8,128)(2,1)}, bf16[96,2048]{1,0:T(8,128)(2,1)}, bf16[96,2048]{1,0:T(8,128)(2,1)}, bf16[96,2048]{1,0:T(8,128)(2,1)}, /*index=5*/f32[8,128]{1,0:T(8,128)}) custom-call(s32[2,128]{1,0:T(2,128)} %bitcast.14, f32[2,128]{1,0:T(2,128)} %bitcast.15, bf16[128,2048]{1,0:T(8,128)(2,1)} %refs_2_.1, ...), custom_call_target="tpu_custom_call" | custom-call | tf_op jit(solution)/shard_map/pallas_call | solution.py:41
  4.8 0.5 collective-permute-start
  5.3 3.7 %collective-permute-start.2 = (bf16[128,2176]{1,0:T(8,128)(2,1)}, bf16[128,2176]{1,0:T(8,128)(2,1)S(1)}, u32[]{:S(2)}, u32[]{:S(2)}) collective-permute-start(bf16[128,2176]{1,0:T(8,128)(2,1)} %get-tuple-element.45.refs_0_), channel_id=1, source_target_pairs={{0,4},{1,5},{2,6},{3,7},{4,0},{5,1},{6,2},{7,3},{8,12},{9,13},{10,... | collective-permute-start | bytes 1671176 | tf_op jit(solution)/shard_map/ppermute | solution.py:327
  9.0 0.7 copy-done.4
  9.7 0.8 %shard_map.85 = (bf16[48,2048]{1,0:T(8,128)(2,1)S(1)}, bf16[96,2048]{1,0:T(8,128)(2,1)S(1)}, bf16[48,2048]{1,0:T(8,128)(2,1)S(1)}, bf16[8,48,768]{2,1,0:T(8,128)(2,1)S(1)}, f32[8,128]{1,0:T(8,128)S(1)}) custom-call(bf16[8,48,768]{2,1,0:T(8,128)(2,1)S(1)} %bitcast.12, bf16[768,2048]{1,0:T(8,128)(2,1)S(1)} %bitcast.8, ...), custom_call_target="tpu_custom_call" | custom-call | tf_op jit(solution)/shard_map/pallas_call | solution.py:41
  10.6 1.6 %collective-permute-start.5 = (bf16[8,48,768]{2,1,0:T(8,128)(2,1)S(1)}, bf16[8,48,768]{2,1,0:T(8,128)(2,1)S(1)}, u32[]{:S(2)}, u32[]{:S(2)}) collective-permute-start(bf16[8,48,768]{2,1,0:T(8,128)(2,1)S(1)} %get-tuple-element.54), channel_id=1, source_target_pairs={{0,8},{8,0},{16,24},{24,16},{1,9},{9,1},{17,25},{25,17},{2,10},{10... | collective-permute-start | bytes 1769480 | tf_op jit(solution)/shard_map/ppermute | solution.py:327
  12.1 1.5 %collective-permute-start.6 = (bf16[8,48,768]{2,1,0:T(8,128)(2,1)S(1)}, bf16[8,48,768]{2,1,0:T(8,128)(2,1)S(1)}, u32[]{:S(2)}, u32[]{:S(2)}) collective-permute-start(bf16[8,48,768]{2,1,0:T(8,128)(2,1)S(1)} %get-tuple-element.54), channel_id=1, source_target_pairs={{0,16},{8,24},{16,0},{24,8},{1,17},{9,25},{17,1},{25,9},{2,18},{10... | collective-permute-start | bytes 1769480 | tf_op jit(solution)/shard_map/ppermute | solution.py:327
  13.6 1.6 %collective-permute-start.3 = (bf16[96,2048]{1,0:T(8,128)(2,1)S(1)}, bf16[96,2048]{1,0:T(8,128)(2,1)S(1)}, u32[]{:S(2)}, u32[]{:S(2)}) collective-permute-start(bf16[96,2048]{1,0:T(8,128)(2,1)S(1)} %copy-done.6), channel_id=1, source_target_pairs={{0,2},{1,3},{2,0},{3,1},{4,6},{5,7},{6,4},{7,5},{8,10},{9,11},{10,... | collective-permute-start | bytes 1179656 | tf_op jit(solution)/shard_map/ppermute | solution.py:327
  15.2 19.3 %collective-permute-done.2.refs_0_ = bf16[128,2176]{1,0:T(8,128)(2,1)S(1)} collective-permute-done((bf16[128,2176]{1,0:T(8,128)(2,1)}, bf16[128,2176]{1,0:T(8,128)(2,1)S(1)}, u32[]{:S(2)}, u32[]{:S(2)}) %collective-permute-start.2) | collective-permute-done | bytes 557088 | tf_op jit(solution)/shard_map/ppermute | solution.py:327
  34.5 1.6 %collective-permute-start.9 = (bf16[8,48,768]{2,1,0:T(8,128)(2,1)S(1)}, bf16[8,48,768]{2,1,0:T(8,128)(2,1)S(1)}, u32[]{:S(2)}, u32[]{:S(2)}) collective-permute-start(bf16[8,48,768]{2,1,0:T(8,128)(2,1)S(1)} %collective-permute-done.5.refs_1_), channel_id=1, source_target_pairs={{0,16},{8,24},{16,0},{24,8},{1,17},{9,25},{17,1},{25,9},{2,18},{10... | collective-permute-start | bytes 1769480 | tf_op jit(solution)/shard_map/ppermute | solution.py:327
  36.1 0.5 shard_map.86
  36.6 0.3 collective-permute-start.10
  36.9 0.7 collective-permute-start.11
  37.6 4.4 %collective-permute-done.4.refs_4_ = bf16[96,2048]{1,0:T(8,128)(2,1)S(1)} collective-permute-done((bf16[96,2048]{1,0:T(8,128)(2,1)S(1)}, bf16[96,2048]{1,0:T(8,128)(2,1)S(1)}, u32[]{:S(2)}, u32[]{:S(2)}) %collective-permute-start.4) | collective-permute-done | bytes 393248 | tf_op jit(solution)/shard_map/ppermute | solution.py:327
  42.0 1.2 %shard_map.87 = (bf16[4,48,768]{2,1,0:T(8,128)(2,1)S(1)}, bf16[192,512]{1,0:T(8,128)(2,1)S(1)}, bf16[192,512]{1,0:T(8,128)(2,1)S(1)}, bf16[192,512]{1,0:T(8,128)...) custom-call(bf16[768,2048]{1,0:T(8,128)(2,1)S(1)} %bitcast.9, bf16[96,2048]{1,0:T(8,128)(2,1)S(1)} %copy-done.2, ...), custom_call_target="tpu_custom_call" | custom-call | tf_op jit(solution)/shard_map/pallas_call | solution.py:41
  43.2 0.8 %collective-permute-start.16 = (bf16[192,512]{1,0:T(8,128)(2,1)S(1)}, bf16[192,512]{1,0:T(8,128)(2,1)S(1)}, u32[]{:S(2)}, u32[]{:S(2)}) collective-permute-start(bf16[192,512]{1,0:T(8,128)(2,1)S(1)} %get-tuple-element.75), channel_id=1, source_target_pairs={{0,8},{8,0},{16,24},{24,16},{1,9},{9,1},{17,25},{25,17},{2,10},{10... | collective-permute-start | bytes 589832 | tf_op jit(solution)/shard_map/ppermute | solution.py:327
  44.1 0.8 shard_map.88
  44.8 6.9 %collective-permute-start.8 = (bf16[128,2176]{1,0:T(8,128)(2,1)S(1)}, bf16[128,2176]{1,0:T(8,128)(2,1)S(1)}, u32[]{:S(2)}, u32[]{:S(2)}) collective-permute-start(bf16[128,2176]{1,0:T(8,128)(2,1)S(1)} %get-tuple-element.60), channel_id=1, source_target_pairs={{0,4},{1,5},{2,6},{3,7},{4,0},{5,1},{6,2},{7,3},{8,12},{9,13},{10,... | collective-permute-start | bytes 1671176 | tf_op jit(solution)/shard_map/ppermute | solution.py:327
  51.8 0.5 collective-permute-start.17
  52.3 2.4 %collective-permute-start.18 = (bf16[192,512]{1,0:T(8,128)(2,1)S(1)}, bf16[192,512]{1,0:T(8,128)(2,1)S(1)}, u32[]{:S(2)}, u32[]{:S(2)}) collective-permute-start(bf16[192,512]{1,0:T(8,128)(2,1)S(1)} %get-tuple-element.77), channel_id=1, source_target_pairs={{0,24},{8,16},{16,8},{24,0},{1,25},{9,17},{17,9},{25,1},{2,26},{10... | collective-permute-start | bytes 589832 | tf_op jit(solution)/shard_map/ppermute | solution.py:327
  54.9 2.1 %shard_map.90 = (bf16[8,48,768]{2,1,0:T(8,128)(2,1)}, bf16[192,512]{1,0:T(8,128)(2,1)S(1)}, bf16[192,512]{1,0:T(8,128)(2,1)S(1)}, bf16[192,512]{1,0:T(8,128)(2,1...) custom-call(bf16[768,2048]{1,0:T(8,128)(2,1)S(1)} %bitcast.10, ...), custom_call_target="tpu_custom_call" | custom-call | tf_op jit(solution)/shard_map/pallas_call | solution.py:41
  56.9 4.8 %collective-permute-done.17.refs_3_ = bf16[192,512]{1,0:T(8,128)(2,1)S(1)} collective-permute-done((bf16[192,512]{1,0:T(8,128)(2,1)S(1)}, bf16[192,512]{1,0:T(8,128)(2,1)S(1)}, u32[]{:S(2)}, u32[]{:S(2)}) %collective-permute-start.17) | collective-permute-done | bytes 196640 | tf_op jit(solution)/shard_map/ppermute | solution.py:327
  61.7 1.1 %collective-permute-start.13 = (bf16[192,512]{1,0:T(8,128)(2,1)S(1)}, bf16[192,512]{1,0:T(8,128)(2,1)S(1)}, u32[]{:S(2)}, u32[]{:S(2)}) collective-permute-start(bf16[192,512]{1,0:T(8,128)(2,1)S(1)} %get-tuple-element.70), channel_id=1, source_target_pairs={{0,8},{8,0},{16,24},{24,16},{1,9},{9,1},{17,25},{25,17},{2,10},{10... | collective-permute-start | bytes 589832 | tf_op jit(solution)/shard_map/ppermute | solution.py:327
  62.8 1.2 %collective-permute-start.14 = (bf16[192,512]{1,0:T(8,128)(2,1)S(1)}, bf16[192,512]{1,0:T(8,128)(2,1)S(1)}, u32[]{:S(2)}, u32[]{:S(2)}) collective-permute-start(bf16[192,512]{1,0:T(8,128)(2,1)S(1)} %get-tuple-element.71), channel_id=1, source_target_pairs={{0,16},{8,24},{16,0},{24,8},{1,17},{9,25},{17,1},{25,9},{2,18},{10... | collective-permute-start | bytes 589832 | tf_op jit(solution)/shard_map/ppermute | solution.py:327
  64.0 1.2 %collective-permute-start.15 = (bf16[192,512]{1,0:T(8,128)(2,1)S(1)}, bf16[192,512]{1,0:T(8,128)(2,1)S(1)}, u32[]{:S(2)}, u32[]{:S(2)}) collective-permute-start(bf16[192,512]{1,0:T(8,128)(2,1)S(1)} %get-tuple-element.72), channel_id=1, source_target_pairs={{0,24},{8,16},{16,8},{24,0},{1,25},{9,17},{17,9},{25,1},{2,26},{10... | collective-permute-start | bytes 589832 | tf_op jit(solution)/shard_map/ppermute | solution.py:327
  65.2 0.7 shard_map.91
  65.8 0.8 %shard_map.92 = (f32[768,512]{1,0:T(8,128)S(1)}, f32[8,128]{1,0:T(8,128)S(1)}) custom-call(bf16[768,768]{1,0:T(8,128)(2,1)S(1)} %get-tuple-element.73.refs_0_, bf16[192,512]{1,0:T(8,128)(2,1)S(1)} %get-tuple-element.74.refs_1_, bf16[192,512]{1,0:T(8,128)(2,1)S(1)} %collective-permute-done.16.refs_2_, bf16[192,512]{1,0:T(8,128)(2,1)S(1)} %collective-permute-done.17.refs_3_, ...), custom_call_target="tpu_custom_call" | custom-call | tf_op jit(solution)/shard_map/pallas_call | solution.py:41
  66.6 1.9 %collective-permute-done.13.refs_2_ = bf16[192,512]{1,0:T(8,128)(2,1)S(1)} collective-permute-done((bf16[192,512]{1,0:T(8,128)(2,1)S(1)}, bf16[192,512]{1,0:T(8,128)(2,1)S(1)}, u32[]{:S(2)}, u32[]{:S(2)}) %collective-permute-start.13) | collective-permute-done | bytes 196640 | tf_op jit(solution)/shard_map/ppermute | solution.py:327
  68.5 3.0 %collective-permute-done.14.refs_3_ = bf16[192,512]{1,0:T(8,128)(2,1)S(1)} collective-permute-done((bf16[192,512]{1,0:T(8,128)(2,1)S(1)}, bf16[192,512]{1,0:T(8,128)(2,1)S(1)}, u32[]{:S(2)}, u32[]{:S(2)}) %collective-permute-start.14) | collective-permute-done | bytes 196640 | tf_op jit(solution)/shard_map/ppermute | solution.py:327
  71.6 1.9 %shard_map.93 = (f32[768,512]{1,0:T(8,128)}, f32[8,128]{1,0:T(8,128)S(1)}) custom-call(bf16[768,768]{1,0:T(8,128)(2,1)S(1)} %get-tuple-element.68.refs_0_, bf16[192,512]{1,0:T(8,128)(2,1)S(1)} %get-tuple-element.69.refs_1_, bf16[192,512]{1,0:T(8,128)(2,1)S(1)} %collective-permute-done.13.refs_2_, bf16[192,512]{1,0:T(8,128)(2,1)S(1)} %collective-permute-done.14.refs_3_, ...), custom_call_target="tpu_custom_call" | custom-call | tf_op jit(solution)/shard_map/pallas_call | solution.py:41
  73.5 1.4 %collective-permute-done.8.refs_4_ = bf16[128,2176]{1,0:T(8,128)(2,1)S(1)} collective-permute-done((bf16[128,2176]{1,0:T(8,128)(2,1)S(1)}, bf16[128,2176]{1,0:T(8,128)(2,1)S(1)}, u32[]{:S(2)}, u32[]{:S(2)}) %collective-permute-start.8) | collective-permute-done | bytes 557088 | tf_op jit(solution)/shard_map/ppermute | solution.py:327
  74.9 1.7 %shard_map.94 = (bf16[128,2048]{1,0:T(8,128)(2,1)}, f32[2,128]{1,0:T(2,128)}, f32[8,128]{1,0:T(8,128)}) custom-call(bf16[128,2176]{1,0:T(8,128)(2,1)S(1)} %copy-done.3, bf16[48,2048]{1,0:T(8,128)(2,1)S(1)} %get-tuple-element.48.refs_1_, bf16[96,2048]{1,0:T(8,128)(2,1)S(1)} %collective-permute-done.1.refs_1_.refs_2_, ...), custom_call_target="tpu_custom_call" | custom-call | tf_op jit(solution)/shard_map/pallas_call | solution.py:41
  (31 shorter events, 0.2 us)
Async XLA Ops:
  0.6 8.4 %copy-start = (bf16[1,768,2048]{2,1,0:T(8,128)(2,1)S(1)}, bf16[1,768,2048]{2,1,0:T(8,128)(2,1)}, u32[]{:S(2)}) copy-start(bf16[1,768,2048]{2,1,0:T(8,128)(2,1)} %param.8) | copy-start | bytes 9437188
  0.6 8.4 %copy-start.1 = (bf16[1,1,8,48,768]{4,3,2,1,0:T(8,128)(2,1)S(1)}, bf16[1,1,8,48,768]{4,3,2,1,0:T(8,128)(2,1)}, u32[]{:S(2)}) copy-start(bf16[1,1,8,48,768]{4,3,2,1,0:T(8,128)(2,1)} %param.7) | copy-start | bytes 1769476
  4.8 4.2 %collective-permute-start = (bf16[96,2048]{1,0:T(8,128)(2,1)}, bf16[96,2048]{1,0:T(8,128)(2,1)S(1)}, u32[]{:S(2)}, u32[]{:S(2)}) collective-permute-start(bf16[96,2048]{1,0:T(8,128)(2,1)} %get-tuple-element.46), channel_id=1, source_target_pairs={{0,1},{1,0},{2,3},{3,2},{4,5},{5,4},{6,7},{7,6},{8,9},{9,8},{10,11... | collective-permute-start | bytes 1179656 | tf_op jit(solution)/shard_map/ppermute | solution.py:327
  5.3 29.1 %collective-permute-start.2 = (bf16[128,2176]{1,0:T(8,128)(2,1)}, bf16[128,2176]{1,0:T(8,128)(2,1)S(1)}, u32[]{:S(2)}, u32[]{:S(2)}) collective-permute-start(bf16[128,2176]{1,0:T(8,128)(2,1)} %get-tuple-element.45.refs_0_), channel_id=1, source_target_pairs={{0,4},{1,5},{2,6},{3,7},{4,0},{5,1},{6,2},{7,3},{8,12},{9,13},{10,... | collective-permute-start | bytes 1671176 | tf_op jit(solution)/shard_map/ppermute | solution.py:327
  9.0 0.7 copy-start.4
  9.7 3.9 %copy-start.6 = (bf16[96,2048]{1,0:T(8,128)(2,1)S(1)}, bf16[96,2048]{1,0:T(8,128)(2,1)}, u32[]{:S(2)}) copy-start(bf16[96,2048]{1,0:T(8,128)(2,1)} %get-tuple-element.52) | copy-start | bytes 1179652
  9.7 5.5 %copy-start.5 = (bf16[96,2048]{1,0:T(8,128)(2,1)S(1)}, bf16[96,2048]{1,0:T(8,128)(2,1)}, u32[]{:S(2)}) copy-start(bf16[96,2048]{1,0:T(8,128)(2,1)} %get-tuple-element.53) | copy-start | bytes 1179652
  10.5 31.5 %copy-start.2 = (bf16[96,2048]{1,0:T(8,128)(2,1)S(1)}, bf16[96,2048]{1,0:T(8,128)(2,1)}, u32[]{:S(2)}) copy-start(bf16[96,2048]{1,0:T(8,128)(2,1)} %get-tuple-element.51.refs_1_) | copy-start | bytes 1179652
  10.6 23.9 %collective-permute-start.5 = (bf16[8,48,768]{2,1,0:T(8,128)(2,1)S(1)}, bf16[8,48,768]{2,1,0:T(8,128)(2,1)S(1)}, u32[]{:S(2)}, u32[]{:S(2)}) collective-permute-start(bf16[8,48,768]{2,1,0:T(8,128)(2,1)S(1)} %get-tuple-element.54), channel_id=1, source_target_pairs={{0,8},{8,0},{16,24},{24,16},{1,9},{9,1},{17,25},{25,17},{2,10},{10... | collective-permute-start | bytes 1769480 | tf_op jit(solution)/shard_map/ppermute | solution.py:327
  12.1 24.0 %collective-permute-start.6 = (bf16[8,48,768]{2,1,0:T(8,128)(2,1)S(1)}, bf16[8,48,768]{2,1,0:T(8,128)(2,1)S(1)}, u32[]{:S(2)}, u32[]{:S(2)}) collective-permute-start(bf16[8,48,768]{2,1,0:T(8,128)(2,1)S(1)} %get-tuple-element.54), channel_id=1, source_target_pairs={{0,16},{8,24},{16,0},{24,8},{1,17},{9,25},{17,1},{25,9},{2,18},{10... | collective-permute-start | bytes 1769480 | tf_op jit(solution)/shard_map/ppermute | solution.py:327
  13.6 23.2 %collective-permute-start.3 = (bf16[96,2048]{1,0:T(8,128)(2,1)S(1)}, bf16[96,2048]{1,0:T(8,128)(2,1)S(1)}, u32[]{:S(2)}, u32[]{:S(2)}) collective-permute-start(bf16[96,2048]{1,0:T(8,128)(2,1)S(1)} %copy-done.6), channel_id=1, source_target_pairs={{0,2},{1,3},{2,0},{3,1},{4,6},{5,7},{6,4},{7,5},{8,10},{9,11},{10,... | collective-permute-start | bytes 1179656 | tf_op jit(solution)/shard_map/ppermute | solution.py:327
  15.2 26.8 %collective-permute-start.4 = (bf16[96,2048]{1,0:T(8,128)(2,1)S(1)}, bf16[96,2048]{1,0:T(8,128)(2,1)S(1)}, u32[]{:S(2)}, u32[]{:S(2)}) collective-permute-start(bf16[96,2048]{1,0:T(8,128)(2,1)S(1)} %copy-done.5), channel_id=1, source_target_pairs={{0,3},{1,2},{2,1},{3,0},{4,7},{5,6},{6,5},{7,4},{8,11},{9,10},{10,... | collective-permute-start | bytes 1179656 | tf_op jit(solution)/shard_map/ppermute | solution.py:327
  34.5 8.8 %collective-permute-start.1 = (bf16[96,2048]{1,0:T(8,128)(2,1)S(1)}, bf16[96,2048]{1,0:T(8,128)(2,1)S(1)}, u32[]{:S(2)}, u32[]{:S(2)}) collective-permute-start(bf16[96,2048]{1,0:T(8,128)(2,1)S(1)} %get-tuple-element.49), channel_id=1, source_target_pairs={{0,1},{1,0},{2,3},{3,2},{4,5},{5,4},{6,7},{7,6},{8,9},{9,8},{10,11... | collective-permute-start | bytes 1179656 | tf_op jit(solution)/shard_map/ppermute | solution.py:327
  34.5 29.5 %collective-permute-start.9 = (bf16[8,48,768]{2,1,0:T(8,128)(2,1)S(1)}, bf16[8,48,768]{2,1,0:T(8,128)(2,1)S(1)}, u32[]{:S(2)}, u32[]{:S(2)}) collective-permute-start(bf16[8,48,768]{2,1,0:T(8,128)(2,1)S(1)} %collective-permute-done.5.refs_1_), channel_id=1, source_target_pairs={{0,16},{8,24},{16,0},{24,8},{1,17},{9,25},{17,1},{25,9},{2,18},{10... | collective-permute-start | bytes 1769480 | tf_op jit(solution)/shard_map/ppermute | solution.py:327
  36.6 8.3 %collective-permute-start.10 = (bf16[48,2048]{1,0:T(8,128)(2,1)S(1)}, bf16[48,2048]{1,0:T(8,128)(2,1)S(1)}, u32[]{:S(2)}, u32[]{:S(2)}) collective-permute-start(bf16[48,2048]{1,0:T(8,128)(2,1)S(1)} %get-tuple-element.63), channel_id=1, source_target_pairs={{0,1},{1,0},{2,3},{3,2},{4,5},{5,4},{6,7},{7,6},{8,9},{9,8},{10,11... | collective-permute-start | bytes 589832 | tf_op jit(solution)/shard_map/ppermute | solution.py:327
  36.9 14.9 %collective-permute-start.11 = (bf16[48,2048]{1,0:T(8,128)(2,1)S(1)}, bf16[48,2048]{1,0:T(8,128)(2,1)S(1)}, u32[]{:S(2)}, u32[]{:S(2)}) collective-permute-start(bf16[48,2048]{1,0:T(8,128)(2,1)S(1)} %get-tuple-element.64), channel_id=1, source_target_pairs={{0,2},{1,3},{2,0},{3,1},{4,6},{5,7},{6,4},{7,5},{8,10},{9,11},{10,... | collective-permute-start | bytes 589832 | tf_op jit(solution)/shard_map/ppermute | solution.py:327
  42.0 10.3 %collective-permute-start.12 = (bf16[48,2048]{1,0:T(8,128)(2,1)S(1)}, bf16[48,2048]{1,0:T(8,128)(2,1)S(1)}, u32[]{:S(2)}, u32[]{:S(2)}) collective-permute-start(bf16[48,2048]{1,0:T(8,128)(2,1)S(1)} %get-tuple-element.65), channel_id=1, source_target_pairs={{0,3},{1,2},{2,1},{3,0},{4,7},{5,6},{6,5},{7,4},{8,11},{9,10},{10,... | collective-permute-start | bytes 589832 | tf_op jit(solution)/shard_map/ppermute | solution.py:327
  43.2 11.5 %collective-permute-start.16 = (bf16[192,512]{1,0:T(8,128)(2,1)S(1)}, bf16[192,512]{1,0:T(8,128)(2,1)S(1)}, u32[]{:S(2)}, u32[]{:S(2)}) collective-permute-start(bf16[192,512]{1,0:T(8,128)(2,1)S(1)} %get-tuple-element.75), channel_id=1, source_target_pairs={{0,8},{8,0},{16,24},{24,16},{1,9},{9,1},{17,25},{25,17},{2,10},{10... | collective-permute-start | bytes 589832 | tf_op jit(solution)/shard_map/ppermute | solution.py:327
  44.8 30.0 %collective-permute-start.8 = (bf16[128,2176]{1,0:T(8,128)(2,1)S(1)}, bf16[128,2176]{1,0:T(8,128)(2,1)S(1)}, u32[]{:S(2)}, u32[]{:S(2)}) collective-permute-start(bf16[128,2176]{1,0:T(8,128)(2,1)S(1)} %get-tuple-element.60), channel_id=1, source_target_pairs={{0,4},{1,5},{2,6},{3,7},{4,0},{5,1},{6,2},{7,3},{8,12},{9,13},{10,... | collective-permute-start | bytes 1671176 | tf_op jit(solution)/shard_map/ppermute | solution.py:327
  51.8 9.9 %collective-permute-start.17 = (bf16[192,512]{1,0:T(8,128)(2,1)S(1)}, bf16[192,512]{1,0:T(8,128)(2,1)S(1)}, u32[]{:S(2)}, u32[]{:S(2)}) collective-permute-start(bf16[192,512]{1,0:T(8,128)(2,1)S(1)} %get-tuple-element.76), channel_id=1, source_target_pairs={{0,16},{8,24},{16,0},{24,8},{1,17},{9,25},{17,1},{25,9},{2,18},{10... | collective-permute-start | bytes 589832 | tf_op jit(solution)/shard_map/ppermute | solution.py:327
  52.3 10.5 %collective-permute-start.18 = (bf16[192,512]{1,0:T(8,128)(2,1)S(1)}, bf16[192,512]{1,0:T(8,128)(2,1)S(1)}, u32[]{:S(2)}, u32[]{:S(2)}) collective-permute-start(bf16[192,512]{1,0:T(8,128)(2,1)S(1)} %get-tuple-element.77), channel_id=1, source_target_pairs={{0,24},{8,16},{16,8},{24,0},{1,25},{9,17},{17,9},{25,1},{2,26},{10... | collective-permute-start | bytes 589832 | tf_op jit(solution)/shard_map/ppermute | solution.py:327
  54.8 18.7 %collective-permute-start.7 = (bf16[96,2048]{1,0:T(8,128)(2,1)S(1)}, bf16[96,2048]{1,0:T(8,128)(2,1)S(1)}, u32[]{:S(2)}, u32[]{:S(2)}) collective-permute-start(bf16[96,2048]{1,0:T(8,128)(2,1)S(1)} %get-tuple-element.59), channel_id=1, source_target_pairs={{0,2},{1,3},{2,0},{3,1},{4,6},{5,7},{6,4},{7,5},{8,10},{9,11},{10,... | collective-permute-start | bytes 1179656 | tf_op jit(solution)/shard_map/ppermute | solution.py:327
  61.7 6.9 %collective-permute-start.13 = (bf16[192,512]{1,0:T(8,128)(2,1)S(1)}, bf16[192,512]{1,0:T(8,128)(2,1)S(1)}, u32[]{:S(2)}, u32[]{:S(2)}) collective-permute-start(bf16[192,512]{1,0:T(8,128)(2,1)S(1)} %get-tuple-element.70), channel_id=1, source_target_pairs={{0,8},{8,0},{16,24},{24,16},{1,9},{9,1},{17,25},{25,17},{2,10},{10... | collective-permute-start | bytes 589832 | tf_op jit(solution)/shard_map/ppermute | solution.py:327
  62.8 8.7 %collective-permute-start.14 = (bf16[192,512]{1,0:T(8,128)(2,1)S(1)}, bf16[192,512]{1,0:T(8,128)(2,1)S(1)}, u32[]{:S(2)}, u32[]{:S(2)}) collective-permute-start(bf16[192,512]{1,0:T(8,128)(2,1)S(1)} %get-tuple-element.71), channel_id=1, source_target_pairs={{0,16},{8,24},{16,0},{24,8},{1,17},{9,25},{17,1},{25,9},{2,18},{10... | collective-permute-start | bytes 589832 | tf_op jit(solution)/shard_map/ppermute | solution.py:327
  64.0 7.6 %collective-permute-start.15 = (bf16[192,512]{1,0:T(8,128)(2,1)S(1)}, bf16[192,512]{1,0:T(8,128)(2,1)S(1)}, u32[]{:S(2)}, u32[]{:S(2)}) collective-permute-start(bf16[192,512]{1,0:T(8,128)(2,1)S(1)} %get-tuple-element.72), channel_id=1, source_target_pairs={{0,24},{8,16},{16,8},{24,0},{1,25},{9,17},{17,9},{25,1},{2,26},{10... | collective-permute-start | bytes 589832 | tf_op jit(solution)/shard_map/ppermute | solution.py:327
  71.5 3.3 %copy-start.3 = (bf16[128,2176]{1,0:T(8,128)(2,1)S(1)}, bf16[128,2176]{1,0:T(8,128)(2,1)}, u32[]{:S(2)}) copy-start(bf16[128,2176]{1,0:T(8,128)(2,1)} %get-tuple-element.45.refs_0_) | copy-start | bytes 1671172

commit v6 on v5

--- a/solution.py
+++ b/solution.py
@@ -109,6 +109,7 @@
 def start_body(capacity, routing_at, gates_at, dout_at, hidden_at, weight_at, *refs):
     message_ref, give_refs = refs[0], refs[1:5]
     routing_ref, gates_ref, dout_ref, hidden_ref, weight_ref, sems = refs[5:]
+    me = lax.axis_index("expert")
     units = weight_ref.shape[0]
     deep = units // WEIGHT_PARTS
     parts = [slice(at, at + deep) for at in range(0, units, deep)]
@@ -119,14 +120,13 @@
                 (routing_at, routing_ref),
                 (gates_at, gates_ref),
                 (dout_at, dout_ref),
-                (hidden_at, hidden_ref),
+                *((hidden_at.at[me ^ (4 + m)], hidden_ref.at[m]) for m in range(4)),
                 *((weight_at.at[part], weight_ref.at[part]) for part in parts),
             )
         )
     ]
     for move in moves:
         move.start()
-    me = lax.axis_index("expert")
     c = capacity
     picks, tokens = routing_ref.shape
     for move in moves[:3]:
@@ -151,10 +151,11 @@
     for m, ref in enumerate(give_refs):
         first = ((me ^ m) * c).astype(f32)
         ref[:c] = rows_for(first, c, slots, gates, dout)
-    moves[3].wait()
-    rows = jnp.concatenate([hidden_ref[me ^ m] for m in range(4, LINE)], axis=0)
+    for move in moves[3:7]:
+        move.wait()
+    rows = jnp.concatenate([hidden_ref[m] for m in range(4)], axis=0)
     total = None
-    for part, move in zip(parts, moves[4:]):
+    for part, move in zip(parts, moves[7:]):
         move.wait()
         product = jnp.dot(rows[:, part], weight_ref[part], preferred_element_type=f32)
         total = product if total is None else total + product
@@ -388,9 +389,9 @@
             pltpu.VMEM((picks, tokens), jnp.int32),
             pltpu.VMEM((picks, tokens), f32),
             pltpu.VMEM((tokens, width), bf16),
-            pltpu.VMEM((LINE, capacity, units), bf16),
+            pltpu.VMEM((4, capacity, units), bf16),
             pltpu.VMEM((units, width), bf16),
-            pltpu.SemaphoreType.DMA((4 + WEIGHT_PARTS,)),
+            pltpu.SemaphoreType.DMA((7 + WEIGHT_PARTS,)),
         ],
         pinned=(0, 1, 2, 3, 4),
         vmem=VMEM_ALL,

time: 76.7 us -> 76.7 us (level)
  no operation moved by 1% of the time
where the time goes in v6:
time: 76.7 us; the launch traced here: 76.5 us
  waiting for transfers between devices  34.8 us (45%)
  starting transfers between devices  25.7 us (34%)
  Pallas kernels  14.5 us (19%)
  between operations  0.78 us (1%)
    ppermute x19, waiting for transfers between devices, value(): lax.ppermute(self.value(source), axis, [(i, i ^ m) for i in range(size)])  34.8 us
    ppermute x19, starting transfers between devices, value(): lax.ppermute(self.value(source), axis, [(i, i ^ m) for i in range(size)])  25.7 us
    pallas_call x11, Pallas kernels, __call__(): pl.pallas_call(kernel, out_shape=[*outs, jax.ShapeDtypeStruct((8, LANES),...  14.5 us
  transfers between devices with their start and end apart: 19, of which 6 were waited for; matrix products, arithmetic and copies ran while one was open for 0% of the time, Pallas kernels for 11%

profile of v6, /device:TPU:0, one launch (start us, length us, event | category | flops | bytes accessed | tf_op | source)
XLA Modules:
  0.0 76.5 jit_solution(16137700896201752875)
XLA Ops:
  0.7 4.1 %shard_map.84 = (bf16[128,2176]{1,0:T(8,128)(2,1)}, bf16[96,2048]{1,0:T(8,128)(2,1)}, bf16[96,2048]{1,0:T(8,128)(2,1)}, bf16[96,2048]{1,0:T(8,128)(2,1)}, bf16[96,2048]{1,0:T(8,128)(2,1)}, /*index=5*/f32[8,128]{1,0:T(8,128)}) custom-call(s32[2,128]{1,0:T(2,128)} %bitcast.14, f32[2,128]{1,0:T(2,128)} %bitcast.15, bf16[128,2048]{1,0:T(8,128)(2,1)} %refs_2_.1, ...), custom_call_target="tpu_custom_call" | custom-call | tf_op jit(solution)/shard_map/pallas_call | solution.py:41
  4.8 0.5 collective-permute-start
  5.3 3.7 %collective-permute-start.2 = (bf16[128,2176]{1,0:T(8,128)(2,1)}, bf16[128,2176]{1,0:T(8,128)(2,1)S(1)}, u32[]{:S(2)}, u32[]{:S(2)}) collective-permute-start(bf16[128,2176]{1,0:T(8,128)(2,1)} %get-tuple-element.45.refs_0_), channel_id=1, source_target_pairs={{0,4},{1,5},{2,6},{3,7},{4,0},{5,1},{6,2},{7,3},{8,12},{9,13},{10,... | collective-permute-start | bytes 1671176 | tf_op jit(solution)/shard_map/ppermute | solution.py:328
  9.0 0.7 copy-done.4
  9.6 0.8 %shard_map.85 = (bf16[48,2048]{1,0:T(8,128)(2,1)S(1)}, bf16[96,2048]{1,0:T(8,128)(2,1)S(1)}, bf16[48,2048]{1,0:T(8,128)(2,1)S(1)}, bf16[8,48,768]{2,1,0:T(8,128)(2,1)S(1)}, f32[8,128]{1,0:T(8,128)S(1)}) custom-call(bf16[8,48,768]{2,1,0:T(8,128)(2,1)S(1)} %bitcast.12, bf16[768,2048]{1,0:T(8,128)(2,1)S(1)} %bitcast.8, ...), custom_call_target="tpu_custom_call" | custom-call | tf_op jit(solution)/shard_map/pallas_call | solution.py:41
  10.5 1.6 %collective-permute-start.5 = (bf16[8,48,768]{2,1,0:T(8,128)(2,1)S(1)}, bf16[8,48,768]{2,1,0:T(8,128)(2,1)S(1)}, u32[]{:S(2)}, u32[]{:S(2)}) collective-permute-start(bf16[8,48,768]{2,1,0:T(8,128)(2,1)S(1)} %get-tuple-element.54), channel_id=1, source_target_pairs={{0,8},{8,0},{16,24},{24,16},{1,9},{9,1},{17,25},{25,17},{2,10},{10... | collective-permute-start | bytes 1769480 | tf_op jit(solution)/shard_map/ppermute | solution.py:328
  12.0 1.5 %collective-permute-start.6 = (bf16[8,48,768]{2,1,0:T(8,128)(2,1)S(1)}, bf16[8,48,768]{2,1,0:T(8,128)(2,1)S(1)}, u32[]{:S(2)}, u32[]{:S(2)}) collective-permute-start(bf16[8,48,768]{2,1,0:T(8,128)(2,1)S(1)} %get-tuple-element.54), channel_id=1, source_target_pairs={{0,16},{8,24},{16,0},{24,8},{1,17},{9,25},{17,1},{25,9},{2,18},{10... | collective-permute-start | bytes 1769480 | tf_op jit(solution)/shard_map/ppermute | solution.py:328
  13.6 1.6 %collective-permute-start.3 = (bf16[96,2048]{1,0:T(8,128)(2,1)S(1)}, bf16[96,2048]{1,0:T(8,128)(2,1)S(1)}, u32[]{:S(2)}, u32[]{:S(2)}) collective-permute-start(bf16[96,2048]{1,0:T(8,128)(2,1)S(1)} %copy-done.6), channel_id=1, source_target_pairs={{0,2},{1,3},{2,0},{3,1},{4,6},{5,7},{6,4},{7,5},{8,10},{9,11},{10,... | collective-permute-start | bytes 1179656 | tf_op jit(solution)/shard_map/ppermute | solution.py:328
  15.1 19.3 %collective-permute-done.2.refs_0_ = bf16[128,2176]{1,0:T(8,128)(2,1)S(1)} collective-permute-done((bf16[128,2176]{1,0:T(8,128)(2,1)}, bf16[128,2176]{1,0:T(8,128)(2,1)S(1)}, u32[]{:S(2)}, u32[]{:S(2)}) %collective-permute-start.2) | collective-permute-done | bytes 557088 | tf_op jit(solution)/shard_map/ppermute | solution.py:328
  34.4 1.6 %collective-permute-start.9 = (bf16[8,48,768]{2,1,0:T(8,128)(2,1)S(1)}, bf16[8,48,768]{2,1,0:T(8,128)(2,1)S(1)}, u32[]{:S(2)}, u32[]{:S(2)}) collective-permute-start(bf16[8,48,768]{2,1,0:T(8,128)(2,1)S(1)} %collective-permute-done.5.refs_1_), channel_id=1, source_target_pairs={{0,16},{8,24},{16,0},{24,8},{1,17},{9,25},{17,1},{25,9},{2,18},{10... | collective-permute-start | bytes 1769480 | tf_op jit(solution)/shard_map/ppermute | solution.py:328
  36.0 0.5 shard_map.86
  36.5 0.3 collective-permute-start.10
  36.8 0.7 collective-permute-start.11
  37.5 4.4 %collective-permute-done.4.refs_4_ = bf16[96,2048]{1,0:T(8,128)(2,1)S(1)} collective-permute-done((bf16[96,2048]{1,0:T(8,128)(2,1)S(1)}, bf16[96,2048]{1,0:T(8,128)(2,1)S(1)}, u32[]{:S(2)}, u32[]{:S(2)}) %collective-permute-start.4) | collective-permute-done | bytes 393248 | tf_op jit(solution)/shard_map/ppermute | solution.py:328
  41.9 1.2 %shard_map.87 = (bf16[4,48,768]{2,1,0:T(8,128)(2,1)S(1)}, bf16[192,512]{1,0:T(8,128)(2,1)S(1)}, bf16[192,512]{1,0:T(8,128)(2,1)S(1)}, bf16[192,512]{1,0:T(8,128)...) custom-call(bf16[768,2048]{1,0:T(8,128)(2,1)S(1)} %bitcast.9, bf16[96,2048]{1,0:T(8,128)(2,1)S(1)} %copy-done.2, ...), custom_call_target="tpu_custom_call" | custom-call | tf_op jit(solution)/shard_map/pallas_call | solution.py:41
  43.2 0.8 %collective-permute-start.16 = (bf16[192,512]{1,0:T(8,128)(2,1)S(1)}, bf16[192,512]{1,0:T(8,128)(2,1)S(1)}, u32[]{:S(2)}, u32[]{:S(2)}) collective-permute-start(bf16[192,512]{1,0:T(8,128)(2,1)S(1)} %get-tuple-element.75), channel_id=1, source_target_pairs={{0,8},{8,0},{16,24},{24,16},{1,9},{9,1},{17,25},{25,17},{2,10},{10... | collective-permute-start | bytes 589832 | tf_op jit(solution)/shard_map/ppermute | solution.py:328
  44.0 0.8 shard_map.88
  44.8 6.9 %collective-permute-start.8 = (bf16[128,2176]{1,0:T(8,128)(2,1)S(1)}, bf16[128,2176]{1,0:T(8,128)(2,1)S(1)}, u32[]{:S(2)}, u32[]{:S(2)}) collective-permute-start(bf16[128,2176]{1,0:T(8,128)(2,1)S(1)} %get-tuple-element.60), channel_id=1, source_target_pairs={{0,4},{1,5},{2,6},{3,7},{4,0},{5,1},{6,2},{7,3},{8,12},{9,13},{10,... | collective-permute-start | bytes 1671176 | tf_op jit(solution)/shard_map/ppermute | solution.py:328
  51.7 0.5 collective-permute-start.17
  52.2 2.4 %collective-permute-start.18 = (bf16[192,512]{1,0:T(8,128)(2,1)S(1)}, bf16[192,512]{1,0:T(8,128)(2,1)S(1)}, u32[]{:S(2)}, u32[]{:S(2)}) collective-permute-start(bf16[192,512]{1,0:T(8,128)(2,1)S(1)} %get-tuple-element.77), channel_id=1, source_target_pairs={{0,24},{8,16},{16,8},{24,0},{1,25},{9,17},{17,9},{25,1},{2,26},{10... | collective-permute-start | bytes 589832 | tf_op jit(solution)/shard_map/ppermute | solution.py:328
  54.8 2.1 %shard_map.90 = (bf16[8,48,768]{2,1,0:T(8,128)(2,1)}, bf16[192,512]{1,0:T(8,128)(2,1)S(1)}, bf16[192,512]{1,0:T(8,128)(2,1)S(1)}, bf16[192,512]{1,0:T(8,128)(2,1...) custom-call(bf16[768,2048]{1,0:T(8,128)(2,1)S(1)} %bitcast.10, ...), custom_call_target="tpu_custom_call" | custom-call | tf_op jit(solution)/shard_map/pallas_call | solution.py:41
  56.8 4.8 %collective-permute-done.17.refs_3_ = bf16[192,512]{1,0:T(8,128)(2,1)S(1)} collective-permute-done((bf16[192,512]{1,0:T(8,128)(2,1)S(1)}, bf16[192,512]{1,0:T(8,128)(2,1)S(1)}, u32[]{:S(2)}, u32[]{:S(2)}) %collective-permute-start.17) | collective-permute-done | bytes 196640 | tf_op jit(solution)/shard_map/ppermute | solution.py:328
  61.6 1.0 %collective-permute-start.13 = (bf16[192,512]{1,0:T(8,128)(2,1)S(1)}, bf16[192,512]{1,0:T(8,128)(2,1)S(1)}, u32[]{:S(2)}, u32[]{:S(2)}) collective-permute-start(bf16[192,512]{1,0:T(8,128)(2,1)S(1)} %get-tuple-element.70), channel_id=1, source_target_pairs={{0,8},{8,0},{16,24},{24,16},{1,9},{9,1},{17,25},{25,17},{2,10},{10... | collective-permute-start | bytes 589832 | tf_op jit(solution)/shard_map/ppermute | solution.py:328
  62.6 1.2 %collective-permute-start.14 = (bf16[192,512]{1,0:T(8,128)(2,1)S(1)}, bf16[192,512]{1,0:T(8,128)(2,1)S(1)}, u32[]{:S(2)}, u32[]{:S(2)}) collective-permute-start(bf16[192,512]{1,0:T(8,128)(2,1)S(1)} %get-tuple-element.71), channel_id=1, source_target_pairs={{0,16},{8,24},{16,0},{24,8},{1,17},{9,25},{17,1},{25,9},{2,18},{10... | collective-permute-start | bytes 589832 | tf_op jit(solution)/shard_map/ppermute | solution.py:328
  63.9 1.2 %collective-permute-start.15 = (bf16[192,512]{1,0:T(8,128)(2,1)S(1)}, bf16[192,512]{1,0:T(8,128)(2,1)S(1)}, u32[]{:S(2)}, u32[]{:S(2)}) collective-permute-start(bf16[192,512]{1,0:T(8,128)(2,1)S(1)} %get-tuple-element.72), channel_id=1, source_target_pairs={{0,24},{8,16},{16,8},{24,0},{1,25},{9,17},{17,9},{25,1},{2,26},{10... | collective-permute-start | bytes 589832 | tf_op jit(solution)/shard_map/ppermute | solution.py:328
  65.1 0.7 shard_map.91
  65.8 0.8 %shard_map.92 = (f32[768,512]{1,0:T(8,128)S(1)}, f32[8,128]{1,0:T(8,128)S(1)}) custom-call(bf16[768,768]{1,0:T(8,128)(2,1)S(1)} %get-tuple-element.73.refs_0_, bf16[192,512]{1,0:T(8,128)(2,1)S(1)} %get-tuple-element.74.refs_1_, bf16[192,512]{1,0:T(8,128)(2,1)S(1)} %collective-permute-done.16.refs_2_, bf16[192,512]{1,0:T(8,128)(2,1)S(1)} %collective-permute-done.17.refs_3_, ...), custom_call_target="tpu_custom_call" | custom-call | tf_op jit(solution)/shard_map/pallas_call | solution.py:41
  66.5 2.0 %collective-permute-done.13.refs_2_ = bf16[192,512]{1,0:T(8,128)(2,1)S(1)} collective-permute-done((bf16[192,512]{1,0:T(8,128)(2,1)S(1)}, bf16[192,512]{1,0:T(8,128)(2,1)S(1)}, u32[]{:S(2)}, u32[]{:S(2)}) %collective-permute-start.13) | collective-permute-done | bytes 196640 | tf_op jit(solution)/shard_map/ppermute | solution.py:328
  68.5 3.0 %collective-permute-done.14.refs_3_ = bf16[192,512]{1,0:T(8,128)(2,1)S(1)} collective-permute-done((bf16[192,512]{1,0:T(8,128)(2,1)S(1)}, bf16[192,512]{1,0:T(8,128)(2,1)S(1)}, u32[]{:S(2)}, u32[]{:S(2)}) %collective-permute-start.14) | collective-permute-done | bytes 196640 | tf_op jit(solution)/shard_map/ppermute | solution.py:328
  71.6 1.9 %shard_map.93 = (f32[768,512]{1,0:T(8,128)}, f32[8,128]{1,0:T(8,128)S(1)}) custom-call(bf16[768,768]{1,0:T(8,128)(2,1)S(1)} %get-tuple-element.68.refs_0_, bf16[192,512]{1,0:T(8,128)(2,1)S(1)} %get-tuple-element.69.refs_1_, bf16[192,512]{1,0:T(8,128)(2,1)S(1)} %collective-permute-done.13.refs_2_, bf16[192,512]{1,0:T(8,128)(2,1)S(1)} %collective-permute-done.14.refs_3_, ...), custom_call_target="tpu_custom_call" | custom-call | tf_op jit(solution)/shard_map/pallas_call | solution.py:41
  73.5 1.3 %collective-permute-done.8.refs_4_ = bf16[128,2176]{1,0:T(8,128)(2,1)S(1)} collective-permute-done((bf16[128,2176]{1,0:T(8,128)(2,1)S(1)}, bf16[128,2176]{1,0:T(8,128)(2,1)S(1)}, u32[]{:S(2)}, u32[]{:S(2)}) %collective-permute-start.8) | collective-permute-done | bytes 557088 | tf_op jit(solution)/shard_map/ppermute | solution.py:328
  74.8 1.7 %shard_map.94 = (bf16[128,2048]{1,0:T(8,128)(2,1)}, f32[2,128]{1,0:T(2,128)}, f32[8,128]{1,0:T(8,128)}) custom-call(bf16[128,2176]{1,0:T(8,128)(2,1)S(1)} %copy-done.3, bf16[48,2048]{1,0:T(8,128)(2,1)S(1)} %get-tuple-element.48.refs_1_, bf16[96,2048]{1,0:T(8,128)(2,1)S(1)} %collective-permute-done.1.refs_1_.refs_2_, ...), custom_call_target="tpu_custom_call" | custom-call | tf_op jit(solution)/shard_map/pallas_call | solution.py:41
  (31 shorter events, 0.2 us)
Async XLA Ops:
  0.6 8.3 %copy-start = (bf16[1,768,2048]{2,1,0:T(8,128)(2,1)S(1)}, bf16[1,768,2048]{2,1,0:T(8,128)(2,1)}, u32[]{:S(2)}) copy-start(bf16[1,768,2048]{2,1,0:T(8,128)(2,1)} %param.8) | copy-start | bytes 9437188
  0.6 8.3 %copy-start.1 = (bf16[1,1,8,48,768]{4,3,2,1,0:T(8,128)(2,1)S(1)}, bf16[1,1,8,48,768]{4,3,2,1,0:T(8,128)(2,1)}, u32[]{:S(2)}) copy-start(bf16[1,1,8,48,768]{4,3,2,1,0:T(8,128)(2,1)} %param.7) | copy-start | bytes 1769476
  4.8 4.2 %collective-permute-start = (bf16[96,2048]{1,0:T(8,128)(2,1)}, bf16[96,2048]{1,0:T(8,128)(2,1)S(1)}, u32[]{:S(2)}, u32[]{:S(2)}) collective-permute-start(bf16[96,2048]{1,0:T(8,128)(2,1)} %get-tuple-element.46), channel_id=1, source_target_pairs={{0,1},{1,0},{2,3},{3,2},{4,5},{5,4},{6,7},{7,6},{8,9},{9,8},{10,11... | collective-permute-start | bytes 1179656 | tf_op jit(solution)/shard_map/ppermute | solution.py:328
  5.3 29.1 %collective-permute-start.2 = (bf16[128,2176]{1,0:T(8,128)(2,1)}, bf16[128,2176]{1,0:T(8,128)(2,1)S(1)}, u32[]{:S(2)}, u32[]{:S(2)}) collective-permute-start(bf16[128,2176]{1,0:T(8,128)(2,1)} %get-tuple-element.45.refs_0_), channel_id=1, source_target_pairs={{0,4},{1,5},{2,6},{3,7},{4,0},{5,1},{6,2},{7,3},{8,12},{9,13},{10,... | collective-permute-start | bytes 1671176 | tf_op jit(solution)/shard_map/ppermute | solution.py:328
  9.0 0.7 copy-start.4
  9.6 3.9 %copy-start.6 = (bf16[96,2048]{1,0:T(8,128)(2,1)S(1)}, bf16[96,2048]{1,0:T(8,128)(2,1)}, u32[]{:S(2)}) copy-start(bf16[96,2048]{1,0:T(8,128)(2,1)} %get-tuple-element.52) | copy-start | bytes 1179652
  9.6 5.5 %copy-start.5 = (bf16[96,2048]{1,0:T(8,128)(2,1)S(1)}, bf16[96,2048]{1,0:T(8,128)(2,1)}, u32[]{:S(2)}) copy-start(bf16[96,2048]{1,0:T(8,128)(2,1)} %get-tuple-element.53) | copy-start | bytes 1179652
  10.5 31.5 %copy-start.2 = (bf16[96,2048]{1,0:T(8,128)(2,1)S(1)}, bf16[96,2048]{1,0:T(8,128)(2,1)}, u32[]{:S(2)}) copy-start(bf16[96,2048]{1,0:T(8,128)(2,1)} %get-tuple-element.51.refs_1_) | copy-start | bytes 1179652
  10.5 23.9 %collective-permute-start.5 = (bf16[8,48,768]{2,1,0:T(8,128)(2,1)S(1)}, bf16[8,48,768]{2,1,0:T(8,128)(2,1)S(1)}, u32[]{:S(2)}, u32[]{:S(2)}) collective-permute-start(bf16[8,48,768]{2,1,0:T(8,128)(2,1)S(1)} %get-tuple-element.54), channel_id=1, source_target_pairs={{0,8},{8,0},{16,24},{24,16},{1,9},{9,1},{17,25},{25,17},{2,10},{10... | collective-permute-start | bytes 1769480 | tf_op jit(solution)/shard_map/ppermute | solution.py:328
  12.0 24.0 %collective-permute-start.6 = (bf16[8,48,768]{2,1,0:T(8,128)(2,1)S(1)}, bf16[8,48,768]{2,1,0:T(8,128)(2,1)S(1)}, u32[]{:S(2)}, u32[]{:S(2)}) collective-permute-start(bf16[8,48,768]{2,1,0:T(8,128)(2,1)S(1)} %get-tuple-element.54), channel_id=1, source_target_pairs={{0,16},{8,24},{16,0},{24,8},{1,17},{9,25},{17,1},{25,9},{2,18},{10... | collective-permute-start | bytes 1769480 | tf_op jit(solution)/shard_map/ppermute | solution.py:328
  13.6 23.2 %collective-permute-start.3 = (bf16[96,2048]{1,0:T(8,128)(2,1)S(1)}, bf16[96,2048]{1,0:T(8,128)(2,1)S(1)}, u32[]{:S(2)}, u32[]{:S(2)}) collective-permute-start(bf16[96,2048]{1,0:T(8,128)(2,1)S(1)} %copy-done.6), channel_id=1, source_target_pairs={{0,2},{1,3},{2,0},{3,1},{4,6},{5,7},{6,4},{7,5},{8,10},{9,11},{10,... | collective-permute-start | bytes 1179656 | tf_op jit(solution)/shard_map/ppermute | solution.py:328
  15.1 26.8 %collective-permute-start.4 = (bf16[96,2048]{1,0:T(8,128)(2,1)S(1)}, bf16[96,2048]{1,0:T(8,128)(2,1)S(1)}, u32[]{:S(2)}, u32[]{:S(2)}) collective-permute-start(bf16[96,2048]{1,0:T(8,128)(2,1)S(1)} %copy-done.5), channel_id=1, source_target_pairs={{0,3},{1,2},{2,1},{3,0},{4,7},{5,6},{6,5},{7,4},{8,11},{9,10},{10,... | collective-permute-start | bytes 1179656 | tf_op jit(solution)/shard_map/ppermute | solution.py:328
  34.4 8.8 %collective-permute-start.1 = (bf16[96,2048]{1,0:T(8,128)(2,1)S(1)}, bf16[96,2048]{1,0:T(8,128)(2,1)S(1)}, u32[]{:S(2)}, u32[]{:S(2)}) collective-permute-start(bf16[96,2048]{1,0:T(8,128)(2,1)S(1)} %get-tuple-element.49), channel_id=1, source_target_pairs={{0,1},{1,0},{2,3},{3,2},{4,5},{5,4},{6,7},{7,6},{8,9},{9,8},{10,11... | collective-permute-start | bytes 1179656 | tf_op jit(solution)/shard_map/ppermute | solution.py:328
  34.4 29.4 %collective-permute-start.9 = (bf16[8,48,768]{2,1,0:T(8,128)(2,1)S(1)}, bf16[8,48,768]{2,1,0:T(8,128)(2,1)S(1)}, u32[]{:S(2)}, u32[]{:S(2)}) collective-permute-start(bf16[8,48,768]{2,1,0:T(8,128)(2,1)S(1)} %collective-permute-done.5.refs_1_), channel_id=1, source_target_pairs={{0,16},{8,24},{16,0},{24,8},{1,17},{9,25},{17,1},{25,9},{2,18},{10... | collective-permute-start | bytes 1769480 | tf_op jit(solution)/shard_map/ppermute | solution.py:328
  36.5 8.3 %collective-permute-start.10 = (bf16[48,2048]{1,0:T(8,128)(2,1)S(1)}, bf16[48,2048]{1,0:T(8,128)(2,1)S(1)}, u32[]{:S(2)}, u32[]{:S(2)}) collective-permute-start(bf16[48,2048]{1,0:T(8,128)(2,1)S(1)} %get-tuple-element.63), channel_id=1, source_target_pairs={{0,1},{1,0},{2,3},{3,2},{4,5},{5,4},{6,7},{7,6},{8,9},{9,8},{10,11... | collective-permute-start | bytes 589832 | tf_op jit(solution)/shard_map/ppermute | solution.py:328
  36.8 14.9 %collective-permute-start.11 = (bf16[48,2048]{1,0:T(8,128)(2,1)S(1)}, bf16[48,2048]{1,0:T(8,128)(2,1)S(1)}, u32[]{:S(2)}, u32[]{:S(2)}) collective-permute-start(bf16[48,2048]{1,0:T(8,128)(2,1)S(1)} %get-tuple-element.64), channel_id=1, source_target_pairs={{0,2},{1,3},{2,0},{3,1},{4,6},{5,7},{6,4},{7,5},{8,10},{9,11},{10,... | collective-permute-start | bytes 589832 | tf_op jit(solution)/shard_map/ppermute | solution.py:328
  41.9 10.3 %collective-permute-start.12 = (bf16[48,2048]{1,0:T(8,128)(2,1)S(1)}, bf16[48,2048]{1,0:T(8,128)(2,1)S(1)}, u32[]{:S(2)}, u32[]{:S(2)}) collective-permute-start(bf16[48,2048]{1,0:T(8,128)(2,1)S(1)} %get-tuple-element.65), channel_id=1, source_target_pairs={{0,3},{1,2},{2,1},{3,0},{4,7},{5,6},{6,5},{7,4},{8,11},{9,10},{10,... | collective-permute-start | bytes 589832 | tf_op jit(solution)/shard_map/ppermute | solution.py:328
  43.2 11.5 %collective-permute-start.16 = (bf16[192,512]{1,0:T(8,128)(2,1)S(1)}, bf16[192,512]{1,0:T(8,128)(2,1)S(1)}, u32[]{:S(2)}, u32[]{:S(2)}) collective-permute-start(bf16[192,512]{1,0:T(8,128)(2,1)S(1)} %get-tuple-element.75), channel_id=1, source_target_pairs={{0,8},{8,0},{16,24},{24,16},{1,9},{9,1},{17,25},{25,17},{2,10},{10... | collective-permute-start | bytes 589832 | tf_op jit(solution)/shard_map/ppermute | solution.py:328
  44.8 30.0 %collective-permute-start.8 = (bf16[128,2176]{1,0:T(8,128)(2,1)S(1)}, bf16[128,2176]{1,0:T(8,128)(2,1)S(1)}, u32[]{:S(2)}, u32[]{:S(2)}) collective-permute-start(bf16[128,2176]{1,0:T(8,128)(2,1)S(1)} %get-tuple-element.60), channel_id=1, source_target_pairs={{0,4},{1,5},{2,6},{3,7},{4,0},{5,1},{6,2},{7,3},{8,12},{9,13},{10,... | collective-permute-start | bytes 1671176 | tf_op jit(solution)/shard_map/ppermute | solution.py:328
  51.7 9.9 %collective-permute-start.17 = (bf16[192,512]{1,0:T(8,128)(2,1)S(1)}, bf16[192,512]{1,0:T(8,128)(2,1)S(1)}, u32[]{:S(2)}, u32[]{:S(2)}) collective-permute-start(bf16[192,512]{1,0:T(8,128)(2,1)S(1)} %get-tuple-element.76), channel_id=1, source_target_pairs={{0,16},{8,24},{16,0},{24,8},{1,17},{9,25},{17,1},{25,9},{2,18},{10... | collective-permute-start | bytes 589832 | tf_op jit(solution)/shard_map/ppermute | solution.py:328
  52.2 10.4 %collective-permute-start.18 = (bf16[192,512]{1,0:T(8,128)(2,1)S(1)}, bf16[192,512]{1,0:T(8,128)(2,1)S(1)}, u32[]{:S(2)}, u32[]{:S(2)}) collective-permute-start(bf16[192,512]{1,0:T(8,128)(2,1)S(1)} %get-tuple-element.77), channel_id=1, source_target_pairs={{0,24},{8,16},{16,8},{24,0},{1,25},{9,17},{17,9},{25,1},{2,26},{10... | collective-permute-start | bytes 589832 | tf_op jit(solution)/shard_map/ppermute | solution.py:328
  54.7 18.8 %collective-permute-start.7 = (bf16[96,2048]{1,0:T(8,128)(2,1)S(1)}, bf16[96,2048]{1,0:T(8,128)(2,1)S(1)}, u32[]{:S(2)}, u32[]{:S(2)}) collective-permute-start(bf16[96,2048]{1,0:T(8,128)(2,1)S(1)} %get-tuple-element.59), channel_id=1, source_target_pairs={{0,2},{1,3},{2,0},{3,1},{4,6},{5,7},{6,4},{7,5},{8,10},{9,11},{10,... | collective-permute-start | bytes 1179656 | tf_op jit(solution)/shard_map/ppermute | solution.py:328
  61.6 6.9 %collective-permute-start.13 = (bf16[192,512]{1,0:T(8,128)(2,1)S(1)}, bf16[192,512]{1,0:T(8,128)(2,1)S(1)}, u32[]{:S(2)}, u32[]{:S(2)}) collective-permute-start(bf16[192,512]{1,0:T(8,128)(2,1)S(1)} %get-tuple-element.70), channel_id=1, source_target_pairs={{0,8},{8,0},{16,24},{24,16},{1,9},{9,1},{17,25},{25,17},{2,10},{10... | collective-permute-start | bytes 589832 | tf_op jit(solution)/shard_map/ppermute | solution.py:328
  62.6 8.9 %collective-permute-start.14 = (bf16[192,512]{1,0:T(8,128)(2,1)S(1)}, bf16[192,512]{1,0:T(8,128)(2,1)S(1)}, u32[]{:S(2)}, u32[]{:S(2)}) collective-permute-start(bf16[192,512]{1,0:T(8,128)(2,1)S(1)} %get-tuple-element.71), channel_id=1, source_target_pairs={{0,16},{8,24},{16,0},{24,8},{1,17},{9,25},{17,1},{25,9},{2,18},{10... | collective-permute-start | bytes 589832 | tf_op jit(solution)/shard_map/ppermute | solution.py:328
  63.9 7.7 %collective-permute-start.15 = (bf16[192,512]{1,0:T(8,128)(2,1)S(1)}, bf16[192,512]{1,0:T(8,128)(2,1)S(1)}, u32[]{:S(2)}, u32[]{:S(2)}) collective-permute-start(bf16[192,512]{1,0:T(8,128)(2,1)S(1)} %get-tuple-element.72), channel_id=1, source_target_pairs={{0,24},{8,16},{16,8},{24,0},{1,25},{9,17},{17,9},{25,1},{2,26},{10... | collective-permute-start | bytes 589832 | tf_op jit(solution)/shard_map/ppermute | solution.py:328
  71.6 3.2 %copy-start.3 = (bf16[128,2176]{1,0:T(8,128)(2,1)S(1)}, bf16[128,2176]{1,0:T(8,128)(2,1)}, u32[]{:S(2)}) copy-start(bf16[128,2176]{1,0:T(8,128)(2,1)} %get-tuple-element.45.refs_0_) | copy-start | bytes 1671172
